TPU v7x, 32 devices: a whole 2x2x4 slice. The times are simulated.
32 devices in a mesh: dp: 4 (over y, x), fsdp: 8 (over z, core).
Axes of the slice: x: 2, y: 2, z: 4, core: 2. Of those that a mesh axis runs over, the one named last changes fastest.
Arguments:
- inputs: bfloat16 [16384, 512], P(('dp', 'fsdp')), may hold values from -6 to 6
- lengths: int32 [32, 3], P(('dp', 'fsdp')), may hold values from 0 to 512, as said below
- filters: bfloat16 [24, 512], replicated
- cotangent: bfloat16 [16384, 512], P(('dp', 'fsdp')), may hold values from -12 to 12
- mixer_weight: float32 [13824, 512], P(('dp', 'fsdp')), may hold values from -0.0546875 to 0.0546875
- gate_up_weight: float32 [4096, 512], P(('dp', 'fsdp')), may hold values from -0.25 to 0.25
- down_weight: float32 [2048, 512], P(('dp', 'fsdp')), may hold values from -0.125 to 0.125
- norm_gains: float32 [2, 512], P(None, ('dp', 'fsdp'))
- mixer_first: float32 [13824, 512], P(('dp', 'fsdp')), may hold values from -0.00021362305 to 0.00021362305
- gate_up_first: float32 [4096, 512], P(('dp', 'fsdp')), may hold values from -7.6293945e-05 to 7.6293945e-05
- down_first: float32 [2048, 512], P(('dp', 'fsdp')), may hold values from -0.00015258789 to 0.00015258789
- gains_first: float32 [2, 512], P(None, ('dp', 'fsdp')), may hold values from -0.00021362305 to 0.00021362305
- mixer_second: float32 [13824, 512], P(('dp', 'fsdp')), may hold values from 5.1835567e-09 to 2.053862e-08
- gate_up_second: float32 [4096, 512], P(('dp', 'fsdp')), may hold values from 8.313251e-10 to 3.3253005e-09
- down_second: float32 [2048, 512], P(('dp', 'fsdp')), may hold values from 3.3253005e-09 to 1.3301202e-08
- gains_second: float32 [2, 512], P(None, ('dp', 'fsdp')), may hold values from 5.1835567e-09 to 2.053862e-08
- mixer_average: float32 [13824, 512], P(('dp', 'fsdp')), may hold values from -0.0546875 to 0.0546875
Outputs:
- output: bfloat16 [16384, 512], P(('dp', 'fsdp'))
- input_grad: float32 [16384, 512], P(('dp', 'fsdp'))
- grad_norm: float32 [], replicated
- mixer_new: float32 [13824, 512], P(('dp', 'fsdp'))
- gate_up_new: float32 [4096, 512], P(('dp', 'fsdp'))
- down_new: float32 [2048, 512], P(('dp', 'fsdp'))
- gains_new: float32 [2, 512], P(None, ('dp', 'fsdp'))
- mixer_first_new: float32 [13824, 512], P(('dp', 'fsdp'))
- gate_up_first_new: float32 [4096, 512], P(('dp', 'fsdp'))
- down_first_new: float32 [2048, 512], P(('dp', 'fsdp'))
- gains_first_new: float32 [2, 512], P(None, ('dp', 'fsdp'))
- mixer_second_new: float32 [13824, 512], P(('dp', 'fsdp'))
- gate_up_second_new: float32 [4096, 512], P(('dp', 'fsdp'))
- down_second_new: float32 [2048, 512], P(('dp', 'fsdp'))
- gains_second_new: float32 [2, 512], P(None, ('dp', 'fsdp'))
- mixer_average_new: float32 [13824, 512], P(('dp', 'fsdp'))
Inputs may be any that keep to these rules, and one draw needn't show every extreme that they name: Each row is one device's documents: either 512, 0, 0, or two lengths from 128 to 192 and a third from 0 to 128. Some row is of the first kind.
All inputs are finite; a program needn't handle non-finite values.
Results may differ from a plain program's by a relative error of at most 0.01.
Values may be sent and summed in bfloat16 or wider, within the bound.
No kernel may reach another device: no remote copies, remote signals or barrier semaphores. Data moves between devices by JAX's collectives and lax.ppermute only.
A program may use at most 192 MiB of HBM per device.

v0:
```python
import functools
import math

import jax
import jax.numpy as jnp
import numpy as np
from jax import lax
from jax.experimental import pallas as pl
from jax.experimental.pallas import tpu as pltpu
from jax.sharding import PartitionSpec as P

bf = jnp.bfloat16
f32 = jnp.float32
FILTERS = 24
AR_ORDER = 3
FF = 2048
STEP = 10
NORM_EPS = 1e-05
CLIP_LIMIT = 1.0
BETA_ONE = 0.9
BETA_TWO = 0.95
ADAM_EPS = 1e-08
RATE_MATRIX = 0.03
RATE_GAIN = 0.5
DECAY_MATRIX = 0.1
AVERAGE_KEEP = 0.9
CHIPS = ("d0", "d1", "z")
EVERY = CHIPS + ("core",)


NT = (((1,), (1,)), ((), ()))
NN = (((1,), (0,)), ((), ()))
TN = (((0,), (0,)), ((), ()))


def dot(a, b, dims=NN):
    return lax.dot_general(a, b, dims, preferred_element_type=f32)


class Chain:
    def __init__(self):
        self.token = None

    def call(self, kernel, name, args, in_specs, out_specs, out_shape, waits=(), through=(), **options):
        count, single = len(args), not isinstance(out_shape, (list, tuple)) and not through
        if single:
            out_specs, out_shape = [out_specs], [out_shape]
        made = len(out_shape)
        aliases = options.pop("input_output_aliases", {})
        aliases = {**aliases, **{count + i: made + i for i in range(len(through))}}
        last = tuple(through) + tuple(waits) + (() if self.token is None else (self.token,))

        def whole(*refs):
            first = count + len(last)
            kernel(*refs[:count], *refs[first : first + made], *refs[first + made + len(through) + 1 :])

        *outs, self.token = pl.pallas_call(
            whole,
            name=name,
            in_specs=list(in_specs) + [anywhere() for _ in last],
            out_specs=list(out_specs) + [anywhere() for _ in through] + [anywhere()],
            out_shape=list(out_shape) + [shaped(v.shape, v.dtype) for v in through] + [shaped((8, 128), f32)],
            input_output_aliases=aliases,
            compiler_params=pltpu.CompilerParams(vmem_limit_bytes=64 << 20),
            cost_estimate=pl.CostEstimate(flops=1, bytes_accessed=1, transcendentals=0),
            **options,
        )(*args, *last)
        return outs[0] if single else outs

    def pause(self, waits=(), through=()):
        return self.call(lambda: None, "pause", (), [], [], [], waits=waits, through=through)


def smem():
    return pl.BlockSpec(memory_space=pltpu.SMEM)


def anywhere():
    return pl.BlockSpec(memory_space=pl.ANY)


def fixed(*shape):
    return pl.BlockSpec(shape, lambda i: (0,) * len(shape))


NOTE = 16


def shaped(shape, dtype):
    return jax.ShapeDtypeStruct(tuple(shape), dtype)


def segment_of(place, ends_ref, group):
    return sum((place >= ends_ref[group, j]).astype(jnp.int32) for j in range(3))


def causal_mask(ends_ref, group, n, transposed):
    down = lax.broadcasted_iota(jnp.int32, (n, 1), 0)
    along = lax.broadcasted_iota(jnp.int32, (1, n), 1)
    one, two = segment_of(down, ends_ref, group), segment_of(along, ends_ref, group)
    order = (down <= along) if transposed else (down >= along)
    return ((one == two) & (one < 3) & order).astype(f32).astype(bf)


def diagonals(row, count):
    wide = jnp.broadcast_to(row, (count, row.shape[-1]))
    return pltpu.roll(wide, 0, 1, stride=1, stride_axis=0).astype(bf)


def spread_kernel(lengths_ref, came_ref, taps_ref, own_ref, other_ref, *refs):
    u_ref, mask, table, ends = refs[-4:]
    n = mask.shape[1]
    q, h, w = n // 4, n // 2, own_ref.shape[1] // 2
    per = taps_ref.shape[1]

    @pl.when(pl.program_id(0) == 0)
    def _():
        find_ends(ends, lengths_ref, came_ref)
        for g in range(2):
            mask[g] = causal_mask(ends, g, n, False)
        table[...] = jnp.zeros_like(table)

    for j in range(per):
        strip = diagonals(taps_ref[0, j : j + 1, :], q)
        for g, tokens in enumerate((own_ref, other_ref)):
            for i in range(4):
                rows, cols = slice(i * q, (i + 1) * q), slice(0, (i + 1) * q)
                table[g, rows, cols] = strip[:, (3 - i) * q :] * mask[g, rows, cols]
            upper = dot(table[g, :h, :h], tokens[:h]).astype(bf)
            lower = dot(table[g, h:, :], tokens[...]).astype(bf)
            for side in range(2):
                cols = slice(side * w, (side + 1) * w)
                u_ref[side, g * n : g * n + h, j * w : (j + 1) * w] = upper[:, cols]
                u_ref[side, g * n + h : (g + 1) * n, j * w : (j + 1) * w] = lower[:, cols]


def find_ends(ends, lengths_ref, came_ref):
    for g, ref in enumerate((lengths_ref, came_ref)):
        total = ref[0, 0]
        ends[g, 0] = total
        for j in range(1, 3):
            total = total + ref[0, j]
            ends[g, j] = total


def spread_call(chain, lengths, taps, own, other, first, steps, into=None):
    blocks, per, n = taps.shape
    w = own.shape[1] // 2
    args = [*lengths, taps, own, other]
    specs = [smem()] * 2 + [pl.BlockSpec((1, per, n), lambda i: (i + first, 0, 0)), fixed(n, 2 * w), fixed(n, 2 * w)]
    options = {}
    if into is not None:
        options = dict(input_output_aliases={len(args): 0})
        args, specs = args + [into], specs + [anywhere()]
    return chain.call(
        spread_kernel, "spread", args, specs,
        pl.BlockSpec((2, 2 * n, per * w), lambda i: (0, 0, i + first)),
        shaped((2, 2 * n, blocks * per * w), bf),
        grid=(steps,),
        scratch_shapes=[pltpu.VMEM((2, n, n), bf), pltpu.VMEM((2, n, n), bf), pltpu.SMEM((2, 3), jnp.int32)],
        **options,
    )


def run_copies(copies):
    for c in copies:
        c.start()
    for c in copies:
        c.wait()


def chip_of(spot_ref, slot, size):
    if isinstance(slot, int):
        return slot
    dy, dx, dz, fixed_z = slot
    return ((spot_ref[0] ^ dy) * 2 + (spot_ref[1] ^ dx)) * size + (dz if fixed_z else spot_ref[2] ^ dz)


def collect(spot_ref, pieces, plan, size, held, sem, columns):
    copies = []
    for at, (piece, row, rows, slot, half) in enumerate(plan):
        place = chip_of(spot_ref, slot, size)
        if half is not None:
            place = place * 2 + (spot_ref[3] ^ half)
        start = pl.multiple_of(place * rows, math.gcd(rows, 512))
        copies.append(
            pltpu.make_async_copy(pieces[piece].at[pl.ds(row, rows)], held.at[pl.ds(start, rows), columns], sem.at[at])
        )
    return copies


def mix_kernel(count, plan, notes, size, width, side, spot_ref, u_ref, *refs):
    pieces, refs = refs[:count], refs[count:]
    first = side == 0
    before, refs = refs[: 0 if first else 2], refs[0 if first else 2 :]
    if not notes:
        gains_ref, refs = refs[0], refs[1:]
    own_ref, other_ref, w_ref, *refs = refs
    if notes:
        gains_ref, refs = refs[0], refs[1:]
    held, u, sem, u_sem, *refs = refs
    *refs, result = refs
    tiles = sums = refs[0] if refs else None
    w = held.shape[1]
    filters = held.shape[0] // width
    rows = own_ref.shape[0]
    copies = collect(spot_ref, pieces, plan, size, held, sem, slice(0, w))
    for at, (piece, row, slot) in enumerate(notes):
        copies.append(
            pltpu.make_async_copy(
                pieces[piece].at[pl.ds(row, NOTE)], tiles.at[chip_of(spot_ref, slot, size)], sem.at[len(plan) + at]
            )
        )
    third = filters // 3
    cols = [pl.ds(t * third * w, third * w) for t in range(3)]
    loads = [pltpu.make_async_copy(u_ref.at[side, :, c], u.at[:, c], u_sem.at[t]) for t, c in enumerate(cols)]
    adds = [pltpu.make_async_copy(ref, sums.at[g], u_sem.at[4 + g]) for g, ref in enumerate(before)]
    for c in copies + loads + adds:
        c.start()
    for c in copies:
        c.wait()
    give = pltpu.make_async_copy(held, w_ref, u_sem.at[3])
    give.start()
    if notes:
        lanes = width // len(notes)
        for b in range(width // 128):
            block = jnp.zeros((NOTE, 128), f32)
            for j in range(128 // lanes):
                tile = tiles[b * (128 // lanes) + j].astype(f32)
                block = block + (pltpu.roll(tile, j * lanes, 1) if j else tile)
            gains_ref[:, b * 128 : (b + 1) * 128] = block
    gain = gains_ref[0:1, pl.ds(pl.multiple_of((spot_ref[3] * 2 + side) * w, w), w)]
    result[...] = jnp.zeros_like(result)

    @pl.loop(0, 3)
    def _(t):
        pltpu.make_async_copy(u_ref.at[side, :, pl.ds(0, third * w)], u.at[:, pl.ds(0, third * w)], u_sem.at[t]).wait()
        first_row = pl.multiple_of(t * third * width, width)
        wide = jnp.concatenate(
            [(held[pl.ds(first_row + k * width, width), :].astype(f32) * gain).astype(bf) for k in range(third)], axis=1
        )
        result[...] += dot(u[:, pl.ds(pl.multiple_of(t * third * w, w), third * w)], wide, NT)

    for g, out in enumerate((own_ref, other_ref)):
        mine = result[g * rows : (g + 1) * rows]
        if not first:
            adds[g].wait()
            mine = mine + sums[g]
        out[...] = mine.astype(out.dtype)
    give.wait()


def mix_call(chain, spot, u, side, pieces, plan, notes, gains, size, width, before=()):
    rows, depth = u.shape[1:]
    w = pieces[0].shape[-1]
    total = depth // w * width
    step = rows // 2
    out = fixed(step, width)
    note = fixed(NOTE, width)
    given = () if notes else (gains,)
    made = 1 - len(given)
    return chain.call(
        functools.partial(mix_kernel, len(pieces), plan, notes, size, width, side), "mix",
        (spot, u, *pieces, *before, *given),
        [smem(), anywhere()] + [anywhere() for _ in (*pieces, *before)] + [note for _ in given],
        [out, out, anywhere()] + [note] * made,
        [shaped((step, width), f32), shaped((step, width), bf if before else f32), shaped((total, w), bf)]
        + [shaped((NOTE, width), f32)] * made,
        grid=(1,),
        scratch_shapes=[
            pltpu.VMEM((total, w), bf), pltpu.VMEM((rows, depth), bf),
            pltpu.SemaphoreType.DMA((len(plan) + len(notes),)), pltpu.SemaphoreType.DMA((6,)),
        ] + [pltpu.VMEM((len(notes), NOTE, 128), bf)] * made + [pltpu.VMEM((2, step, width), f32)] * min(1, len(before))
        + [pltpu.VMEM((rows, width), f32)],
    )


def hidden_kernel(source_ref, own_ref, came_ref, gain_ref, hidden_ref, *normed_refs):
    hidden = source_ref[...].astype(f32) + (own_ref[...] + came_ref[...].astype(f32))
    scale = lax.rsqrt(jnp.mean(hidden * hidden, axis=-1, keepdims=True) + NORM_EPS)
    hidden_ref[...] = hidden
    normed = (hidden * scale * gain_ref[1:2]).astype(bf)
    width = normed_refs[0].shape[1]
    for i, ref in enumerate(normed_refs):
        ref[...] = normed[:, i * width : (i + 1) * width]


def hidden_call(chain, source, own, came, gain, parts=2):
    rows, width = source.shape
    block = pl.BlockSpec((rows // parts, width), lambda i: (i, 0))
    thin = pl.BlockSpec((rows // parts, width // 2), lambda i: (i, 0))
    return chain.call(
        hidden_kernel, "hidden", (source, own, came, gain), [block, block, block, fixed(NOTE, width)],
        [block, thin, thin], [shaped((rows, width), f32)] + [shaped((rows, width // 2), bf)] * 2,
        grid=(parts,),
    )


def norm_back(grad, hat, scale, gain):
    weighted = grad * gain
    return scale * (weighted - hat * jnp.mean(weighted * hat, axis=-1, keepdims=True))


def add_rows(ref, values, step):
    total = jnp.sum(values, axis=0, keepdims=True)

    @pl.when(step == 0)
    def _():
        ref[...] = total

    @pl.when(step > 0)
    def _():
        ref[...] += total


def turn_kernel(lengths_ref, hidden_ref, back_ref, own_ref, came_ref, gain_ref, grad_ref, low_ref, gains_ref):
    hidden = hidden_ref[...]
    scale = lax.rsqrt(jnp.mean(hidden * hidden, axis=-1, keepdims=True) + NORM_EPS)
    hat = hidden * scale
    two = own_ref[...] + came_ref[...].astype(f32)
    back = live_rows(back_ref[...].astype(f32), lengths_ref, pl.program_id(0) * hidden.shape[0])
    grad = back + norm_back(two, hat, scale, gain_ref[1:2])
    grad_ref[...] = grad
    low_ref[...] = grad.astype(bf)
    add_rows(gains_ref, two * hat, pl.program_id(0))


def turn_call(chain, lengths, hidden, back, own, came, gain, parts=2):
    rows, width = hidden.shape
    block = pl.BlockSpec((rows // parts, width), lambda i: (i, 0))
    return chain.call(
        turn_kernel, "turn", (lengths, hidden, back, own, came, gain), [smem()] + [block] * 4 + [fixed(NOTE, width)],
        [block, block, fixed(1, width)],
        [shaped((rows, width), f32), shaped((rows, width), bf), shaped((1, width), f32)],
        grid=(parts,),
    )


def output_kernel(hidden_ref, own_ref, came_ref, out_ref):
    out_ref[...] = (hidden_ref[...] + (own_ref[...] + came_ref[...].astype(f32))).astype(bf)


def output_call(chain, hidden, own, came, parts=2):
    rows, width = hidden.shape
    block = pl.BlockSpec((rows // parts, width), lambda i: (i, 0))
    return chain.call(
        output_kernel, "output", (hidden, own, came), [block] * 3, block, shaped((rows, width), bf), grid=(parts,),
    )


def last_kernel(spot_ref, grad_ref, source_ref, own_ref, came_ref, gain_ref, out_ref, one):
    half = own_ref.shape[1]
    core = spot_ref[3]
    one[:, pl.ds(pl.multiple_of(core * half, half), half)] = own_ref[...]
    one[:, pl.ds(pl.multiple_of((1 - core) * half, half), half)] = came_ref[...]
    source = source_ref[...].astype(f32)
    scale = lax.rsqrt(jnp.mean(source * source, axis=-1, keepdims=True) + NORM_EPS)
    out_ref[...] = grad_ref[...] + norm_back(one[...], source * scale, scale, gain_ref[0:1])


def last_call(chain, spot, grad_hidden, source, own, came, gain, parts=2):
    rows, width = source.shape
    block = pl.BlockSpec((rows // parts, width), lambda i: (i, 0))
    thin = pl.BlockSpec((rows // parts, width // 2), lambda i: (i, 0))
    return chain.call(
        last_kernel, "last", (spot, grad_hidden, source, own, came, gain),
        [smem(), block, block, thin, thin, fixed(NOTE, width)], block, shaped((rows, width), f32),
        grid=(parts,), scratch_shapes=[pltpu.VMEM((rows // parts, width), f32)],
    )


def grad_kernel(slots, size, side, spot_ref, gains_ref, own_ref, other_ref, u_ref, *refs):
    outs, (turned, held, sem) = refs[:-3], refs[-3:]
    n, width = own_ref.shape
    w = held.shape[1]
    per = u_ref.shape[2] // w
    step = pl.program_id(0)

    @pl.when(step == 0)
    def _():
        turned[:, :n] = own_ref[...].T
        turned[:, n:] = other_ref[...].T

    gain = gains_ref[0:1, pl.ds(pl.multiple_of((spot_ref[3] * 2 + side) * w, w), w)]
    result = dot(turned[...], u_ref[0])
    for j in range(per):
        at = pl.multiple_of((step * per + j) * width, width)
        held[pl.ds(at, width), :] = (result[:, j * w : (j + 1) * w] * gain).astype(bf)

    @pl.when(step == pl.num_programs(0) - 1)
    def _():
        rows = held.shape[0] // len(slots)
        copies, at = [], 0
        for ref in outs:
            for b in range(ref.shape[0] // rows):
                start = pl.multiple_of(chip_of(spot_ref, slots[at], size) * rows, math.gcd(rows, 512))
                copies.append(
                    pltpu.make_async_copy(held.at[pl.ds(start, rows)], ref.at[pl.ds(b * rows, rows)], sem.at[at])
                )
                at += 1
        run_copies(copies)


def grad_call(chain, spot, gains, own, other, u, side, w, blocks, slots, size, per=9):
    rows, depth = u.shape[1:]
    n, width = own.shape
    count = depth // w
    each = count * width // len(slots)
    return chain.call(
        functools.partial(grad_kernel, slots, size, side), "mixer_grad", (spot, gains, own, other, u),
        [smem(), fixed(NOTE, width), fixed(n, width), fixed(n, width), pl.BlockSpec((1, rows, per * w), lambda i: (side, 0, i))],
        [anywhere() for _ in blocks], [shaped((b * each, w), bf) for b in blocks],
        grid=(count // per,),
        scratch_shapes=[
            pltpu.VMEM((width, rows), bf), pltpu.VMEM((count * width, w), bf), pltpu.SemaphoreType.DMA((len(slots),)),
        ],
    )


def gain_rows(rows_ref, one, two, core, wide):
    devices, half = rows_ref.shape[0], one.shape[1]
    lanes = 2 * half // devices
    if lanes < 1 or 128 % lanes or 2 * lanes > 128:
        return
    wide[...] = jnp.zeros_like(wide)
    wide[:, pl.ds(pl.multiple_of(core * half, half), half)] = jnp.broadcast_to(one, (8, half))
    lane = lax.broadcasted_iota(jnp.int32, (8, 128), 1)
    for i in range(devices):
        block, turn = divmod(i * lanes, 128)
        cols = slice(block * 128, (block + 1) * 128)
        pair = []
        for tile, at in ((wide[:, cols], 0), (jnp.broadcast_to(two[:, cols], (8, 128)), lanes)):
            shift = (at - turn) % 128
            pair.append(pltpu.roll(tile, shift, 1) if shift else tile)
        row = jnp.where(lane < lanes, pair[0], jnp.where(lane < 2 * lanes, pair[1], 0.0))
        rows_ref[i : i + 1, :] = row[:1]


def back_kernel(first, spot_ref, lengths_ref, came_ref, taps_ref, own_ref, other_ref, left_ref, right_ref, *refs):
    if first:
        own_before, other_before, own_hat, other_hat, two_ref, own_out, other_out, gains_ref, rows_ref, wide, *refs = refs
        before = own_before, other_before
    else:
        own_out, other_out, *refs = refs
    mask, low_low, low_high, high, v_low, v_high, ends = refs
    n = mask.shape[1]
    q, h, d = n // 4, n // 2, own_ref.shape[1]
    per = taps_ref.shape[1]

    @pl.when(pl.program_id(0) == 0)
    def _():
        find_ends(ends, lengths_ref, came_ref)
        for g in range(2):
            mask[g] = causal_mask(ends, g, n, True)
        low_low[...] = jnp.zeros_like(low_low)
        high[...] = jnp.zeros_like(high)
        for g, ref in enumerate((own_out, other_out)):
            ref[...] = before[g][...] if first else jnp.zeros_like(ref)

    for j in range(per):
        weight = jnp.concatenate([left_ref[j * d : (j + 1) * d], right_ref[j * d : (j + 1) * d]], axis=1)
        s = diagonals(taps_ref[0, j : j + 1, :], q)
        a = j * h
        for g, grad in enumerate((own_ref, other_ref)):
            v = dot(grad[...], weight).astype(bf)
            v_low[g, a : a + h] = v[:h]
            v_high[g, a : a + h] = v[h:]
            m = mask[g]
            low_low[g, 0:q, a : a + q] = s[:, :q] * m[0:q, 0:q]
            low_low[g, 0:q, a + q : a + h] = s[:, q : 2 * q] * m[0:q, q : 2 * q]
            low_low[g, q:h, a + q : a + h] = s[:, :q] * m[q:h, q:h]
            low_high[g, 0:q, a : a + h] = s[:, 2 * q : 4 * q] * m[0:q, h:]
            low_high[g, q:h, a : a + h] = s[:, q : 3 * q] * m[q:h, h:]
            high[g, 0:q, a : a + h] = s[:, 0 : 2 * q] * m[h : h + q, h:]
            high[g, q:h, a + q : a + h] = s[:, 0:q] * m[h + q :, h + q :]
    for g, out in enumerate((own_out, other_out)):
        out[:h] += dot(low_low[g], v_low[g]) + dot(low_high[g], v_high[g])
        out[h:] += dot(high[g], v_high[g])
    if first:

        @pl.when(pl.program_id(0) == pl.num_programs(0) - 1)
        def _():
            products = own_out[...] * own_hat[...].astype(f32) + other_out[...] * other_hat[...].astype(f32)
            one = jnp.sum(products, axis=0, keepdims=True)
            gains_ref[...] = one
            gain_rows(rows_ref, one, two_ref, spot_ref[3], wide)


def back_call(chain, spot, lengths, taps, own, other, weights, first, steps, before=(), hats=(), two=None, devices=0):
    blocks, per, n = taps.shape
    rows, d = own.shape
    w = weights[0].shape[1]
    width = 2 * w
    scratch = lambda *s: pltpu.VMEM(s, bf)
    weight = pl.BlockSpec((per * d, w), lambda i: (i + first, 0))
    half = fixed(rows, width)
    more = (*before, *hats, two) if before else ()
    outs, shapes = [half] * 2, [shaped((rows, width), f32)] * 2
    scratches = [
        scratch(2, n, n), scratch(2, n // 2, per * n // 2),
        scratch(2, n // 2, per * n // 2), scratch(2, n // 2, per * n // 2),
        scratch(2, per * n // 2, width), scratch(2, per * n // 2, width), pltpu.SMEM((2, 3), jnp.int32),
    ]
    if before:
        outs = outs + [fixed(1, width), fixed(devices, 128)]
        shapes = shapes + [shaped((1, width), f32), shaped((devices, 128), f32)]
        scratches = [pltpu.VMEM((8, 2 * width), f32)] + scratches
    return chain.call(
        functools.partial(back_kernel, first), "spread_back", (spot, *lengths, taps, own, other, *weights, *more),
        [smem()] * 3 + [pl.BlockSpec((1, per, n), lambda i: (i + first, 0, 0)), fixed(rows, d), fixed(rows, d)]
        + [weight, weight] + [fixed(*v.shape) for v in more],
        outs, shapes, grid=(steps,), scratch_shapes=scratches,
    )


def flat(v):
    return v.reshape(-1, v.shape[-1])


def ffn_kernel(count, outs, steps, slots, out_slots, size, crossed, spot_ref, lengths_ref, came_ref, *refs):
    turned = spot_ref[3] if crossed else 0
    tokens, pieces, refs = refs[:6], refs[6 : 6 + count], refs[6 + count :]
    results, grads, (held, dealt, normed, back, sums, sem) = refs[:4], refs[4 : 4 + outs], refs[4 + outs :]
    n = tokens[0].shape[0]
    chips, units, width = held.shape[0], held.shape[1] * 2 // 3, held.shape[2]
    own, half = chips // 2 // steps, units // 2
    step = pl.program_id(0)

    @pl.when(step == 0)
    def _():
        copies, at = [], 0
        for ref in pieces:
            for b in range(ref.shape[0]):
                chip = chip_of(spot_ref, slots[at], size)
                copies.append(
                    pltpu.make_async_copy(ref.at[b, pl.ds(0, units)], held.at[chip, pl.ds(0, units)], sem.at[0, at])
                )
                copies.append(
                    pltpu.make_async_copy(
                        ref.at[b, pl.ds(units, half)], held.at[chip ^ turned, pl.ds(units, half)], sem.at[1, at]
                    )
                )
                at += 1
        for c in copies:
            c.start()
        half_width = tokens[0].shape[1]
        for i in range(2):
            cols = slice(i * half_width, (i + 1) * half_width)
            normed[:n, cols], normed[n:, cols] = tokens[i][...], tokens[2 + i][...]
        back[:n] = live_rows(tokens[4][...].astype(f32), lengths_ref).astype(bf)
        back[n:] = live_rows(tokens[5][...].astype(f32), came_ref).astype(bf)
        for c in copies:
            c.wait()

    w_gate = flat(held[pl.ds(step * own, own), 0:units])
    w_up = flat(held[pl.ds(chips // 2 + step * own, own), 0:units])
    w_down = flat(held[pl.ds(step * 2 * own, 2 * own), units : units + half])
    gate, up = dot(normed[...], w_gate, NT), dot(normed[...], w_up, NT)
    grad_act = dot(back[...], w_down, NT)
    sigma = 1.0 / (1.0 + jnp.exp(-gate))
    swish = gate * sigma
    act = (swish * up).astype(bf)
    grad_gate = (grad_act * up * (sigma * (1.0 + gate * (1.0 - sigma)))).astype(bf)
    grad_up = (grad_act * swish).astype(bf)
    branch = dot(act, w_down)
    two = dot(jnp.concatenate([grad_gate, grad_up], axis=1), jnp.concatenate([w_gate, w_up], axis=0))
    for i, value in enumerate((branch, two)):
        if steps > 1:

            @pl.when(step == 0)
            def _():
                sums[i] = value

            @pl.when((step > 0) & (step < steps - 1))
            def _():
                sums[i] += value

        @pl.when(step == steps - 1)
        def _():
            total = value + sums[i] if steps > 1 else value
            results[2 * i][...] = total[:n]
            results[2 * i + 1][...] = total[n:].astype(bf)

    put = lambda v: v.astype(bf).reshape(own, units, width)
    dealt[pl.ds(step * own, own), 0:units] = put(dot(grad_gate, normed[...], TN))
    dealt[pl.ds(chips // 2 + step * own, own), 0:units] = put(dot(grad_up, normed[...], TN))
    grad_down = dot(act, back[...], TN).astype(bf)
    for b in range(2 * own):
        dealt[(step * 2 * own + b) ^ turned, units : units + half] = grad_down[b * half : (b + 1) * half]

    @pl.when(step == steps - 1)
    def _():
        copies, at = [], 0
        for ref in grads:
            for b in range(ref.shape[0]):
                copies.append(
                    pltpu.make_async_copy(dealt.at[chip_of(spot_ref, out_slots[at], size)], ref.at[b], sem.at[0, at])
                )
                at += 1
        run_copies(copies)


def ffn_call(chain, spot, lengths, tokens, pieces, blocks, slots, out_slots, size, crossed, chunk=512):
    n, d = tokens[-1].shape
    chips, rows = len(slots), pieces[0].shape[1]
    units = rows * 2 // 3
    steps = chips // 2 * units // chunk
    return chain.call(
        functools.partial(ffn_kernel, len(pieces), len(blocks), steps, slots, out_slots, size, crossed), "ffn",
        (spot, *lengths, *tokens, *pieces),
        [smem()] * 3 + [fixed(*v.shape) for v in tokens] + [anywhere() for _ in pieces],
        [fixed(n, d)] * 4 + [anywhere() for _ in blocks],
        [shaped((n, d), f32), shaped((n, d), bf)] * 2 + [shaped((b, rows, d), bf) for b in blocks],
        grid=(steps,),
        scratch_shapes=[
            pltpu.VMEM((chips, rows, d), bf), pltpu.VMEM((chips, rows, d), bf),
            pltpu.VMEM((2 * n, d), bf), pltpu.VMEM((2 * n, d), bf), pltpu.VMEM((2, 2 * n, d), f32),
            pltpu.SemaphoreType.DMA((2, chips)),
        ],
    )


def normed_kernel(spot_ref, own_ref, other_ref, own_out, other_out, full):
    half = own_out.shape[1]
    cols = pl.ds(pl.multiple_of(spot_ref[3] * half, half), half)
    for ref, out in ((own_ref, own_out), (other_ref, other_out)):
        source = ref[...].astype(f32)
        scale = lax.rsqrt(jnp.mean(source * source, axis=-1, keepdims=True) + NORM_EPS)
        full[...] = (source * scale).astype(bf)
        out[...] = full[:, cols]


def normed_call(chain, spot, own, other, parts=2):
    rows, width = own.shape
    block = pl.BlockSpec((rows // parts, width), lambda i: (i, 0))
    thin = pl.BlockSpec((rows // parts, width // 2), lambda i: (i, 0))
    return chain.call(
        normed_kernel, "normed", (spot, own, other), [smem(), block, block],
        [thin] * 2, [shaped((rows, width // 2), bf)] * 2,
        grid=(parts,), scratch_shapes=[pltpu.VMEM((rows // parts, width), bf)],
    )


def live_rows(values, lengths_ref, first=0):
    total = lengths_ref[0, 0] + lengths_ref[0, 1] + lengths_ref[0, 2]
    place = lax.broadcasted_iota(jnp.int32, (values.shape[0], 1), 0) + first
    return jnp.where(place < total, values, jnp.zeros((), values.dtype))


def pack_kernel(
    spot_ref, mixer_ref, gate_up_ref, down_ref, gains_ref, mixer_mine, mixer_theirs, gate_mine, gate_theirs, down_low, note
):
    half, units, core = mixer_mine.shape[1], gate_mine.shape[0], spot_ref[3]
    for ref, cols, rows, c in ((mixer_mine, half, units, core), (mixer_theirs, half, units, 1 - core)):
        ref[...] = mixer_ref[:, pl.ds(pl.multiple_of(c * half, half), half)].astype(bf)
    for ref, c in ((gate_mine, core), (gate_theirs, 1 - core)):
        ref[:units] = gate_up_ref[pl.ds(pl.multiple_of(c * units, units), units), :].astype(bf)
    count, own = gains_ref.shape
    note[...] = jnp.zeros_like(note)
    note[:count, :own] = gains_ref[...].astype(bf)
    gate_theirs[units:] = jnp.zeros((note.shape[0], gate_theirs.shape[1]), bf)
    gate_theirs[units:, : note.shape[1]] = note[...]
    down_low[...] = down_ref[...].astype(bf)


def pack_call(chain, spot, mixer, gate_up, down, gains):
    (rows, width), (units, _), (half, _) = mixer.shape, gate_up.shape, down.shape
    shapes = [(rows, width // 2)] * 2 + [(units // 2, width), (units // 2 + NOTE, width), (half, width), (NOTE, 128)]
    return chain.call(
        pack_kernel, "pack", (spot, mixer, gate_up, down, gains),
        [smem(), fixed(rows, width), fixed(units, width), fixed(half, width), fixed(*gains.shape)],
        [fixed(*s) for s in shapes], [shaped(s, bf) for s in shapes], grid=(1,),
    )


def block_kernel(own_gains, spot_ref, mine_ref, came_ref, note_ref, gate_ref, all_ref, copies_ref):
    rows, w = mine_ref.shape[0], all_ref.shape[1]
    mine = note_ref[...].astype(f32)
    came = gate_ref[gate_ref.shape[0] - NOTE :, :w].astype(f32)
    turned = lambda v: pltpu.roll(v, own_gains, 1)
    note = jnp.where(spot_ref[3] == 0, mine + turned(came), came + turned(mine)).astype(bf)
    at = 0
    for side in range(2):
        cols = slice(side * w, (side + 1) * w)
        all_ref[at : at + rows] = mine_ref[:, cols]
        all_ref[at + rows : at + 2 * rows] = came_ref[:, cols]
        all_ref[at + 2 * rows : at + 2 * rows + NOTE] = note
        at += 2 * rows + NOTE
    count = 2 * rows + NOTE
    for c in range(copies_ref.shape[0] // count):
        copies_ref[c * count : (c + 1) * count] = all_ref[:count]


def block_call(chain, spot, mine, came, note, gate_came, own_gains, copies, waits):
    rows, width = mine.shape
    w = width // 2
    each = 2 * rows + NOTE
    return chain.call(
        functools.partial(block_kernel, own_gains), "block", (spot, mine, came, note, gate_came),
        [smem()] + [fixed(*v.shape) for v in (mine, came, note, gate_came)],
        [fixed(2 * each, w), fixed(copies * each, w)], [shaped((2 * each, w), bf), shaped((copies * each, w), bf)],
        grid=(1,), waits=waits,
    )


def stack_kernel(count, moves, spot_ref, *refs):
    for i, a, rows, o, b in moves:
        if not isinstance(a, int):
            stride, distance, first = a
            a = pl.multiple_of((spot_ref[2] ^ distance) * stride + first, NOTE)
        refs[count + o][b : b + rows] = refs[i][pl.ds(a, rows)]


def stack_call(chain, spot, arrays, rows, moves, waits=()):
    like = {o: arrays[i] for i, _, _, o, _ in moves}
    shapes = [(r,) + like[o].shape[1:] for o, r in enumerate(rows)]
    return chain.call(
        functools.partial(stack_kernel, len(arrays), moves), "stack", (spot, *arrays),
        [smem()] + [fixed(*v.shape) for v in arrays],
        [fixed(*s) for s in shapes], [shaped(s, like[o].dtype) for o, s in enumerate(shapes)], grid=(1,), waits=waits,
    )


def corner_kernel(cut, extra, x_ref, y_ref, to_x_ref, to_y_ref):
    rows = x_ref.shape[0]
    to_x_ref[:cut] = y_ref[:cut]
    if extra:
        to_x_ref[cut:] = y_ref[rows - extra :]
    to_y_ref[...] = x_ref[cut : rows - extra]


def corner_call(chain, from_x, from_y, extra):
    total, width = from_x.shape
    cut = (total - extra) // 2
    shapes = [(cut + extra, width), (cut, width)]
    return chain.call(
        functools.partial(corner_kernel, cut, extra), "corner", (from_x, from_y), [fixed(total, width)] * 2,
        [fixed(*s) for s in shapes], [shaped(s, bf) for s in shapes], grid=(1,),
    )


def near_kernel(to_x_ref, to_y_ref, by_x_ref, by_y_ref, new_x_ref, new_y_ref):
    new_x_ref[...] = (to_x_ref[...].astype(f32) + by_y_ref[...].astype(f32)).astype(bf)
    new_y_ref[...] = (to_y_ref[...].astype(f32) + by_x_ref[...].astype(f32)).astype(bf)


def near_call(chain, to_x, to_y, by_x, by_y, parts=2, **options):
    rows, width = by_x.shape
    block = (rows // parts, width)
    low, high = pl.BlockSpec(block, lambda i: (i, 0)), pl.BlockSpec(block, lambda i: (i + parts, 0))
    return chain.call(
        near_kernel, "near", (to_x, to_y, by_x, by_y), [high, low, low, low], [high, low],
        [shaped(to_x.shape, bf), shaped(to_y.shape, bf)], grid=(parts,), input_output_aliases={0: 0, 1: 1}, **options,
    )


def line_kernel(count, *refs):
    parts, refs = refs[:count], refs[count:]
    rows = refs[-1].shape[0]

    def total(at):
        result = parts[0][pl.ds(at, rows)].astype(f32)
        for ref in parts[1:]:
            result = result + ref[pl.ds(at, rows)].astype(f32)
        return result

    for s, ref in enumerate(refs):
        ref[...] = total(s * rows).astype(ref.dtype)


def line_call(chain, parts, size, apart, **options):
    quarters = 4 if len(parts) == 1 else 1
    rows, width = parts[0].shape[0] // quarters // size, parts[0].shape[1]
    if apart:
        whole = lambda q: pl.BlockSpec((size * rows, width), lambda i: (q, 0))
        ins = [whole(q) for q in range(quarters)] if quarters > 1 else [whole(0)] * len(parts)
        specs = [fixed(rows, width)] * size
        shapes = [shaped((rows, width), f32)] + [shaped((rows, width), bf)] * (size - 1)
        steps = 1
    else:
        steps = 2
        half = size * rows // steps
        ins = [pl.BlockSpec((half, width), lambda i, q=q: (i + q * steps, 0)) for q in range(quarters)]
        ins = ins if quarters > 1 else ins * len(parts)
        specs, shapes = [pl.BlockSpec((half, width), lambda i: (i, 0))], [shaped((size * rows, width), bf)]
    parts = parts * quarters
    return chain.call(
        functools.partial(line_kernel, len(parts)), "line", parts, ins, specs, shapes, grid=(steps,), **options
    )


def finish_kernel(cuts, count, note, spot_ref, first_ref, *refs):
    came, more, outs, squares_ref, total = (
        refs[:count], refs[count : -len(cuts) - 2], refs[-len(cuts) - 2 : -2], refs[-2], refs[-1]
    )
    rows = total.shape[0]
    result = first_ref[:rows].astype(f32)
    for b in range(1, first_ref.shape[0] // rows):
        result = result + first_ref[b * rows : (b + 1) * rows].astype(f32)
    for ref in came:
        result = result + ref[...].astype(f32)
    total[...] = result
    squares = jnp.sum(result * result, axis=0, keepdims=True)
    if note:
        whole = jnp.sum(squares, axis=1, keepdims=True)
        for ref in more[:-1]:
            whole = whole + jnp.sum(ref[...], axis=1, keepdims=True)
        gains = jnp.sum(more[-1][...], axis=0, keepdims=True)
        squares = jnp.broadcast_to(whole + jnp.sum(gains * gains, axis=1, keepdims=True), squares_ref.shape)
    squares_ref[...] = squares
    for ref, start in zip(outs, cuts):
        rows = ref.shape[0]
        if not isinstance(start, int):
            start = pl.multiple_of((spot_ref[3] ^ start[0]) * rows, rows & -rows)
        ref[...] = total[pl.ds(start, rows), :]


def finish_call(chain, spot, first, came, blocks, cuts, note=0, more=(), waits=()):
    rows, width = first.shape[0] // blocks, first.shape[1]
    shapes = [(r, width) for _, r in cuts] + [(note, 128) if note else (1, width)]
    return chain.call(
        functools.partial(finish_kernel, [c for c, _ in cuts], len(came), note), "finish", (spot, first, *came, *more),
        [smem(), fixed(*first.shape)] + [fixed(rows, width)] * len(came) + [fixed(*v.shape) for v in more],
        [fixed(*s) for s in shapes], [shaped(s, f32) for s in shapes],
        grid=(1,), scratch_shapes=[pltpu.VMEM((rows, width), f32)], waits=waits,
    )


def adam_step(weight, grad, first, second, rate, decay):
    first_new = BETA_ONE * first + (1.0 - BETA_ONE) * grad
    second_new = BETA_TWO * second + (1.0 - BETA_TWO) * grad * grad
    corr_one = 1.0 / (1.0 - BETA_ONE**STEP)
    corr_two = 1.0 / (1.0 - BETA_TWO**STEP)
    update = first_new * (rate * corr_one) / (jnp.sqrt(second_new * corr_two) + ADAM_EPS)
    return (weight * (1.0 - rate * decay) - update, first_new, second_new)


def adam_kernel(spot_ref, note_ref, *refs):
    ins, outs, wide, tall = refs[:21], refs[21:35], refs[35], refs[36]
    mixer, gate_up, down, gains, parts = ins[:4], ins[4:7], ins[7:10], ins[10:13], ins[13:]
    mixer_out, gate_up_out, down_out, gains_out, norm_out = outs[:4], outs[4:7], outs[7:10], outs[10:13], outs[13]
    core, quarter = spot_ref[3], parts[0].shape[1]
    norm = jnp.sqrt(jnp.sum(note_ref[...], axis=0, keepdims=True)[:, :1])
    factor = CLIP_LIMIT / jnp.maximum(norm, CLIP_LIMIT)

    rows, step = mixer[0].shape[0], wide.shape[0]

    @pl.loop(0, rows // step)
    def _(i):
        at = pl.ds(pl.multiple_of(i * step, step & -step), step)
        for s in range(2):
            mine = pl.multiple_of(core * 2 * quarter, quarter) + s * quarter
            came = pl.multiple_of((1 - core) * 2 * quarter, quarter) + s * quarter
            wide[:, pl.ds(pl.multiple_of(mine, quarter), quarter)] = parts[s][at]
            wide[:, pl.ds(pl.multiple_of(came, quarter), quarter)] = parts[2 + s][at]
        old, first, second, average = (r[at] for r in mixer)
        new, first, second = adam_step(old, wide[...] * factor, first, second, RATE_MATRIX, DECAY_MATRIX)
        average = AVERAGE_KEEP * average + (1.0 - AVERAGE_KEEP) * new
        for ref, value in zip(mixer_out, (new, first, second, average)):
            ref[at] = value

    @pl.when(pl.program_id(0) == 0)
    def _():
        half = parts[4].shape[0]
        tall[pl.ds(pl.multiple_of(core * half, half), half), :] = parts[4][...]
        tall[pl.ds(pl.multiple_of((1 - core) * half, half), half), :] = parts[5][...]
        own = gains[0].shape[1]
        sums = jnp.sum(parts[7][...], axis=0, keepdims=True)
        gain_grad = jnp.concatenate([sums[:, :own], sums[:, own : 2 * own]])
        for olds, news, grad, rate, decay in (
            (gate_up, gate_up_out, tall[...], RATE_MATRIX, DECAY_MATRIX),
            (down, down_out, parts[6][...], RATE_MATRIX, DECAY_MATRIX),
            (gains, gains_out, gain_grad, RATE_GAIN, 0.0),
        ):
            old, first, second = (r[...] for r in olds)
            scale = factor if rate == RATE_MATRIX else factor[:, :1]
            for ref, value in zip(news, adam_step(old, grad * scale, first, second, rate, decay)):
                ref[...] = value
        norm_out[...] = norm


def adam_call(chain, spot, note, mixer, gate_up, down, gains, parts, blocks=1):
    rows, width = mixer[0].shape
    step = rows // blocks
    block = pl.BlockSpec((step, width), lambda i: (i, 0))
    piece = pl.BlockSpec((step, parts[0].shape[1]), lambda i: (i, 0))
    whole = lambda v: fixed(*v.shape)
    others = [*gate_up, *down, *gains]
    shapes = [v.shape for v in (*mixer, *others)] + [(1, 1)]
    return chain.call(
        adam_kernel, "adam", (spot, note, *mixer, *others, *parts),
        [smem(), whole(note)] + [block] * 4 + [whole(v) for v in others] + [piece] * 4
        + [whole(v) for v in parts[4:]],
        [block] * 4 + [whole(v) for v in others] + [fixed(1, 1)], [shaped(s, f32) for s in shapes],
        grid=(blocks,),
        scratch_shapes=[pltpu.VMEM((step // 3, width), f32), pltpu.VMEM(gate_up[0].shape, f32)],
    )


def flip(v, axis, bits=1):
    size = lax.axis_size(axis)
    return lax.ppermute(v, axis, [(i, i ^ bits) for i in range(size)])


def swap(v):
    return flip(v, "core")


def join(mine, other, core, axis=0):
    return jnp.where(
        core == 0,
        jnp.concatenate([mine, other], axis=axis),
        jnp.concatenate([other, mine], axis=axis),
    )


def part(v, index, axis=0):
    size = v.shape[axis] // 2
    return lax.dynamic_slice_in_dim(v, index * size, size, axis)


def low(v):
    return v.astype(bf)


def wide(v):
    return v.astype(f32)


class Whole:
    crossed = False
    mixer_slots = ((0,), (0,))
    mixer_blocks = (1,)

    def __init__(self, spot, groups):
        self.spot, self.core = spot, spot[3]
        self.size = lax.axis_size("z")
        self.chips = lax.axis_size("d0") * lax.axis_size("d1") * self.size
        self.ffn_in = self.ffn_out = tuple(range(groups))
        self.ffn_blocks = (groups,)

    def gather(self, chain, mixer, gate_up, down, gains, waits):
        def trade(v, axis):
            return join(part(v, self.core, axis), swap(part(v, 1 - self.core, axis)), self.core)

        everything = lambda v: lax.all_gather(v, CHIPS, axis=0, tiled=True)
        mixer_block = trade(low(mixer), 1)
        w, groups = mixer_block.shape[1] // 2, len(self.ffn_in)
        sides = []
        for s in range(2):
            whole = everything(mixer_block[:, s * w : (s + 1) * w])
            sides.append(([whole], ((0, 0, whole.shape[0], 0, None),), ()))
        ffn = [everything(v).reshape(groups, -1, v.shape[1]) for v in (trade(low(gate_up), 0), low(down))]
        ffn = [jnp.concatenate(ffn, axis=1)]
        gains = lax.all_gather(wide(low(gains)), EVERY, axis=1, tiled=True)
        yield jnp.pad(gains, ((0, NOTE - 2), (0, 0)))
        while True:
            yield sides, ffn

    def scatter(self, chain, parts, cuts, groups=1, apart=False):
        grads = parts[0].reshape(groups, -1, parts[0].shape[-1])
        rows = grads.shape[1] * 2 // 3
        if groups > 1:
            shards = [grads[:, :rows], grads[:, rows:]]
        else:
            shards = [grads]
        shards = [wide(lax.psum_scatter(flat(v), CHIPS, scatter_dimension=0, tiled=True)) for v in shards]
        outs = [part(shards[0], self.core), part(shards[0], 1 - self.core)] + shards[1:]
        squares = sum(jnp.sum(v * v, axis=0, keepdims=True) for v in shards)
        if groups == 1:
            yield
            yield ()
        through = yield ()
        yield (), through
        yield
        yield outs + [squares]

    def spread_gains(self, grads, rows):
        one, two = grads
        nothing = jnp.zeros_like(one)
        one = join(one, nothing, self.core, 1)
        return lax.psum_scatter(jnp.concatenate([one, two]), EVERY, scatter_dimension=1, tiled=True)

    def total(self, v):
        return lax.psum(v, EVERY)


class Cube(Whole):
    crossed = True
    near = ((0, 0), (0, 1), (1, 0), (1, 1))

    def __init__(self, spot, groups):
        super().__init__(spot, groups)
        slots = lambda fixed_z: tuple((y, x, s, fixed_z) for y, x in self.near for s in range(self.size))
        self.mixer_slots = slots(False), slots(True)
        self.ffn_in = slots(True)
        self.ffn_out = tuple((y, x, z, True) for z in range(self.size) for y, x in self.near)
        self.mixer_blocks = (self.size,) * 3 + (self.size // 2,) * 2

    def lines(self, block):
        return [flip(block, "z", s) for s in range(1, self.size)]

    def gather(self, chain, mixer, gate_up, down, gains, waits):
        spot = self.spot
        mixer_mine, mixer_theirs, gate_mine, gate_theirs, down_low, note = pack_call(
            chain, spot, mixer, gate_up, down, gains
        )
        gate_came = swap(gate_theirs)
        size = self.size
        own, block = block_call(
            chain, spot, mixer_mine, swap(mixer_theirs), note, gate_came, gains.shape[1], size, waits
        )
        line = self.along_z(block)
        own_x, own_y = flip(own, "d1"), flip(own, "d0")
        yield None
        rows = own.shape[0] // 2 - NOTE
        half = rows // 2
        sides = []

        def spread_out(line):
            return line, flip(line, "d1"), flip(line, "d0")

        def turn_corner(from_x, from_y, extra=0):
            to_x, to_y = corner_call(chain, from_x, from_y, extra)
            return flip(to_x, "d1"), flip(to_y, "d0")

        def plan(side):
            found = [(p, side * (rows + NOTE) + h * half, half, near + (0, False), h) for p, near in enumerate(self.near[:3]) for h in range(2)]
            found += [(3, h * half, half, (1, 1, 0, False), h) for h in range(2)]
            last = (size - 1) * 2
            for at in range(last):
                s, h = at // 2 + 1, at % 2
                found += [(4 + p, at * half, half, near + (s, False), h) for p, near in enumerate(self.near[:3])]
                found.append((7 + (at >= last // 2), at % (last // 2) * half, half, (1, 1, s, False), h))
            return tuple(found)

        corner = turn_corner(own_x, own_y)
        yield
        chain.pause(corner)
        others, line_rows = range(1, size), (size - 1) * rows
        moves = [(0, (rows + NOTE, s, 0), rows, 0, (s - 1) * rows) for s in others]
        moves += [(0, (rows + NOTE, s, rows), NOTE, 0, line_rows + (s - 1) * NOTE) for s in others]
        moves += [(1, rows + NOTE, rows, 1, s * rows) for s in range(size)]
        line, block = stack_call(
            chain, spot, (line, own), (line_rows + (size - 1) * NOTE, size * rows), tuple(moves)
        )
        first = spread_out(line)
        line = self.along_z(block)
        yield
        first_corner = turn_corner(*first[1:], (size - 1) * NOTE)
        notes = [(p, rows, near + (0, False)) for p, near in enumerate(self.near)]
        for s in others:
            notes += [(4 + p, line_rows + (s - 1) * NOTE, near + (s, False)) for p, near in enumerate(self.near[:3])]
            notes.append((7, line_rows // 2 + (s - 1) * NOTE, (1, 1, s, False)))
        sides.append(([own, own_x, own_y, corner[0], *first, *first_corner], plan(0), tuple(notes)))
        units, count = gate_mine.shape[0], down_low.shape[0]
        ffn_rows = 2 * units + count
        moves = [(0, (rows, s, 0), rows, 0, (s - 1) * rows) for s in others]
        for s in range(size):
            at = s * ffn_rows
            moves += [(1, 0, units, 1, at), (2, 0, units, 1, at + units), (3, 0, count, 1, at + 2 * units)]
        line, block = stack_call(
            chain, spot, (line, gate_mine, gate_came, down_low), (line_rows, size * ffn_rows), tuple(moves)
        )
        across, line = line, self.along_z(block)
        second = spread_out(*chain.pause(first_corner, (across,)))
        yield sides, None
        second_corner = turn_corner(*second[1:])
        sides.append(([own, own_x, own_y, corner[1], *second, *second_corner], plan(1), ()))
        ffn = spread_out(*chain.pause(second_corner, (line,)))
        yield sides, None
        ffn = (*ffn, *turn_corner(*ffn[1:]))
        yield sides, [v.reshape(-1, ffn_rows, v.shape[-1]) for v in ffn]

    def along_z(self, v):
        return lax.all_to_all(v, "z", 0, 0, tiled=True)

    def scatter(self, chain, parts, cuts, groups=1, apart=False):
        if groups > 1:
            came = (self.along_z(flat(parts[0])),)
        else:
            own, to_x, to_y, far_low, far_high = (flat(v) for v in parts)
            by_x, by_y = flip(far_low, "d1"), flip(far_high, "d0")
            yield
            to_x, to_y = yield near_call(chain, to_x, to_y, by_x, by_y)
            came = own, flip(to_x, "d1"), flip(to_y, "d0")
        through = yield came
        outs = line_call(chain, came, self.size, apart, through=through or ())
        count = self.size if apart else 1
        first, *rest = yield outs[:count], outs[count:]
        if groups > 1:
            to_x, to_y, far = rest
            far = lax.ppermute(far, ("d0", "d1"), [(i, i ^ 3) for i in range(4)])
            came = flip(to_x, "d1"), flip(to_y, "d0"), far
        elif apart:
            came = [flip(v, "z", s + 1) for s, v in enumerate(rest)]
        else:
            first, came = self.along_z(first), ()
        more, waits = yield
        yield finish_call(
            chain, self.spot, first, came, 1 if apart else self.size, cuts, 2 * self.chips if more else 0, more, waits
        )

    def spread_gains(self, grads, rows):
        return self.everyone(rows)

    def everyone(self, rows):
        return lax.all_to_all(rows, EVERY, 0, 0, tiled=True)


def body(
    inputs, lengths, filters, cotangent, mixer_weight, gate_up_weight, down_weight, norm_gains,
    mixer_first, gate_up_first, down_first, gains_first,
    mixer_second, gate_up_second, down_second, gains_second, mixer_average,
):
    slots, width = inputs.shape
    size = lax.axis_size("z")
    groups = 2 * FF // 256
    cube = lax.axis_size("d0") == 2 and lax.axis_size("d1") == 2 and size == 4
    spot = jnp.stack([lax.axis_index(a) for a in EVERY]).astype(jnp.int32)
    core = spot[3]
    links = (Cube if cube else Whole)(spot, groups)
    units = gate_up_weight.shape[0]
    chain = Chain()

    sums = lengths, swap(lengths)
    source_other, cotangent_other = swap(inputs), swap(cotangent)
    taps = jnp.concatenate([wide(filters), jnp.eye(AR_ORDER, slots, dtype=f32)])
    taps_turned = jnp.roll(taps[:, ::-1], 1 - slots // 4, axis=1)
    taps, taps_turned = (v.reshape(-1, 3, slots) for v in (taps, taps_turned))

    weights = links.gather(
        chain, mixer_weight, gate_up_weight, down_weight, norm_gains, (sums[1], source_other, cotangent_other)
    )
    gains = next(weights)
    tokens = hat_tokens = normed_call(chain, spot, inputs, source_other)
    blocks = taps.shape[0]
    cuts, spread = (0, blocks // 3, blocks * 4 // 9, blocks), None
    for at in range(3):
        spread = spread_call(chain, sums, taps_turned, *tokens, cuts[at], cuts[at + 1] - cuts[at], spread)
        sides = next(weights)
    sides, _ = sides
    quarter = sides[0][0][0].shape[1]
    *mixed, left, gains = (*mix_call(chain, spot, spread, 0, *sides[0], gains, size, width), gains)[:4]
    sides, _ = next(weights)
    mixed_own, mixed_other, right = mix_call(chain, spot, spread, 1, *sides[1], gains, size, width, mixed)
    _, ffn = next(weights)

    hidden, *normed_two = hidden_call(chain, inputs, mixed_own, swap(mixed_other), gains)
    tokens = (*normed_two, *(swap(v) for v in normed_two), cotangent, cotangent_other)
    branch_own, branch_other, two_own, two_other, *grad_ffn = ffn_call(
        chain, spot, sums, tokens, ffn, links.ffn_blocks, links.ffn_in, links.ffn_out, size, links.crossed
    )
    if cube:
        grad_ffn = chain.pause(through=grad_ffn)
    ffn_sum = links.scatter(chain, grad_ffn, ((0, units // 2), (units // 2, units // 2), (units, units // 2)), groups, True)
    ffn_came = next(ffn_sum)
    grad_hidden, grad_low, gains_two = turn_call(
        chain, lengths, hidden, cotangent, two_own, swap(two_other), gains
    )
    grad_other = swap(grad_low)
    rows = mixer_weight.shape[0]
    cuts = (((0,), rows), ((1,), rows))
    grads_of = lambda s: grad_call(
        chain, spot, gains, grad_low, grad_other, spread, s, quarter, links.mixer_blocks, links.mixer_slots[s], size
    )
    first_sum = links.scatter(chain, grads_of(0), cuts, apart=True)
    next(first_sum)
    second_sum = links.scatter(chain, grads_of(1), cuts)
    next(second_sum)
    backward = lambda first, steps, *more: back_call(
        chain, spot, sums, taps, grad_low, grad_other, (left, right), first, steps, *more
    )
    early = blocks // 2
    first_sum.send(next(first_sum))
    one = backward(0, early)
    second_sum.send(next(second_sum))
    one_own, one_other, gains_one, note_rows = backward(
        early, blocks - early, one, hat_tokens, gains_two, 2 * links.chips
    )
    outs, _ = first_sum.send(())
    first_sum.send(outs)
    if cube:
        (note_rows,) = chain.pause(ffn_came, (note_rows,))
    shard_gains = links.spread_gains((gains_one, gains_two), note_rows)
    outs, _ = second_sum.send(())
    chain.pause((shard_gains,))
    first_mine, first_theirs, square = first_sum.send(((), ()))
    first_theirs, branch_other, *outs = chain.pause(through=(first_theirs, branch_other, *outs))
    second_sum.send(outs)
    outs, _ = ffn_sum.send(())
    ffn_sum.send(outs)
    output = output_call(chain, hidden, branch_own, swap(branch_other))
    input_grad = last_call(chain, spot, grad_hidden, inputs, one_own, swap(one_other), gains)
    gate_up_mine, gate_up_theirs, shard_down, *squares = ffn_sum.send(((), ()))
    squares.append(square)
    gate_up_came, first_came = swap(gate_up_theirs), swap(first_theirs)
    second_mine, second_theirs, note = second_sum.send(((*squares, shard_gains), ()))
    second_came = swap(second_theirs)
    mixer = mixer_weight, mixer_first, mixer_second, mixer_average
    gate_up, down = (gate_up_weight, gate_up_first, gate_up_second), (down_weight, down_first, down_second)
    gain = norm_gains, gains_first, gains_second
    if cube:
        (
            mixer_new, mixer_first_new, mixer_second_new, mixer_average_new, gate_up_new, gate_up_first_new,
            gate_up_second_new, down_new, down_first_new, down_second_new, gains_new, gains_first_new, gains_second_new,
            grad_norm,
        ) = adam_call(
            chain, spot, links.everyone(note), mixer, gate_up, down, gain,
            (first_mine, second_mine, first_came, second_came, gate_up_mine, gate_up_came, shard_down, shard_gains),
        )
        grad_norm = grad_norm[0, 0]
    else:
        squares = sum(jnp.sum(v) for v in (*squares, note)) + jnp.sum(shard_gains * shard_gains)
        grad_norm = jnp.sqrt(links.total(squares))
        factor = CLIP_LIMIT / jnp.maximum(grad_norm, CLIP_LIMIT)
        shard_mixer = join(
            jnp.concatenate([first_mine, second_mine], axis=1), jnp.concatenate([first_came, second_came], axis=1), core, 1
        )
        shard_gate_up = join(gate_up_mine, gate_up_came, core)
        step = lambda old, grad: adam_step(old[0], grad * factor, old[1], old[2], RATE_MATRIX, DECAY_MATRIX)
        mixer_new, mixer_first_new, mixer_second_new = step(mixer, shard_mixer)
        gate_up_new, gate_up_first_new, gate_up_second_new = step(gate_up, shard_gate_up)
        down_new, down_first_new, down_second_new = step(down, shard_down)
        gains_new, gains_first_new, gains_second_new = adam_step(
            gain[0], shard_gains * factor, gain[1], gain[2], RATE_GAIN, 0.0
        )
        mixer_average_new = AVERAGE_KEEP * mixer_average + (1.0 - AVERAGE_KEEP) * mixer_new
    return (
        output, input_grad, grad_norm, mixer_new, gate_up_new, down_new, gains_new,
        mixer_first_new, gate_up_first_new, down_first_new, gains_first_new,
        mixer_second_new, gate_up_second_new, down_second_new, gains_second_new, mixer_average_new,
    )


def solution(mesh):
    outer, inner = mesh.shape["dp"], mesh.shape["fsdp"]
    side = math.isqrt(outer)
    if side * side != outer:
        side = 1
    split = jax.sharding.Mesh(
        np.asarray(mesh.devices).reshape(side, outer // side, inner // 2, 2), EVERY
    )
    rows, columns, whole = P(EVERY, None), P(None, EVERY), P()
    return jax.shard_map(
        body,
        mesh=split,
        in_specs=(
            rows, rows, whole, rows, rows, rows, rows, columns,
            rows, rows, rows, columns, rows, rows, rows, columns, rows,
        ),
        out_specs=(
            rows, rows, whole, rows, rows, rows, columns, rows, rows, rows, columns,
            rows, rows, rows, columns, rows,
        ),
        check_vma=False,
    )
```

profile of v0, /device:TPU:0, one launch (start us, length us, event | category | flops | bytes accessed | tf_op | source)
XLA Modules:
  0.0 291.1 jit_solution(16238948101090115286)
XLA Ops:
  8.5 6.2 %all-to-all-start = ((bf16[4,880,128]{2,1,0:T(8,128)(2,1)}), bf16[4,880,128]{2,1,0:T(8,128)(2,1)}, u32[]{:S(2)}, u32[]{:S(2)}) async-start(bf16[4,880,128]{2,1,0:T(8,128)(2,1)} %bitcast.31), calls=%async_computation | async-start | bytes 1802240 | tf_op jit(solution)/shard_map/all_to_all | solution.py:1076
  22.3 5.9 %spread.3 = (bf16[2,1024,3456]{2,1,0:T(8,128)(2,1)}, f32[8,128]{1,0:T(8,128)}) custom-call(s32[1,3]{1,0:T(1,128)} %refs_1_.9, s32[1,3]{1,0:T(1,128)} %collective-permute-done.refs_5_.refs_1_.refs_2_, f32[9,3,512]{2,1,0:T(4,128)} %reshape.69.refs_2_, bf16[512,256]{1,0:T(8,128)(2,1)} %get-tuple-element.162.refs_3_.refs_10_, ...), custom_call_target="tpu_custom_call" | custom-call | flops 1 | bytes 1 | tf_op jit(solution)/shard_map/spread/pallas_call | solution.py:57
  33.1 3.5 %spread.4 = (bf16[2,1024,3456]{2,1,0:T(8,128)(2,1)}, f32[8,128]{1,0:T(8,128)}) custom-call(s32[1,3]{1,0:T(1,128)} %refs_1_.9, s32[1,3]{1,0:T(1,128)} %collective-permute-done.refs_5_.refs_1_.refs_2_, f32[9,3,512]{2,1,0:T(4,128)} %reshape.69.refs_2_, bf16[512,256]{1,0:T(8,128)(2,1)} %get-tuple-element.162.refs_3_.refs_10_, ...), custom_call_target="tpu_custom_call", output_to_operand_aliasing={{0}: (5, {})} | custom-call | flops 1 | bytes 1 | tf_op jit(solution)/shard_map/spread/pallas_call | solution.py:57
  37.9 2.5 stack.22
  40.4 4.8 %all-to-all-start.1 = ((bf16[4,864,128]{2,1,0:T(8,128)(2,1)}), bf16[4,864,128]{2,1,0:T(8,128)(2,1)}, u32[]{:S(2)}, u32[]{:S(2)}) async-start(bf16[4,864,128]{2,1,0:T(8,128)(2,1)} %bitcast.32), calls=%async_computation.1 | async-start | bytes 1769472 | tf_op jit(solution)/shard_map/all_to_all | solution.py:1076
  48.2 8.0 %spread.5 = (bf16[2,1024,3456]{2,1,0:T(8,128)(2,1)}, f32[8,128]{1,0:T(8,128)}) custom-call(s32[1,3]{1,0:T(1,128)} %refs_1_.9, s32[1,3]{1,0:T(1,128)} %collective-permute-done.refs_5_.refs_1_.refs_2_, f32[9,3,512]{2,1,0:T(4,128)} %reshape.69.refs_2_, bf16[512,256]{1,0:T(8,128)(2,1)} %get-tuple-element.162.refs_3_.refs_10_, ...), custom_call_target="tpu_custom_call", output_to_operand_aliasing={{0}: (5, {})} | custom-call | flops 1 | bytes 1 | tf_op jit(solution)/shard_map/spread/pallas_call | solution.py:57
  56.2 4.8 %collective-permute-done.9.refs_0_.refs_7_ = bf16[2640,128]{1,0:T(8,128)(2,1)} collective-permute-done((bf16[2640,128]{1,0:T(8,128)(2,1)}, bf16[2640,128]{1,0:T(8,128)(2,1)}, u32[]{:S(2)}, u32[]{:S(2)}) %collective-permute-start.9) | collective-permute-done | bytes 675872 | tf_op jit(solution)/shard_map/ppermute | solution.py:902
  68.9 4.7 %all-to-all-start.2 = ((bf16[4,192,512]{2,1,0:T(8,128)(2,1)}), bf16[4,192,512]{2,1,0:T(8,128)(2,1)}, u32[]{:S(2)}, u32[]{:S(2)}) async-start(bf16[4,192,512]{2,1,0:T(8,128)(2,1)} %bitcast.33), calls=%async_computation.2 | async-start | bytes 1572864 | tf_op jit(solution)/shard_map/all_to_all | solution.py:1076
  76.2 10.7 %mix.2 = (f32[512,512]{1,0:T(8,128)}, f32[512,512]{1,0:T(8,128)}, bf16[13824,128]{1,0:T(8,128)(2,1)}, f32[16,512]{1,0:T(8,128)}, f32[8,128]{1,0:T(8,128)}) custom-call(s32[4]{0:T(128)} %pad_add_fusion.refs_0_, bf16[2,1024,3456]{2,1,0:T(8,128)(2,1)} %get-tuple-element.175.refs_1_.refs_4_, bf16[1760,128]{1,0:T(8,128)(2,1)} %get-tuple-element.166.refs_2_, ...), custom_call_target="tpu_custom_call" | custom-call | flops 1 | bytes 1 | tf_op jit(solution)/shard_map/mix/pallas_call | solution.py:57
  86.9 2.4 collective-permute-done.13.refs_0_.refs_7_
  94.8 5.4 %collective-permute-done.15.refs_1_.refs_9_ = bf16[1296,128]{1,0:T(8,128)(2,1)} collective-permute-done((bf16[1296,128]{1,0:T(8,128)(2,1)}, bf16[1296,128]{1,0:T(8,128)(2,1)}, u32[]{:S(2)}, u32[]{:S(2)}) %collective-permute-start.15) | collective-permute-done | bytes 331808 | tf_op jit(solution)/shard_map/ppermute | solution.py:902
  103.9 11.5 %mix.3 = (f32[512,512]{1,0:T(8,128)}, bf16[512,512]{1,0:T(8,128)(2,1)}, bf16[13824,128]{1,0:T(8,128)(2,1)}, f32[8,128]{1,0:T(8,128)}) custom-call(s32[4]{0:T(128)} %pad_add_fusion.refs_0_, bf16[2,1024,3456]{2,1,0:T(8,128)(2,1)} %get-tuple-element.175.refs_1_.refs_4_, bf16[1760,128]{1,0:T(8,128)(2,1)} %get-tuple-element.166.refs_2_, ...), custom_call_target="tpu_custom_call" | custom-call | flops 1 | bytes 1 | tf_op jit(solution)/shard_map/mix/pallas_call | solution.py:57
  123.0 2.6 hidden.1
  129.9 18.5 %ffn.1 = (f32[512,512]{1,0:T(8,128)}, bf16[512,512]{1,0:T(8,128)(2,1)}, f32[512,512]{1,0:T(8,128)}, bf16[512,512]{1,0:T(8,128)(2,1)}, bf16[16,192,512]{2,1,0:T(8,128)(2,1)}, /*index=5*/f32[8,128]{1,0:T(8,128)}) custom-call(s32[4]{0:T(128)} %pad_add_fusion.refs_0_, s32[1,3]{1,0:T(1,128)} %refs_1_.9, s32[1,3]{1,0:T(1,128)} %collective-permute-done.refs_5_.refs_1_.refs_2_, ...), custom_call_target="tpu_custom_call" | custom-call | flops 1 | bytes 1 | tf_op jit(solution)/shard_map/ffn/pallas_call | solution.py:57
  148.4 5.0 %all-to-all-start.3 = ((bf16[4,768,512]{2,1,0:T(8,128)(2,1)}), bf16[4,768,512]{2,1,0:T(8,128)(2,1)}, u32[]{:S(2)}, u32[]{:S(2)}) async-start(bf16[4,768,512]{2,1,0:T(8,128)(2,1)} %bitcast.29), calls=%async_computation.3 | async-start | bytes 6291456 | tf_op jit(solution)/shard_map/all_to_all | solution.py:1076
  155.5 3.1 %turn.1 = (f32[512,512]{1,0:T(8,128)}, bf16[512,512]{1,0:T(8,128)(2,1)}, f32[1,512]{1,0:T(1,128)}, f32[8,128]{1,0:T(8,128)}) custom-call(s32[1,3]{1,0:T(1,128)} %refs_1_.9, f32[512,512]{1,0:T(8,128)} %get-tuple-element.202.refs_1_.refs_0_, bf16[512,512]{1,0:T(8,128)(2,1)} %refs_2_.5, f32[512,512]{1,0:T(8,128)} %get-tuple-element.209.refs_3_, ...), custom_call_target="tpu_custom_call" | custom-call | flops 1 | bytes 1 | tf_op jit(solution)/shard_map/turn/pallas_call | solution.py:57
  160.9 9.1 %mixer_grad.2 = (bf16[3456,128]{1,0:T(8,128)(2,1)}, bf16[3456,128]{1,0:T(8,128)(2,1)}, bf16[3456,128]{1,0:T(8,128)(2,1)}, bf16[1728,128]{1,0:T(8,128)(2,1)}, bf1...) custom-call(s32[4]{0:T(128)} %pad_add_fusion.refs_0_, f32[16,512]{1,0:T(8,128)} %get-tuple-element.193.refs_13_.refs_3_.refs_5_.refs_1_, ...), custom_call_target="tpu_custom_call" | custom-call | flops 1 | bytes 1 | tf_op jit(solution)/shard_map/mixer_grad/pallas_call | solution.py:57
  172.6 9.1 %mixer_grad.3 = (bf16[3456,128]{1,0:T(8,128)(2,1)}, bf16[3456,128]{1,0:T(8,128)(2,1)}, bf16[3456,128]{1,0:T(8,128)(2,1)}, bf16[1728,128]{1,0:T(8,128)(2,1)}, bf1...) custom-call(s32[4]{0:T(128)} %pad_add_fusion.refs_0_, f32[16,512]{1,0:T(8,128)} %get-tuple-element.193.refs_13_.refs_3_.refs_5_.refs_1_, ...), custom_call_target="tpu_custom_call" | custom-call | flops 1 | bytes 1 | tf_op jit(solution)/shard_map/mixer_grad/pallas_call | solution.py:57
  189.6 9.5 %spread_back.2 = (f32[512,256]{1,0:T(8,128)}, f32[512,256]{1,0:T(8,128)}, f32[8,128]{1,0:T(8,128)}) custom-call(s32[4]{0:T(128)} %pad_add_fusion.refs_0_, s32[1,3]{1,0:T(1,128)} %refs_1_.9, s32[1,3]{1,0:T(1,128)} %collective-permute-done.refs_5_.refs_1_.refs_2_, f32[9,3,512]{2,1,0:T(4,128)} %reshape.75.refs_3_, ...), custom_call_target="tpu_custom_call" | custom-call | flops 1 | bytes 1 | tf_op jit(solution)/shard_map/spread_back/pallas_call | solution.py:57
  203.6 12.1 %spread_back.3 = (f32[512,256]{1,0:T(8,128)}, f32[512,256]{1,0:T(8,128)}, f32[1,256]{1,0:T(1,128)}, f32[32,128]{1,0:T(8,128)}, f32[8,128]{1,0:T(8,128)}) custom-call(s32[4]{0:T(128)} %pad_add_fusion.refs_0_, s32[1,3]{1,0:T(1,128)} %refs_1_.9, s32[1,3]{1,0:T(1,128)} %collective-permute-done.refs_5_.refs_1_.refs_2_, f32[9,3,512]{2,1,0:T(4,128)} %reshape.75.refs_3_, ...), custom_call_target="tpu_custom_call" | custom-call | flops 1 | bytes 1 | tf_op jit(solution)/shard_map/spread_back/pallas_call | solution.py:57
  215.7 2.8 line.3
  223.4 4.3 %all-to-all-start.4 = ((f32[32,1,128]{2,1,0:T(1,128)}), f32[32,1,128]{2,1,0:T(1,128)}, u32[]{:S(2)}, u32[]{:S(2)}) async-start(f32[32,1,128]{2,1,0:T(1,128)} %bitcast.35), calls=%async_computation.4 | async-start | bytes 32768 | tf_op jit(solution)/shard_map/all_to_all | solution.py:1108
  227.7 3.9 %collective-permute-done.35.refs_1_ = bf16[3456,128]{1,0:T(8,128)(2,1)} collective-permute-done((bf16[3456,128]{1,0:T(8,128)(2,1)}, bf16[3456,128]{1,0:T(8,128)(2,1)}, u32[]{:S(2)}, u32[]{:S(2)}) %collective-permute-start.35) | collective-permute-done | bytes 884768 | tf_op jit(solution)/shard_map/ppermute | solution.py:902
  232.1 2.6 line.4
  234.7 7.7 %all-to-all-done.4 = f32[32,1,128]{2,1,0:T(1,128)} async-done(((f32[32,1,128]{2,1,0:T(1,128)}), f32[32,1,128]{2,1,0:T(1,128)}, u32[]{:S(2)}, u32[]{:S(2)}) %all-to-all-start.4) | async-done | bytes 16416 | tf_op jit(solution)/shard_map/all_to_all | solution.py:1108
  244.6 4.2 %all-to-all-start.5 = ((bf16[4,864,128]{2,1,0:T(8,128)(2,1)}), bf16[4,864,128]{2,1,0:T(8,128)(2,1)}, u32[]{:S(2)}, u32[]{:S(2)}) async-start(bf16[4,864,128]{2,1,0:T(8,128)(2,1)} %bitcast.30), calls=%async_computation.5 | async-start | bytes 1769472 | tf_op jit(solution)/shard_map/all_to_all | solution.py:1076
  249.4 2.9 line.5
  258.2 2.8 last.1
  266.6 4.9 %all-to-all-done.5 = bf16[4,864,128]{2,1,0:T(8,128)(2,1)} async-done(((bf16[4,864,128]{2,1,0:T(8,128)(2,1)}), bf16[4,864,128]{2,1,0:T(8,128)(2,1)}, u32[]{:S(2)}, u32[]{:S(2)}) %all-to-all-start.5) | async-done | bytes 884768 | tf_op jit(solution)/shard_map/all_to_all | solution.py:1076
  274.3 3.2 %all-to-all-start.6 = ((f32[32,1,128]{2,1,0:T(1,128)}), f32[32,1,128]{2,1,0:T(1,128)}, u32[]{:S(2)}, u32[]{:S(2)}) async-start(f32[32,1,128]{2,1,0:T(1,128)} %bitcast.36), calls=%async_computation.6 | async-start | bytes 32768 | tf_op jit(solution)/shard_map/all_to_all | solution.py:1108
  277.5 7.0 %all-to-all-done.6 = f32[32,1,128]{2,1,0:T(1,128)} async-done(((f32[32,1,128]{2,1,0:T(1,128)}), f32[32,1,128]{2,1,0:T(1,128)}, u32[]{:S(2)}, u32[]{:S(2)}) %all-to-all-start.6) | async-done | bytes 16416 | tf_op jit(solution)/shard_map/all_to_all | solution.py:1108
  284.6 6.3 %adam.1 = (f32[432,512]{1,0:T(8,128)}, f32[432,512]{1,0:T(8,128)}, f32[432,512]{1,0:T(8,128)}, f32[432,512]{1,0:T(8,128)}, f32[128,512]{1,0:T(8,128)}, /*index=5...) custom-call(s32[4]{0:T(128)} %pad_add_fusion.refs_0_, ...), custom_call_target="tpu_custom_call" | custom-call | flops 1 | bytes 1 | tf_op jit(solution)/shard_map/adam/pallas_call | solution.py:57
  (129 shorter events, 97.9 us)
Async XLA Ops:
  8.5 29.4 %all-to-all-start = ((bf16[4,880,128]{2,1,0:T(8,128)(2,1)}), bf16[4,880,128]{2,1,0:T(8,128)(2,1)}, u32[]{:S(2)}, u32[]{:S(2)}) async-start(bf16[4,880,128]{2,1,0:T(8,128)(2,1)} %bitcast.31), calls=%async_computation | async-start | bytes 1802240 | tf_op jit(solution)/shard_map/all_to_all | solution.py:1076
  15.4 12.7 %collective-permute-start.5 = (bf16[1760,128]{1,0:T(8,128)(2,1)}, bf16[1760,128]{1,0:T(8,128)(2,1)}, u32[]{:S(2)}, u32[]{:S(2)}) collective-permute-start(bf16[1760,128]{1,0:T(8,128)(2,1)} %get-tuple-element.166.refs_2_), channel_id=1, source_target_pairs={{0,8},{8,0},{1,9},{9,1},{2,10},{10,2},{3,11},{11,3},{4,12},{12,4},... | collective-permute-start | bytes 1351688 | tf_op jit(solution)/shard_map/ppermute | solution.py:902
  16.9 12.2 %collective-permute-start.6 = (bf16[1760,128]{1,0:T(8,128)(2,1)}, bf16[1760,128]{1,0:T(8,128)(2,1)}, u32[]{:S(2)}, u32[]{:S(2)}) collective-permute-start(bf16[1760,128]{1,0:T(8,128)(2,1)} %get-tuple-element.166.refs_2_), channel_id=1, source_target_pairs={{0,16},{16,0},{1,17},{17,1},{2,18},{18,2},{3,19},{19,3},{4,20},{20... | collective-permute-start | bytes 1351688 | tf_op jit(solution)/shard_map/ppermute | solution.py:902
  40.4 26.1 %all-to-all-start.1 = ((bf16[4,864,128]{2,1,0:T(8,128)(2,1)}), bf16[4,864,128]{2,1,0:T(8,128)(2,1)}, u32[]{:S(2)}, u32[]{:S(2)}) async-start(bf16[4,864,128]{2,1,0:T(8,128)(2,1)} %bitcast.32), calls=%async_computation.1 | async-start | bytes 1769472 | tf_op jit(solution)/shard_map/all_to_all | solution.py:1076
  45.2 15.8 %collective-permute-start.9 = (bf16[2640,128]{1,0:T(8,128)(2,1)}, bf16[2640,128]{1,0:T(8,128)(2,1)}, u32[]{:S(2)}, u32[]{:S(2)}) collective-permute-start(bf16[2640,128]{1,0:T(8,128)(2,1)} %get-tuple-element.179.refs_6_), channel_id=1, source_target_pairs={{0,8},{8,0},{1,9},{9,1},{2,10},{10,2},{3,11},{11,3},{4,12},{12,4},... | collective-permute-start | bytes 2027528 | tf_op jit(solution)/shard_map/ppermute | solution.py:902
  46.7 15.5 %collective-permute-start.10 = (bf16[2640,128]{1,0:T(8,128)(2,1)}, bf16[2640,128]{1,0:T(8,128)(2,1)}, u32[]{:S(2)}, u32[]{:S(2)}) collective-permute-start(bf16[2640,128]{1,0:T(8,128)(2,1)} %get-tuple-element.179.refs_6_), channel_id=1, source_target_pairs={{0,16},{16,0},{1,17},{17,1},{2,18},{18,2},{3,19},{19,3},{4,20},{20... | collective-permute-start | bytes 2027528 | tf_op jit(solution)/shard_map/ppermute | solution.py:902
  64.4 9.2 %collective-permute-start.11 = (bf16[1344,128]{1,0:T(8,128)(2,1)}, bf16[1344,128]{1,0:T(8,128)(2,1)}, u32[]{:S(2)}, u32[]{:S(2)}) collective-permute-start(bf16[1344,128]{1,0:T(8,128)(2,1)} %get-tuple-element.183), channel_id=1, source_target_pairs={{0,8},{8,0},{1,9},{9,1},{2,10},{10,2},{3,11},{11,3},{4,12},{12,4},... | collective-permute-start | bytes 1032200 | tf_op jit(solution)/shard_map/ppermute | solution.py:902
  68.9 31.8 %all-to-all-start.2 = ((bf16[4,192,512]{2,1,0:T(8,128)(2,1)}), bf16[4,192,512]{2,1,0:T(8,128)(2,1)}, u32[]{:S(2)}, u32[]{:S(2)}) async-start(bf16[4,192,512]{2,1,0:T(8,128)(2,1)} %bitcast.33), calls=%async_computation.2 | async-start | bytes 1572864 | tf_op jit(solution)/shard_map/all_to_all | solution.py:1076
  73.6 15.8 %collective-permute-start.13 = (bf16[2592,128]{1,0:T(8,128)(2,1)}, bf16[2592,128]{1,0:T(8,128)(2,1)}, u32[]{:S(2)}, u32[]{:S(2)}) collective-permute-start(bf16[2592,128]{1,0:T(8,128)(2,1)} %get-tuple-element.186.refs_6_), channel_id=1, source_target_pairs={{0,8},{8,0},{1,9},{9,1},{2,10},{10,2},{3,11},{11,3},{4,12},{12,4},... | collective-permute-start | bytes 1990664 | tf_op jit(solution)/shard_map/ppermute | solution.py:902
  75.2 15.4 %collective-permute-start.14 = (bf16[2592,128]{1,0:T(8,128)(2,1)}, bf16[2592,128]{1,0:T(8,128)(2,1)}, u32[]{:S(2)}, u32[]{:S(2)}) collective-permute-start(bf16[2592,128]{1,0:T(8,128)(2,1)} %get-tuple-element.186.refs_6_), channel_id=1, source_target_pairs={{0,16},{16,0},{1,17},{17,1},{2,18},{18,2},{3,19},{19,3},{4,20},{20... | collective-permute-start | bytes 1990664 | tf_op jit(solution)/shard_map/ppermute | solution.py:902
  100.7 16.3 %collective-permute-start.18 = (bf16[768,512]{1,0:T(8,128)(2,1)}, bf16[768,512]{1,0:T(8,128)(2,1)}, u32[]{:S(2)}, u32[]{:S(2)}) collective-permute-start(bf16[768,512]{1,0:T(8,128)(2,1)} %get-tuple-element.199), channel_id=1, source_target_pairs={{0,8},{8,0},{1,9},{9,1},{2,10},{10,2},{3,11},{11,3},{4,12},{12,4},... | collective-permute-start | bytes 2359304 | tf_op jit(solution)/shard_map/ppermute | solution.py:902
  102.3 16.0 %collective-permute-start.19 = (bf16[768,512]{1,0:T(8,128)(2,1)}, bf16[768,512]{1,0:T(8,128)(2,1)}, u32[]{:S(2)}, u32[]{:S(2)}) collective-permute-start(bf16[768,512]{1,0:T(8,128)(2,1)} %get-tuple-element.199), channel_id=1, source_target_pairs={{0,16},{16,0},{1,17},{17,1},{2,18},{18,2},{3,19},{19,3},{4,20},{20... | collective-permute-start | bytes 2359304 | tf_op jit(solution)/shard_map/ppermute | solution.py:902
  148.4 75.0 %all-to-all-start.3 = ((bf16[4,768,512]{2,1,0:T(8,128)(2,1)}), bf16[4,768,512]{2,1,0:T(8,128)(2,1)}, u32[]{:S(2)}, u32[]{:S(2)}) async-start(bf16[4,768,512]{2,1,0:T(8,128)(2,1)} %bitcast.29), calls=%async_computation.3 | async-start | bytes 6291456 | tf_op jit(solution)/shard_map/all_to_all | solution.py:1076
  170.0 13.3 %collective-permute-start.26 = (bf16[1728,128]{1,0:T(8,128)(2,1)}, bf16[1728,128]{1,0:T(8,128)(2,1)}, u32[]{:S(2)}, u32[]{:S(2)}) collective-permute-start(bf16[1728,128]{1,0:T(8,128)(2,1)} %get-tuple-element.219), channel_id=1, source_target_pairs={{0,8},{8,0},{1,9},{9,1},{2,10},{10,2},{3,11},{11,3},{4,12},{12,4},... | collective-permute-start | bytes 1327112 | tf_op jit(solution)/shard_map/ppermute | solution.py:902
  171.6 12.2 %collective-permute-start.27 = (bf16[1728,128]{1,0:T(8,128)(2,1)}, bf16[1728,128]{1,0:T(8,128)(2,1)}, u32[]{:S(2)}, u32[]{:S(2)}) collective-permute-start(bf16[1728,128]{1,0:T(8,128)(2,1)} %get-tuple-element.220), channel_id=1, source_target_pairs={{0,16},{16,0},{1,17},{17,1},{2,18},{18,2},{3,19},{19,3},{4,20},{20... | collective-permute-start | bytes 1327112 | tf_op jit(solution)/shard_map/ppermute | solution.py:902
  181.7 17.5 %collective-permute-start.30 = (bf16[1728,128]{1,0:T(8,128)(2,1)}, bf16[1728,128]{1,0:T(8,128)(2,1)}, u32[]{:S(2)}, u32[]{:S(2)}) collective-permute-start(bf16[1728,128]{1,0:T(8,128)(2,1)} %get-tuple-element.233), channel_id=1, source_target_pairs={{0,8},{8,0},{1,9},{9,1},{2,10},{10,2},{3,11},{11,3},{4,12},{12,4},... | collective-permute-start | bytes 1327112 | tf_op jit(solution)/shard_map/ppermute | solution.py:902
  182.4 16.7 %collective-permute-start.31 = (bf16[1728,128]{1,0:T(8,128)(2,1)}, bf16[1728,128]{1,0:T(8,128)(2,1)}, u32[]{:S(2)}, u32[]{:S(2)}) collective-permute-start(bf16[1728,128]{1,0:T(8,128)(2,1)} %get-tuple-element.234), channel_id=1, source_target_pairs={{0,16},{16,0},{1,17},{17,1},{2,18},{18,2},{3,19},{19,3},{4,20},{20... | collective-permute-start | bytes 1327112 | tf_op jit(solution)/shard_map/ppermute | solution.py:902
  186.2 29.5 %collective-permute-start.28 = (bf16[3456,128]{1,0:T(8,128)(2,1)}, bf16[3456,128]{1,0:T(8,128)(2,1)}, u32[]{:S(2)}, u32[]{:S(2)}) collective-permute-start(bf16[3456,128]{1,0:T(8,128)(2,1)} %get-tuple-element.223), channel_id=1, source_target_pairs={{0,8},{8,0},{1,9},{9,1},{2,10},{10,2},{3,11},{11,3},{4,12},{12,4},... | collective-permute-start | bytes 2654216 | tf_op jit(solution)/shard_map/ppermute | solution.py:902
  187.1 28.5 %collective-permute-start.29 = (bf16[3456,128]{1,0:T(8,128)(2,1)}, bf16[3456,128]{1,0:T(8,128)(2,1)}, u32[]{:S(2)}, u32[]{:S(2)}) collective-permute-start(bf16[3456,128]{1,0:T(8,128)(2,1)} %get-tuple-element.224), channel_id=1, source_target_pairs={{0,16},{16,0},{1,17},{17,1},{2,18},{18,2},{3,19},{19,3},{4,20},{20... | collective-permute-start | bytes 2654216 | tf_op jit(solution)/shard_map/ppermute | solution.py:902
  201.5 30.1 %collective-permute-start.35 = (bf16[3456,128]{1,0:T(8,128)(2,1)}, bf16[3456,128]{1,0:T(8,128)(2,1)}, u32[]{:S(2)}, u32[]{:S(2)}) collective-permute-start(bf16[3456,128]{1,0:T(8,128)(2,1)} %get-tuple-element.247), channel_id=1, source_target_pairs={{0,8},{8,0},{1,9},{9,1},{2,10},{10,2},{3,11},{11,3},{4,12},{12,4},... | collective-permute-start | bytes 2654216 | tf_op jit(solution)/shard_map/ppermute | solution.py:902
  202.6 29.5 %collective-permute-start.36 = (bf16[3456,128]{1,0:T(8,128)(2,1)}, bf16[3456,128]{1,0:T(8,128)(2,1)}, u32[]{:S(2)}, u32[]{:S(2)}) collective-permute-start(bf16[3456,128]{1,0:T(8,128)(2,1)} %get-tuple-element.248), channel_id=1, source_target_pairs={{0,16},{16,0},{1,17},{17,1},{2,18},{18,2},{3,19},{19,3},{4,20},{20... | collective-permute-start | bytes 2654216 | tf_op jit(solution)/shard_map/ppermute | solution.py:902
  218.5 23.9 %collective-permute-start.32 = (bf16[864,128]{1,0:T(8,128)(2,1)}, bf16[864,128]{1,0:T(8,128)(2,1)}, u32[]{:S(2)}, u32[]{:S(2)}) collective-permute-start(bf16[864,128]{1,0:T(8,128)(2,1)} %get-tuple-element.239), channel_id=1, source_target_pairs={{0,2},{2,0},{4,6},{6,4},{1,3},{3,1},{5,7},{7,5},{8,10},{10,8},{12,... | collective-permute-start | bytes 663560 | tf_op jit(solution)/shard_map/ppermute | solution.py:902
  220.2 22.2 %collective-permute-start.33 = (bf16[864,128]{1,0:T(8,128)(2,1)}, bf16[864,128]{1,0:T(8,128)(2,1)}, u32[]{:S(2)}, u32[]{:S(2)}) collective-permute-start(bf16[864,128]{1,0:T(8,128)(2,1)} %get-tuple-element.240), channel_id=1, source_target_pairs={{0,4},{2,6},{4,0},{6,2},{1,5},{3,7},{5,1},{7,3},{8,12},{10,14},{12... | collective-permute-start | bytes 663560 | tf_op jit(solution)/shard_map/ppermute | solution.py:902
  222.6 19.8 %collective-permute-start.34 = (bf16[864,128]{1,0:T(8,128)(2,1)}, bf16[864,128]{1,0:T(8,128)(2,1)}, u32[]{:S(2)}, u32[]{:S(2)}) collective-permute-start(bf16[864,128]{1,0:T(8,128)(2,1)} %get-tuple-element.241), channel_id=1, source_target_pairs={{0,6},{2,4},{4,2},{6,0},{1,7},{3,5},{5,3},{7,1},{8,14},{10,12},{12... | collective-permute-start | bytes 663560 | tf_op jit(solution)/shard_map/ppermute | solution.py:902
  223.4 19.0 %all-to-all-start.4 = ((f32[32,1,128]{2,1,0:T(1,128)}), f32[32,1,128]{2,1,0:T(1,128)}, u32[]{:S(2)}, u32[]{:S(2)}) async-start(f32[32,1,128]{2,1,0:T(1,128)} %bitcast.35), calls=%async_computation.4 | async-start | bytes 32768 | tf_op jit(solution)/shard_map/all_to_all | solution.py:1108
  244.6 27.0 %all-to-all-start.5 = ((bf16[4,864,128]{2,1,0:T(8,128)(2,1)}), bf16[4,864,128]{2,1,0:T(8,128)(2,1)}, u32[]{:S(2)}, u32[]{:S(2)}) async-start(bf16[4,864,128]{2,1,0:T(8,128)(2,1)} %bitcast.30), calls=%async_computation.5 | async-start | bytes 1769472 | tf_op jit(solution)/shard_map/all_to_all | solution.py:1076
  248.9 9.3 %collective-permute-start.38 = (f32[512,256]{1,0:T(8,128)}, f32[512,256]{1,0:T(8,128)}, u32[]{:S(2)}, u32[]{:S(2)}) collective-permute-start(f32[512,256]{1,0:T(8,128)} %get-tuple-element.261), channel_id=1, source_target_pairs={{0,1},{1,0},{2,3},{3,2},{4,5},{5,4},{6,7},{7,6},{8,9},{9,8},{10,11... | collective-permute-start | bytes 1572872 | tf_op jit(solution)/shard_map/ppermute | solution.py:902
  253.0 10.2 %collective-permute-start.40 = (bf16[192,512]{1,0:T(8,128)(2,1)}, bf16[192,512]{1,0:T(8,128)(2,1)}, u32[]{:S(2)}, u32[]{:S(2)}) collective-permute-start(bf16[192,512]{1,0:T(8,128)(2,1)} %get-tuple-element.267), channel_id=1, source_target_pairs={{0,16},{16,0},{1,17},{17,1},{2,18},{18,2},{3,19},{19,3},{4,20},{20... | collective-permute-start | bytes 589832 | tf_op jit(solution)/shard_map/ppermute | solution.py:902
  254.5 10.1 %collective-permute-start.41 = (bf16[192,512]{1,0:T(8,128)(2,1)}, bf16[192,512]{1,0:T(8,128)(2,1)}, u32[]{:S(2)}, u32[]{:S(2)}) collective-permute-start(bf16[192,512]{1,0:T(8,128)(2,1)} %get-tuple-element.268), channel_id=1, source_target_pairs={{0,24},{8,16},{16,8},{24,0},{1,25},{9,17},{17,9},{25,1},{2,26},{10... | collective-permute-start | bytes 589832 | tf_op jit(solution)/shard_map/ppermute | solution.py:1093
  255.8 21.7 %collective-permute-start.42 = (f32[432,128]{1,0:T(8,128)}, f32[432,128]{1,0:T(8,128)}, u32[]{:S(2)}, u32[]{:S(2)}) collective-permute-start(f32[432,128]{1,0:T(8,128)} %get-tuple-element.276), channel_id=1, source_target_pairs={{0,1},{1,0},{2,3},{3,2},{4,5},{5,4},{6,7},{7,6},{8,9},{9,8},{10,11... | collective-permute-start | bytes 663560 | tf_op jit(solution)/shard_map/ppermute | solution.py:902
  273.8 10.8 %collective-permute-start.43 = (f32[432,128]{1,0:T(8,128)}, f32[432,128]{1,0:T(8,128)}, u32[]{:S(2)}, u32[]{:S(2)}) collective-permute-start(f32[432,128]{1,0:T(8,128)} %get-tuple-element.277), channel_id=1, source_target_pairs={{0,1},{1,0},{2,3},{3,2},{4,5},{5,4},{6,7},{7,6},{8,9},{9,8},{10,11... | collective-permute-start | bytes 663560 | tf_op jit(solution)/shard_map/ppermute | solution.py:902
  274.3 10.2 %all-to-all-start.6 = ((f32[32,1,128]{2,1,0:T(1,128)}), f32[32,1,128]{2,1,0:T(1,128)}, u32[]{:S(2)}, u32[]{:S(2)}) async-start(f32[32,1,128]{2,1,0:T(1,128)} %bitcast.36), calls=%async_computation.6 | async-start | bytes 32768 | tf_op jit(solution)/shard_map/all_to_all | solution.py:1108
  (23 other events, 113.8 us)
where the time goes:
time: 293 us; the launch traced here: 291 us
  Pallas kernels  155 us (53%)
  starting transfers between devices  72.4 us (25%)
  waiting for transfers between devices  58.4 us (20%)
    pallas_call x39, Pallas kernels, call(): pl.pallas_call(whole, name=name, in_specs=list(in_specs) + [anywhere() fo...  155 us
    ppermute x44, starting transfers between devices, flip(): return lax.ppermute(v, axis, [(i, i ^ bits) for i in range(size)])  38.6 us
    ppermute x44, waiting for transfers between devices, flip(): return lax.ppermute(v, axis, [(i, i ^ bits) for i in range(size)])  36.7 us
    all_to_all x5, starting transfers between devices, along_z(): return lax.all_to_all(v, 'z', 0, 0, tiled=True)  25 us
    all_to_all x2, waiting for transfers between devices, everyone(): return lax.all_to_all(rows, EVERY, 0, 0, tiled=True)  14.7 us
    all_to_all x2, starting transfers between devices, everyone(): return lax.all_to_all(rows, EVERY, 0, 0, tiled=True)  7.5 us
  transfers between devices with their start and end apart: 52, of which 27 were waited for; matrix products, arithmetic and copies ran while one was open for 1% of the time, Pallas kernels for 42%

commit v1 on v0

--- a/solution.py
+++ b/solution.py
@@ -120,8 +120,10 @@
             mask[g] = causal_mask(ends, g, n, False)
         table[...] = jnp.zeros_like(table)
 
-    for j in range(per):
-        strip = diagonals(taps_ref[0, j : j + 1, :], q)
+    @pl.loop(0, per)
+    def _(j):
+        at = pl.multiple_of(j * w, w)
+        strip = diagonals(taps_ref[0, pl.ds(j, 1), :], q)
         for g, tokens in enumerate((own_ref, other_ref)):
             for i in range(4):
                 rows, cols = slice(i * q, (i + 1) * q), slice(0, (i + 1) * q)
@@ -130,8 +132,8 @@
             lower = dot(table[g, h:, :], tokens[...]).astype(bf)
             for side in range(2):
                 cols = slice(side * w, (side + 1) * w)
-                u_ref[side, g * n : g * n + h, j * w : (j + 1) * w] = upper[:, cols]
-                u_ref[side, g * n + h : (g + 1) * n, j * w : (j + 1) * w] = lower[:, cols]
+                u_ref[side, g * n : g * n + h, pl.ds(at, w)] = upper[:, cols]
+                u_ref[side, g * n + h : (g + 1) * n, pl.ds(at, w)] = lower[:, cols]
 
 
 def find_ends(ends, lengths_ref, came_ref):
@@ -520,15 +522,22 @@
 def ffn_kernel(count, outs, steps, slots, out_slots, size, crossed, spot_ref, lengths_ref, came_ref, *refs):
     turned = spot_ref[3] if crossed else 0
     tokens, pieces, refs = refs[:6], refs[6 : 6 + count], refs[6 + count :]
-    results, grads, (held, dealt, normed, back, sums, sem) = refs[:4], refs[4 : 4 + outs], refs[4 + outs :]
-    n = tokens[0].shape[0]
+    results, grads, (held, dealt, normed, back, sums, sem, token_sem) = refs[:4], refs[4 : 4 + outs], refs[4 + outs :]
+    n = tokens[-1].shape[0]
     chips, units, width = held.shape[0], held.shape[1] * 2 // 3, held.shape[2]
     own, half = chips // 2 // steps, units // 2
     step = pl.program_id(0)
 
     @pl.when(step == 0)
     def _():
+        half_width = tokens[0].shape[1]
         copies, at = [], 0
+        for g in range(2):
+            rows = pl.ds(g * n, n)
+            for i in range(2):
+                cols = pl.ds(i * half_width, half_width)
+                copies.append(pltpu.make_async_copy(tokens[2 * g + i], normed.at[rows, cols], token_sem.at[2 * g + i]))
+            copies.append(pltpu.make_async_copy(tokens[4 + g], back.at[rows], token_sem.at[4 + g]))
         for ref in pieces:
             for b in range(ref.shape[0]):
                 chip = chip_of(spot_ref, slots[at], size)
@@ -543,13 +552,11 @@
                 at += 1
         for c in copies:
             c.start()
-        half_width = tokens[0].shape[1]
-        for i in range(2):
-            cols = slice(i * half_width, (i + 1) * half_width)
-            normed[:n, cols], normed[n:, cols] = tokens[i][...], tokens[2 + i][...]
-        back[:n] = live_rows(tokens[4][...].astype(f32), lengths_ref).astype(bf)
-        back[n:] = live_rows(tokens[5][...].astype(f32), came_ref).astype(bf)
-        for c in copies:
+        for c in copies[:6]:
+            c.wait()
+        for g, ref in enumerate((lengths_ref, came_ref)):
+            back[g * n : (g + 1) * n] = live_rows(back[g * n : (g + 1) * n].astype(f32), ref).astype(bf)
+        for c in copies[6:]:
             c.wait()
 
     w_gate = flat(held[pl.ds(step * own, own), 0:units])
@@ -562,25 +569,6 @@
     act = (swish * up).astype(bf)
     grad_gate = (grad_act * up * (sigma * (1.0 + gate * (1.0 - sigma)))).astype(bf)
     grad_up = (grad_act * swish).astype(bf)
-    branch = dot(act, w_down)
-    two = dot(jnp.concatenate([grad_gate, grad_up], axis=1), jnp.concatenate([w_gate, w_up], axis=0))
-    for i, value in enumerate((branch, two)):
-        if steps > 1:
-
-            @pl.when(step == 0)
-            def _():
-                sums[i] = value
-
-            @pl.when((step > 0) & (step < steps - 1))
-            def _():
-                sums[i] += value
-
-        @pl.when(step == steps - 1)
-        def _():
-            total = value + sums[i] if steps > 1 else value
-            results[2 * i][...] = total[:n]
-            results[2 * i + 1][...] = total[n:].astype(bf)
-
     put = lambda v: v.astype(bf).reshape(own, units, width)
     dealt[pl.ds(step * own, own), 0:units] = put(dot(grad_gate, normed[...], TN))
     dealt[pl.ds(chips // 2 + step * own, own), 0:units] = put(dot(grad_up, normed[...], TN))
@@ -588,19 +576,46 @@
     for b in range(2 * own):
         dealt[(step * 2 * own + b) ^ turned, units : units + half] = grad_down[b * half : (b + 1) * half]
 
-    @pl.when(step == steps - 1)
-    def _():
+    def deal():
         copies, at = [], 0
         for ref in grads:
             for b in range(ref.shape[0]):
-                copies.append(
-                    pltpu.make_async_copy(dealt.at[chip_of(spot_ref, out_slots[at], size)], ref.at[b], sem.at[0, at])
-                )
+                chip = chip_of(spot_ref, out_slots[at], size)
+                copies.append(pltpu.make_async_copy(dealt.at[chip], ref.at[b], sem.at[0, at]))
                 at += 1
-        run_copies(copies)
-
-
-def ffn_call(chain, spot, lengths, tokens, pieces, blocks, slots, out_slots, size, crossed, chunk=512):
+        return copies
+
+    @pl.when(step == steps - 1)
+    def _():
+        for c in deal():
+            c.start()
+
+    branch = dot(act, w_down)
+    two = dot(jnp.concatenate([grad_gate, grad_up], axis=1), jnp.concatenate([w_gate, w_up], axis=0))
+    for i, value in enumerate((branch, two)):
+        if steps > 1:
+
+            @pl.when(step == 0)
+            def _():
+                sums[i] = value
+
+            @pl.when((step > 0) & (step < steps - 1))
+            def _():
+                sums[i] += value
+
+        @pl.when(step == steps - 1)
+        def _():
+            total = value + sums[i] if steps > 1 else value
+            results[2 * i][...] = total[:n]
+            results[2 * i + 1][...] = total[n:].astype(bf)
+
+    @pl.when(step == steps - 1)
+    def _():
+        for c in deal():
+            c.wait()
+
+
+def ffn_call(chain, spot, lengths, tokens, pieces, blocks, slots, out_slots, size, crossed, chunk=1024):
     n, d = tokens[-1].shape
     chips, rows = len(slots), pieces[0].shape[1]
     units = rows * 2 // 3
@@ -608,14 +623,14 @@
     return chain.call(
         functools.partial(ffn_kernel, len(pieces), len(blocks), steps, slots, out_slots, size, crossed), "ffn",
         (spot, *lengths, *tokens, *pieces),
-        [smem()] * 3 + [fixed(*v.shape) for v in tokens] + [anywhere() for _ in pieces],
+        [smem()] * 3 + [anywhere() for _ in (*tokens, *pieces)],
         [fixed(n, d)] * 4 + [anywhere() for _ in blocks],
         [shaped((n, d), f32), shaped((n, d), bf)] * 2 + [shaped((b, rows, d), bf) for b in blocks],
         grid=(steps,),
         scratch_shapes=[
             pltpu.VMEM((chips, rows, d), bf), pltpu.VMEM((chips, rows, d), bf),
             pltpu.VMEM((2 * n, d), bf), pltpu.VMEM((2 * n, d), bf), pltpu.VMEM((2, 2 * n, d), f32),
-            pltpu.SemaphoreType.DMA((2, chips)),
+            pltpu.SemaphoreType.DMA((2, chips)), pltpu.SemaphoreType.DMA((6,)),
         ],
     )
 

time: 293 us -> 290 us (0.990)
  transfers between devices with their start and end apart: 52 -> 52, of which waited for: 27 -> 26; matrix products, arithmetic and copies ran while one was open for 1% -> 1% of each run, Pallas kernels for 42% -> 44%
where the time goes in v1:
time: 290 us; the launch traced here: 289 us
  Pallas kernels  156 us (54%)
  starting transfers between devices  71.7 us (25%)
  waiting for transfers between devices  55.5 us (19%)
    pallas_call x39, Pallas kernels, call(): pl.pallas_call(whole, name=name, in_specs=list(in_specs) + [anywhere() fo...  156 us
    ppermute x44, starting transfers between devices, flip(): return lax.ppermute(v, axis, [(i, i ^ bits) for i in range(size)])  37.7 us
    ppermute x44, waiting for transfers between devices, flip(): return lax.ppermute(v, axis, [(i, i ^ bits) for i in range(size)])  34.2 us
    all_to_all x5, starting transfers between devices, along_z(): return lax.all_to_all(v, 'z', 0, 0, tiled=True)  25 us
    all_to_all x2, waiting for transfers between devices, everyone(): return lax.all_to_all(rows, EVERY, 0, 0, tiled=True)  14.7 us
    all_to_all x2, starting transfers between devices, everyone(): return lax.all_to_all(rows, EVERY, 0, 0, tiled=True)  7.76 us
  transfers between devices with their start and end apart: 52, of which 26 were waited for; matrix products, arithmetic and copies ran while one was open for 1% of the time, Pallas kernels for 44%

profile of v1, /device:TPU:0, one launch (start us, length us, event | category | flops | bytes accessed | tf_op | source)
XLA Modules:
  0.0 288.9 jit_solution(12399328934313857094)
XLA Ops:
  8.5 6.2 %all-to-all-start = ((bf16[4,880,128]{2,1,0:T(8,128)(2,1)}), bf16[4,880,128]{2,1,0:T(8,128)(2,1)}, u32[]{:S(2)}, u32[]{:S(2)}) async-start(bf16[4,880,128]{2,1,0:T(8,128)(2,1)} %bitcast.31), calls=%async_computation | async-start | bytes 1802240 | tf_op jit(solution)/shard_map/all_to_all | solution.py:1091
  22.3 6.9 %spread.3 = (bf16[2,1024,3456]{2,1,0:T(8,128)(2,1)}, f32[8,128]{1,0:T(8,128)}) custom-call(s32[1,3]{1,0:T(1,128)} %refs_1_.9, s32[1,3]{1,0:T(1,128)} %collective-permute-done.refs_5_.refs_1_.refs_2_, f32[9,3,512]{2,1,0:T(4,128)} %reshape.69.refs_2_, bf16[512,256]{1,0:T(8,128)(2,1)} %get-tuple-element.162.refs_3_.refs_10_, ...), custom_call_target="tpu_custom_call" | custom-call | flops 1 | bytes 1 | tf_op jit(solution)/shard_map/spread/pallas_call | solution.py:57
  33.1 4.1 %spread.4 = (bf16[2,1024,3456]{2,1,0:T(8,128)(2,1)}, f32[8,128]{1,0:T(8,128)}) custom-call(s32[1,3]{1,0:T(1,128)} %refs_1_.9, s32[1,3]{1,0:T(1,128)} %collective-permute-done.refs_5_.refs_1_.refs_2_, f32[9,3,512]{2,1,0:T(4,128)} %reshape.69.refs_2_, bf16[512,256]{1,0:T(8,128)(2,1)} %get-tuple-element.162.refs_3_.refs_10_, ...), custom_call_target="tpu_custom_call", output_to_operand_aliasing={{0}: (5, {})} | custom-call | flops 1 | bytes 1 | tf_op jit(solution)/shard_map/spread/pallas_call | solution.py:57
  38.5 2.5 stack.22
  41.1 4.8 %all-to-all-start.1 = ((bf16[4,864,128]{2,1,0:T(8,128)(2,1)}), bf16[4,864,128]{2,1,0:T(8,128)(2,1)}, u32[]{:S(2)}, u32[]{:S(2)}) async-start(bf16[4,864,128]{2,1,0:T(8,128)(2,1)} %bitcast.32), calls=%async_computation.1 | async-start | bytes 1769472 | tf_op jit(solution)/shard_map/all_to_all | solution.py:1091
  48.2 9.7 %spread.5 = (bf16[2,1024,3456]{2,1,0:T(8,128)(2,1)}, f32[8,128]{1,0:T(8,128)}) custom-call(s32[1,3]{1,0:T(1,128)} %refs_1_.9, s32[1,3]{1,0:T(1,128)} %collective-permute-done.refs_5_.refs_1_.refs_2_, f32[9,3,512]{2,1,0:T(4,128)} %reshape.69.refs_2_, bf16[512,256]{1,0:T(8,128)(2,1)} %get-tuple-element.162.refs_3_.refs_10_, ...), custom_call_target="tpu_custom_call", output_to_operand_aliasing={{0}: (5, {})} | custom-call | flops 1 | bytes 1 | tf_op jit(solution)/shard_map/spread/pallas_call | solution.py:57
  57.9 3.1 %collective-permute-done.9.refs_0_.refs_7_ = bf16[2640,128]{1,0:T(8,128)(2,1)} collective-permute-done((bf16[2640,128]{1,0:T(8,128)(2,1)}, bf16[2640,128]{1,0:T(8,128)(2,1)}, u32[]{:S(2)}, u32[]{:S(2)}) %collective-permute-start.9) | collective-permute-done | bytes 675872 | tf_op jit(solution)/shard_map/ppermute | solution.py:917
  68.9 4.7 %all-to-all-start.2 = ((bf16[4,192,512]{2,1,0:T(8,128)(2,1)}), bf16[4,192,512]{2,1,0:T(8,128)(2,1)}, u32[]{:S(2)}, u32[]{:S(2)}) async-start(bf16[4,192,512]{2,1,0:T(8,128)(2,1)} %bitcast.33), calls=%async_computation.2 | async-start | bytes 1572864 | tf_op jit(solution)/shard_map/all_to_all | solution.py:1091
  76.0 10.7 %mix.2 = (f32[512,512]{1,0:T(8,128)}, f32[512,512]{1,0:T(8,128)}, bf16[13824,128]{1,0:T(8,128)(2,1)}, f32[16,512]{1,0:T(8,128)}, f32[8,128]{1,0:T(8,128)}) custom-call(s32[4]{0:T(128)} %pad_add_fusion.refs_0_, bf16[2,1024,3456]{2,1,0:T(8,128)(2,1)} %get-tuple-element.175.refs_1_.refs_4_, bf16[1760,128]{1,0:T(8,128)(2,1)} %get-tuple-element.166.refs_2_, ...), custom_call_target="tpu_custom_call" | custom-call | flops 1 | bytes 1 | tf_op jit(solution)/shard_map/mix/pallas_call | solution.py:57
  86.7 2.4 collective-permute-done.13.refs_0_.refs_7_
  94.6 5.4 %collective-permute-done.15.refs_1_.refs_9_ = bf16[1296,128]{1,0:T(8,128)(2,1)} collective-permute-done((bf16[1296,128]{1,0:T(8,128)(2,1)}, bf16[1296,128]{1,0:T(8,128)(2,1)}, u32[]{:S(2)}, u32[]{:S(2)}) %collective-permute-start.15) | collective-permute-done | bytes 331808 | tf_op jit(solution)/shard_map/ppermute | solution.py:917
  103.7 11.5 %mix.3 = (f32[512,512]{1,0:T(8,128)}, bf16[512,512]{1,0:T(8,128)(2,1)}, bf16[13824,128]{1,0:T(8,128)(2,1)}, f32[8,128]{1,0:T(8,128)}) custom-call(s32[4]{0:T(128)} %pad_add_fusion.refs_0_, bf16[2,1024,3456]{2,1,0:T(8,128)(2,1)} %get-tuple-element.175.refs_1_.refs_4_, bf16[1760,128]{1,0:T(8,128)(2,1)} %get-tuple-element.166.refs_2_, ...), custom_call_target="tpu_custom_call" | custom-call | flops 1 | bytes 1 | tf_op jit(solution)/shard_map/mix/pallas_call | solution.py:57
  122.8 2.5 hidden.1
  129.7 16.5 %ffn.1 = (f32[512,512]{1,0:T(8,128)}, bf16[512,512]{1,0:T(8,128)(2,1)}, f32[512,512]{1,0:T(8,128)}, bf16[512,512]{1,0:T(8,128)(2,1)}, bf16[16,192,512]{2,1,0:T(8,128)(2,1)}, /*index=5*/f32[8,128]{1,0:T(8,128)}) custom-call(s32[4]{0:T(128)} %pad_add_fusion.refs_0_, s32[1,3]{1,0:T(1,128)} %refs_1_.9, s32[1,3]{1,0:T(1,128)} %collective-permute-done.refs_5_.refs_1_.refs_2_, ...), custom_call_target="tpu_custom_call" | custom-call | flops 1 | bytes 1 | tf_op jit(solution)/shard_map/ffn/pallas_call | solution.py:57
  146.2 5.0 %all-to-all-start.3 = ((bf16[4,768,512]{2,1,0:T(8,128)(2,1)}), bf16[4,768,512]{2,1,0:T(8,128)(2,1)}, u32[]{:S(2)}, u32[]{:S(2)}) async-start(bf16[4,768,512]{2,1,0:T(8,128)(2,1)} %bitcast.29), calls=%async_computation.3 | async-start | bytes 6291456 | tf_op jit(solution)/shard_map/all_to_all | solution.py:1091
  153.4 3.1 %turn.1 = (f32[512,512]{1,0:T(8,128)}, bf16[512,512]{1,0:T(8,128)(2,1)}, f32[1,512]{1,0:T(1,128)}, f32[8,128]{1,0:T(8,128)}) custom-call(s32[1,3]{1,0:T(1,128)} %refs_1_.9, f32[512,512]{1,0:T(8,128)} %get-tuple-element.202.refs_1_.refs_0_, bf16[512,512]{1,0:T(8,128)(2,1)} %refs_2_.5, f32[512,512]{1,0:T(8,128)} %get-tuple-element.209.refs_3_, ...), custom_call_target="tpu_custom_call" | custom-call | flops 1 | bytes 1 | tf_op jit(solution)/shard_map/turn/pallas_call | solution.py:57
  158.8 9.1 %mixer_grad.2 = (bf16[3456,128]{1,0:T(8,128)(2,1)}, bf16[3456,128]{1,0:T(8,128)(2,1)}, bf16[3456,128]{1,0:T(8,128)(2,1)}, bf16[1728,128]{1,0:T(8,128)(2,1)}, bf1...) custom-call(s32[4]{0:T(128)} %pad_add_fusion.refs_0_, f32[16,512]{1,0:T(8,128)} %get-tuple-element.193.refs_13_.refs_3_.refs_5_.refs_1_, ...), custom_call_target="tpu_custom_call" | custom-call | flops 1 | bytes 1 | tf_op jit(solution)/shard_map/mixer_grad/pallas_call | solution.py:57
  170.4 9.1 %mixer_grad.3 = (bf16[3456,128]{1,0:T(8,128)(2,1)}, bf16[3456,128]{1,0:T(8,128)(2,1)}, bf16[3456,128]{1,0:T(8,128)(2,1)}, bf16[1728,128]{1,0:T(8,128)(2,1)}, bf1...) custom-call(s32[4]{0:T(128)} %pad_add_fusion.refs_0_, f32[16,512]{1,0:T(8,128)} %get-tuple-element.193.refs_13_.refs_3_.refs_5_.refs_1_, ...), custom_call_target="tpu_custom_call" | custom-call | flops 1 | bytes 1 | tf_op jit(solution)/shard_map/mixer_grad/pallas_call | solution.py:57
  187.5 9.5 %spread_back.2 = (f32[512,256]{1,0:T(8,128)}, f32[512,256]{1,0:T(8,128)}, f32[8,128]{1,0:T(8,128)}) custom-call(s32[4]{0:T(128)} %pad_add_fusion.refs_0_, s32[1,3]{1,0:T(1,128)} %refs_1_.9, s32[1,3]{1,0:T(1,128)} %collective-permute-done.refs_5_.refs_1_.refs_2_, f32[9,3,512]{2,1,0:T(4,128)} %reshape.75.refs_3_, ...), custom_call_target="tpu_custom_call" | custom-call | flops 1 | bytes 1 | tf_op jit(solution)/shard_map/spread_back/pallas_call | solution.py:57
  201.5 12.1 %spread_back.3 = (f32[512,256]{1,0:T(8,128)}, f32[512,256]{1,0:T(8,128)}, f32[1,256]{1,0:T(1,128)}, f32[32,128]{1,0:T(8,128)}, f32[8,128]{1,0:T(8,128)}) custom-call(s32[4]{0:T(128)} %pad_add_fusion.refs_0_, s32[1,3]{1,0:T(1,128)} %refs_1_.9, s32[1,3]{1,0:T(1,128)} %collective-permute-done.refs_5_.refs_1_.refs_2_, f32[9,3,512]{2,1,0:T(4,128)} %reshape.75.refs_3_, ...), custom_call_target="tpu_custom_call" | custom-call | flops 1 | bytes 1 | tf_op jit(solution)/shard_map/spread_back/pallas_call | solution.py:57
  213.6 2.8 line.3
  221.0 4.6 %all-to-all-start.4 = ((f32[32,1,128]{2,1,0:T(1,128)}), f32[32,1,128]{2,1,0:T(1,128)}, u32[]{:S(2)}, u32[]{:S(2)}) async-start(f32[32,1,128]{2,1,0:T(1,128)} %bitcast.35), calls=%async_computation.4 | async-start | bytes 32768 | tf_op jit(solution)/shard_map/all_to_all | solution.py:1123
  225.6 3.9 %collective-permute-done.35.refs_1_ = bf16[3456,128]{1,0:T(8,128)(2,1)} collective-permute-done((bf16[3456,128]{1,0:T(8,128)(2,1)}, bf16[3456,128]{1,0:T(8,128)(2,1)}, u32[]{:S(2)}, u32[]{:S(2)}) %collective-permute-start.35) | collective-permute-done | bytes 884768 | tf_op jit(solution)/shard_map/ppermute | solution.py:917
  229.9 2.6 line.4
  232.5 7.6 %all-to-all-done.4 = f32[32,1,128]{2,1,0:T(1,128)} async-done(((f32[32,1,128]{2,1,0:T(1,128)}), f32[32,1,128]{2,1,0:T(1,128)}, u32[]{:S(2)}, u32[]{:S(2)}) %all-to-all-start.4) | async-done | bytes 16416 | tf_op jit(solution)/shard_map/all_to_all | solution.py:1123
  242.4 4.2 %all-to-all-start.5 = ((bf16[4,864,128]{2,1,0:T(8,128)(2,1)}), bf16[4,864,128]{2,1,0:T(8,128)(2,1)}, u32[]{:S(2)}, u32[]{:S(2)}) async-start(bf16[4,864,128]{2,1,0:T(8,128)(2,1)} %bitcast.30), calls=%async_computation.5 | async-start | bytes 1769472 | tf_op jit(solution)/shard_map/all_to_all | solution.py:1091
  247.2 2.9 %line.5 = (f32[192,512]{1,0:T(8,128)}, bf16[192,512]{1,0:T(8,128)(2,1)}, bf16[192,512]{1,0:T(8,128)(2,1)}, bf16[192,512]{1,0:T(8,128)(2,1)}, f32[8,128]{1,0:T(8,128)}) custom-call(bf16[3072,512]{1,0:T(8,128)(2,1)} %bitcast.16.refs_1_.refs_0_.refs_2_.refs_3_, bf16[3072,512]{1,0:T(8,128)(2,1)} %bitcast.16.refs_1_.refs_0_.refs_2_.refs_3_, ...), custom_call_target="tpu_custom_call" | custom-call | flops 1 | bytes 1 | tf_op jit(solution)/shard_map/line/pallas_call | solution.py:57
  256.1 2.8 last.1
  264.4 4.9 %all-to-all-done.5 = bf16[4,864,128]{2,1,0:T(8,128)(2,1)} async-done(((bf16[4,864,128]{2,1,0:T(8,128)(2,1)}), bf16[4,864,128]{2,1,0:T(8,128)(2,1)}, u32[]{:S(2)}, u32[]{:S(2)}) %all-to-all-start.5) | async-done | bytes 884768 | tf_op jit(solution)/shard_map/all_to_all | solution.py:1091
  272.1 3.2 %all-to-all-start.6 = ((f32[32,1,128]{2,1,0:T(1,128)}), f32[32,1,128]{2,1,0:T(1,128)}, u32[]{:S(2)}, u32[]{:S(2)}) async-start(f32[32,1,128]{2,1,0:T(1,128)} %bitcast.36), calls=%async_computation.6 | async-start | bytes 32768 | tf_op jit(solution)/shard_map/all_to_all | solution.py:1123
  275.3 7.0 %all-to-all-done.6 = f32[32,1,128]{2,1,0:T(1,128)} async-done(((f32[32,1,128]{2,1,0:T(1,128)}), f32[32,1,128]{2,1,0:T(1,128)}, u32[]{:S(2)}, u32[]{:S(2)}) %all-to-all-start.6) | async-done | bytes 16416 | tf_op jit(solution)/shard_map/all_to_all | solution.py:1123
  282.4 6.3 %adam.1 = (f32[432,512]{1,0:T(8,128)}, f32[432,512]{1,0:T(8,128)}, f32[432,512]{1,0:T(8,128)}, f32[432,512]{1,0:T(8,128)}, f32[128,512]{1,0:T(8,128)}, /*index=5...) custom-call(s32[4]{0:T(128)} %pad_add_fusion.refs_0_, ...), custom_call_target="tpu_custom_call" | custom-call | flops 1 | bytes 1 | tf_op jit(solution)/shard_map/adam/pallas_call | solution.py:57
  (129 shorter events, 95.8 us)
Async XLA Ops:
  8.5 30.0 %all-to-all-start = ((bf16[4,880,128]{2,1,0:T(8,128)(2,1)}), bf16[4,880,128]{2,1,0:T(8,128)(2,1)}, u32[]{:S(2)}, u32[]{:S(2)}) async-start(bf16[4,880,128]{2,1,0:T(8,128)(2,1)} %bitcast.31), calls=%async_computation | async-start | bytes 1802240 | tf_op jit(solution)/shard_map/all_to_all | solution.py:1091
  15.4 13.8 %collective-permute-start.5 = (bf16[1760,128]{1,0:T(8,128)(2,1)}, bf16[1760,128]{1,0:T(8,128)(2,1)}, u32[]{:S(2)}, u32[]{:S(2)}) collective-permute-start(bf16[1760,128]{1,0:T(8,128)(2,1)} %get-tuple-element.166.refs_2_), channel_id=1, source_target_pairs={{0,8},{8,0},{1,9},{9,1},{2,10},{10,2},{3,11},{11,3},{4,12},{12,4},... | collective-permute-start | bytes 1351688 | tf_op jit(solution)/shard_map/ppermute | solution.py:917
  16.9 12.3 %collective-permute-start.6 = (bf16[1760,128]{1,0:T(8,128)(2,1)}, bf16[1760,128]{1,0:T(8,128)(2,1)}, u32[]{:S(2)}, u32[]{:S(2)}) collective-permute-start(bf16[1760,128]{1,0:T(8,128)(2,1)} %get-tuple-element.166.refs_2_), channel_id=1, source_target_pairs={{0,16},{16,0},{1,17},{17,1},{2,18},{18,2},{3,19},{19,3},{4,20},{20... | collective-permute-start | bytes 1351688 | tf_op jit(solution)/shard_map/ppermute | solution.py:917
  41.1 25.4 %all-to-all-start.1 = ((bf16[4,864,128]{2,1,0:T(8,128)(2,1)}), bf16[4,864,128]{2,1,0:T(8,128)(2,1)}, u32[]{:S(2)}, u32[]{:S(2)}) async-start(bf16[4,864,128]{2,1,0:T(8,128)(2,1)} %bitcast.32), calls=%async_computation.1 | async-start | bytes 1769472 | tf_op jit(solution)/shard_map/all_to_all | solution.py:1091
  45.9 15.2 %collective-permute-start.9 = (bf16[2640,128]{1,0:T(8,128)(2,1)}, bf16[2640,128]{1,0:T(8,128)(2,1)}, u32[]{:S(2)}, u32[]{:S(2)}) collective-permute-start(bf16[2640,128]{1,0:T(8,128)(2,1)} %get-tuple-element.179.refs_6_), channel_id=1, source_target_pairs={{0,8},{8,0},{1,9},{9,1},{2,10},{10,2},{3,11},{11,3},{4,12},{12,4},... | collective-permute-start | bytes 2027528 | tf_op jit(solution)/shard_map/ppermute | solution.py:917
  47.4 14.9 %collective-permute-start.10 = (bf16[2640,128]{1,0:T(8,128)(2,1)}, bf16[2640,128]{1,0:T(8,128)(2,1)}, u32[]{:S(2)}, u32[]{:S(2)}) collective-permute-start(bf16[2640,128]{1,0:T(8,128)(2,1)} %get-tuple-element.179.refs_6_), channel_id=1, source_target_pairs={{0,16},{16,0},{1,17},{17,1},{2,18},{18,2},{3,19},{19,3},{4,20},{20... | collective-permute-start | bytes 2027528 | tf_op jit(solution)/shard_map/ppermute | solution.py:917
  64.4 9.2 %collective-permute-start.11 = (bf16[1344,128]{1,0:T(8,128)(2,1)}, bf16[1344,128]{1,0:T(8,128)(2,1)}, u32[]{:S(2)}, u32[]{:S(2)}) collective-permute-start(bf16[1344,128]{1,0:T(8,128)(2,1)} %get-tuple-element.183), channel_id=1, source_target_pairs={{0,8},{8,0},{1,9},{9,1},{2,10},{10,2},{3,11},{11,3},{4,12},{12,4},... | collective-permute-start | bytes 1032200 | tf_op jit(solution)/shard_map/ppermute | solution.py:917
  68.9 31.6 %all-to-all-start.2 = ((bf16[4,192,512]{2,1,0:T(8,128)(2,1)}), bf16[4,192,512]{2,1,0:T(8,128)(2,1)}, u32[]{:S(2)}, u32[]{:S(2)}) async-start(bf16[4,192,512]{2,1,0:T(8,128)(2,1)} %bitcast.33), calls=%async_computation.2 | async-start | bytes 1572864 | tf_op jit(solution)/shard_map/all_to_all | solution.py:1091
  73.6 15.6 %collective-permute-start.13 = (bf16[2592,128]{1,0:T(8,128)(2,1)}, bf16[2592,128]{1,0:T(8,128)(2,1)}, u32[]{:S(2)}, u32[]{:S(2)}) collective-permute-start(bf16[2592,128]{1,0:T(8,128)(2,1)} %get-tuple-element.186.refs_6_), channel_id=1, source_target_pairs={{0,8},{8,0},{1,9},{9,1},{2,10},{10,2},{3,11},{11,3},{4,12},{12,4},... | collective-permute-start | bytes 1990664 | tf_op jit(solution)/shard_map/ppermute | solution.py:917
  75.2 15.2 %collective-permute-start.14 = (bf16[2592,128]{1,0:T(8,128)(2,1)}, bf16[2592,128]{1,0:T(8,128)(2,1)}, u32[]{:S(2)}, u32[]{:S(2)}) collective-permute-start(bf16[2592,128]{1,0:T(8,128)(2,1)} %get-tuple-element.186.refs_6_), channel_id=1, source_target_pairs={{0,16},{16,0},{1,17},{17,1},{2,18},{18,2},{3,19},{19,3},{4,20},{20... | collective-permute-start | bytes 1990664 | tf_op jit(solution)/shard_map/ppermute | solution.py:917
  100.5 16.3 %collective-permute-start.18 = (bf16[768,512]{1,0:T(8,128)(2,1)}, bf16[768,512]{1,0:T(8,128)(2,1)}, u32[]{:S(2)}, u32[]{:S(2)}) collective-permute-start(bf16[768,512]{1,0:T(8,128)(2,1)} %get-tuple-element.199), channel_id=1, source_target_pairs={{0,8},{8,0},{1,9},{9,1},{2,10},{10,2},{3,11},{11,3},{4,12},{12,4},... | collective-permute-start | bytes 2359304 | tf_op jit(solution)/shard_map/ppermute | solution.py:917
  102.1 16.0 %collective-permute-start.19 = (bf16[768,512]{1,0:T(8,128)(2,1)}, bf16[768,512]{1,0:T(8,128)(2,1)}, u32[]{:S(2)}, u32[]{:S(2)}) collective-permute-start(bf16[768,512]{1,0:T(8,128)(2,1)} %get-tuple-element.199), channel_id=1, source_target_pairs={{0,16},{16,0},{1,17},{17,1},{2,18},{18,2},{3,19},{19,3},{4,20},{20... | collective-permute-start | bytes 2359304 | tf_op jit(solution)/shard_map/ppermute | solution.py:917
  146.2 74.8 %all-to-all-start.3 = ((bf16[4,768,512]{2,1,0:T(8,128)(2,1)}), bf16[4,768,512]{2,1,0:T(8,128)(2,1)}, u32[]{:S(2)}, u32[]{:S(2)}) async-start(bf16[4,768,512]{2,1,0:T(8,128)(2,1)} %bitcast.29), calls=%async_computation.3 | async-start | bytes 6291456 | tf_op jit(solution)/shard_map/all_to_all | solution.py:1091
  167.9 13.3 %collective-permute-start.26 = (bf16[1728,128]{1,0:T(8,128)(2,1)}, bf16[1728,128]{1,0:T(8,128)(2,1)}, u32[]{:S(2)}, u32[]{:S(2)}) collective-permute-start(bf16[1728,128]{1,0:T(8,128)(2,1)} %get-tuple-element.219), channel_id=1, source_target_pairs={{0,8},{8,0},{1,9},{9,1},{2,10},{10,2},{3,11},{11,3},{4,12},{12,4},... | collective-permute-start | bytes 1327112 | tf_op jit(solution)/shard_map/ppermute | solution.py:917
  169.4 12.2 %collective-permute-start.27 = (bf16[1728,128]{1,0:T(8,128)(2,1)}, bf16[1728,128]{1,0:T(8,128)(2,1)}, u32[]{:S(2)}, u32[]{:S(2)}) collective-permute-start(bf16[1728,128]{1,0:T(8,128)(2,1)} %get-tuple-element.220), channel_id=1, source_target_pairs={{0,16},{16,0},{1,17},{17,1},{2,18},{18,2},{3,19},{19,3},{4,20},{20... | collective-permute-start | bytes 1327112 | tf_op jit(solution)/shard_map/ppermute | solution.py:917
  179.5 17.5 %collective-permute-start.30 = (bf16[1728,128]{1,0:T(8,128)(2,1)}, bf16[1728,128]{1,0:T(8,128)(2,1)}, u32[]{:S(2)}, u32[]{:S(2)}) collective-permute-start(bf16[1728,128]{1,0:T(8,128)(2,1)} %get-tuple-element.233), channel_id=1, source_target_pairs={{0,8},{8,0},{1,9},{9,1},{2,10},{10,2},{3,11},{11,3},{4,12},{12,4},... | collective-permute-start | bytes 1327112 | tf_op jit(solution)/shard_map/ppermute | solution.py:917
  180.3 16.7 %collective-permute-start.31 = (bf16[1728,128]{1,0:T(8,128)(2,1)}, bf16[1728,128]{1,0:T(8,128)(2,1)}, u32[]{:S(2)}, u32[]{:S(2)}) collective-permute-start(bf16[1728,128]{1,0:T(8,128)(2,1)} %get-tuple-element.234), channel_id=1, source_target_pairs={{0,16},{16,0},{1,17},{17,1},{2,18},{18,2},{3,19},{19,3},{4,20},{20... | collective-permute-start | bytes 1327112 | tf_op jit(solution)/shard_map/ppermute | solution.py:917
  184.0 29.5 %collective-permute-start.28 = (bf16[3456,128]{1,0:T(8,128)(2,1)}, bf16[3456,128]{1,0:T(8,128)(2,1)}, u32[]{:S(2)}, u32[]{:S(2)}) collective-permute-start(bf16[3456,128]{1,0:T(8,128)(2,1)} %get-tuple-element.223), channel_id=1, source_target_pairs={{0,8},{8,0},{1,9},{9,1},{2,10},{10,2},{3,11},{11,3},{4,12},{12,4},... | collective-permute-start | bytes 2654216 | tf_op jit(solution)/shard_map/ppermute | solution.py:917
  185.0 28.5 %collective-permute-start.29 = (bf16[3456,128]{1,0:T(8,128)(2,1)}, bf16[3456,128]{1,0:T(8,128)(2,1)}, u32[]{:S(2)}, u32[]{:S(2)}) collective-permute-start(bf16[3456,128]{1,0:T(8,128)(2,1)} %get-tuple-element.224), channel_id=1, source_target_pairs={{0,16},{16,0},{1,17},{17,1},{2,18},{18,2},{3,19},{19,3},{4,20},{20... | collective-permute-start | bytes 2654216 | tf_op jit(solution)/shard_map/ppermute | solution.py:917
  199.4 30.1 %collective-permute-start.35 = (bf16[3456,128]{1,0:T(8,128)(2,1)}, bf16[3456,128]{1,0:T(8,128)(2,1)}, u32[]{:S(2)}, u32[]{:S(2)}) collective-permute-start(bf16[3456,128]{1,0:T(8,128)(2,1)} %get-tuple-element.247), channel_id=1, source_target_pairs={{0,8},{8,0},{1,9},{9,1},{2,10},{10,2},{3,11},{11,3},{4,12},{12,4},... | collective-permute-start | bytes 2654216 | tf_op jit(solution)/shard_map/ppermute | solution.py:917
  200.4 29.5 %collective-permute-start.36 = (bf16[3456,128]{1,0:T(8,128)(2,1)}, bf16[3456,128]{1,0:T(8,128)(2,1)}, u32[]{:S(2)}, u32[]{:S(2)}) collective-permute-start(bf16[3456,128]{1,0:T(8,128)(2,1)} %get-tuple-element.248), channel_id=1, source_target_pairs={{0,16},{16,0},{1,17},{17,1},{2,18},{18,2},{3,19},{19,3},{4,20},{20... | collective-permute-start | bytes 2654216 | tf_op jit(solution)/shard_map/ppermute | solution.py:917
  216.3 23.9 %collective-permute-start.32 = (bf16[864,128]{1,0:T(8,128)(2,1)}, bf16[864,128]{1,0:T(8,128)(2,1)}, u32[]{:S(2)}, u32[]{:S(2)}) collective-permute-start(bf16[864,128]{1,0:T(8,128)(2,1)} %get-tuple-element.239), channel_id=1, source_target_pairs={{0,2},{2,0},{4,6},{6,4},{1,3},{3,1},{5,7},{7,5},{8,10},{10,8},{12,... | collective-permute-start | bytes 663560 | tf_op jit(solution)/shard_map/ppermute | solution.py:917
  218.2 21.9 %collective-permute-start.33 = (bf16[864,128]{1,0:T(8,128)(2,1)}, bf16[864,128]{1,0:T(8,128)(2,1)}, u32[]{:S(2)}, u32[]{:S(2)}) collective-permute-start(bf16[864,128]{1,0:T(8,128)(2,1)} %get-tuple-element.240), channel_id=1, source_target_pairs={{0,4},{2,6},{4,0},{6,2},{1,5},{3,7},{5,1},{7,3},{8,12},{10,14},{12... | collective-permute-start | bytes 663560 | tf_op jit(solution)/shard_map/ppermute | solution.py:917
  220.6 19.6 %collective-permute-start.34 = (bf16[864,128]{1,0:T(8,128)(2,1)}, bf16[864,128]{1,0:T(8,128)(2,1)}, u32[]{:S(2)}, u32[]{:S(2)}) collective-permute-start(bf16[864,128]{1,0:T(8,128)(2,1)} %get-tuple-element.241), channel_id=1, source_target_pairs={{0,6},{2,4},{4,2},{6,0},{1,7},{3,5},{5,3},{7,1},{8,14},{10,12},{12... | collective-permute-start | bytes 663560 | tf_op jit(solution)/shard_map/ppermute | solution.py:917
  221.0 19.2 %all-to-all-start.4 = ((f32[32,1,128]{2,1,0:T(1,128)}), f32[32,1,128]{2,1,0:T(1,128)}, u32[]{:S(2)}, u32[]{:S(2)}) async-start(f32[32,1,128]{2,1,0:T(1,128)} %bitcast.35), calls=%async_computation.4 | async-start | bytes 32768 | tf_op jit(solution)/shard_map/all_to_all | solution.py:1123
  242.4 27.0 %all-to-all-start.5 = ((bf16[4,864,128]{2,1,0:T(8,128)(2,1)}), bf16[4,864,128]{2,1,0:T(8,128)(2,1)}, u32[]{:S(2)}, u32[]{:S(2)}) async-start(bf16[4,864,128]{2,1,0:T(8,128)(2,1)} %bitcast.30), calls=%async_computation.5 | async-start | bytes 1769472 | tf_op jit(solution)/shard_map/all_to_all | solution.py:1091
  246.7 9.3 %collective-permute-start.38 = (f32[512,256]{1,0:T(8,128)}, f32[512,256]{1,0:T(8,128)}, u32[]{:S(2)}, u32[]{:S(2)}) collective-permute-start(f32[512,256]{1,0:T(8,128)} %get-tuple-element.261), channel_id=1, source_target_pairs={{0,1},{1,0},{2,3},{3,2},{4,5},{5,4},{6,7},{7,6},{8,9},{9,8},{10,11... | collective-permute-start | bytes 1572872 | tf_op jit(solution)/shard_map/ppermute | solution.py:917
  250.9 10.1 %collective-permute-start.40 = (bf16[192,512]{1,0:T(8,128)(2,1)}, bf16[192,512]{1,0:T(8,128)(2,1)}, u32[]{:S(2)}, u32[]{:S(2)}) collective-permute-start(bf16[192,512]{1,0:T(8,128)(2,1)} %get-tuple-element.267), channel_id=1, source_target_pairs={{0,16},{16,0},{1,17},{17,1},{2,18},{18,2},{3,19},{19,3},{4,20},{20... | collective-permute-start | bytes 589832 | tf_op jit(solution)/shard_map/ppermute | solution.py:917
  252.3 10.1 %collective-permute-start.41 = (bf16[192,512]{1,0:T(8,128)(2,1)}, bf16[192,512]{1,0:T(8,128)(2,1)}, u32[]{:S(2)}, u32[]{:S(2)}) collective-permute-start(bf16[192,512]{1,0:T(8,128)(2,1)} %get-tuple-element.268), channel_id=1, source_target_pairs={{0,24},{8,16},{16,8},{24,0},{1,25},{9,17},{17,9},{25,1},{2,26},{10... | collective-permute-start | bytes 589832 | tf_op jit(solution)/shard_map/ppermute | solution.py:1108
  253.6 21.7 %collective-permute-start.42 = (f32[432,128]{1,0:T(8,128)}, f32[432,128]{1,0:T(8,128)}, u32[]{:S(2)}, u32[]{:S(2)}) collective-permute-start(f32[432,128]{1,0:T(8,128)} %get-tuple-element.276), channel_id=1, source_target_pairs={{0,1},{1,0},{2,3},{3,2},{4,5},{5,4},{6,7},{7,6},{8,9},{9,8},{10,11... | collective-permute-start | bytes 663560 | tf_op jit(solution)/shard_map/ppermute | solution.py:917
  271.6 10.8 %collective-permute-start.43 = (f32[432,128]{1,0:T(8,128)}, f32[432,128]{1,0:T(8,128)}, u32[]{:S(2)}, u32[]{:S(2)}) collective-permute-start(f32[432,128]{1,0:T(8,128)} %get-tuple-element.277), channel_id=1, source_target_pairs={{0,1},{1,0},{2,3},{3,2},{4,5},{5,4},{6,7},{7,6},{8,9},{9,8},{10,11... | collective-permute-start | bytes 663560 | tf_op jit(solution)/shard_map/ppermute | solution.py:917
  272.1 10.2 %all-to-all-start.6 = ((f32[32,1,128]{2,1,0:T(1,128)}), f32[32,1,128]{2,1,0:T(1,128)}, u32[]{:S(2)}, u32[]{:S(2)}) async-start(f32[32,1,128]{2,1,0:T(1,128)} %bitcast.36), calls=%async_computation.6 | async-start | bytes 32768 | tf_op jit(solution)/shard_map/all_to_all | solution.py:1123
  (23 other events, 114.9 us)

commit v2 on v1

--- a/solution.py
+++ b/solution.py
@@ -726,13 +726,13 @@
         refs[count + o][b : b + rows] = refs[i][pl.ds(a, rows)]
 
 
-def stack_call(chain, spot, arrays, rows, moves, waits=()):
+def stack_call(chain, spot, arrays, rows, moves, through=()):
     like = {o: arrays[i] for i, _, _, o, _ in moves}
     shapes = [(r,) + like[o].shape[1:] for o, r in enumerate(rows)]
     return chain.call(
         functools.partial(stack_kernel, len(arrays), moves), "stack", (spot, *arrays),
         [smem()] + [fixed(*v.shape) for v in arrays],
-        [fixed(*s) for s in shapes], [shaped(s, like[o].dtype) for o, s in enumerate(shapes)], grid=(1,), waits=waits,
+        [fixed(*s) for s in shapes], [shaped(s, like[o].dtype) for o, s in enumerate(shapes)], grid=(1,), through=through,
     )
 
 
@@ -744,12 +744,21 @@
     to_y_ref[...] = x_ref[cut : rows - extra]
 
 
+def whole_corner_kernel(x_ref, y_ref, to_x_ref, to_y_ref):
+    to_x_ref[...] = y_ref[...]
+    to_y_ref[...] = x_ref[...]
+
+
 def corner_call(chain, from_x, from_y, extra):
     total, width = from_x.shape
     cut = (total - extra) // 2
     shapes = [(cut + extra, width), (cut, width)]
-    return chain.call(
-        functools.partial(corner_kernel, cut, extra), "corner", (from_x, from_y), [fixed(total, width)] * 2,
+    ins, kernel = [fixed(total, width)] * 2, functools.partial(corner_kernel, cut, extra)
+    if not extra:
+        ins = [pl.BlockSpec((cut, width), lambda i: (1, 0)), pl.BlockSpec((cut, width), lambda i: (0, 0))]
+        kernel = whole_corner_kernel
+    return chain.call(
+        kernel, "corner", (from_x, from_y), ins,
         [fixed(*s) for s in shapes], [shaped(s, bf) for s in shapes], grid=(1,),
     )
 
@@ -1027,8 +1036,17 @@
         )
         line = self.along_z(block)
         own_x, own_y = flip(own, "d1"), flip(own, "d0")
+        rows = own.shape[0] // 2 - NOTE
+        units, count = gate_mine.shape[0], down_low.shape[0]
+        ffn_rows = 2 * units + count
+        moves = [(0, rows + NOTE, rows, 0, s * rows) for s in range(size)]
+        for s in range(size):
+            at = s * ffn_rows
+            moves += [(1, 0, units, 1, at), (2, 0, units, 1, at + units), (3, 0, count, 1, at + 2 * units)]
+        second_block, ffn_block = stack_call(
+            chain, spot, (own, gate_mine, gate_came, down_low), (size * rows, size * ffn_rows), tuple(moves)
+        )
         yield None
-        rows = own.shape[0] // 2 - NOTE
         half = rows // 2
         sides = []
 
@@ -1055,9 +1073,8 @@
         others, line_rows = range(1, size), (size - 1) * rows
         moves = [(0, (rows + NOTE, s, 0), rows, 0, (s - 1) * rows) for s in others]
         moves += [(0, (rows + NOTE, s, rows), NOTE, 0, line_rows + (s - 1) * NOTE) for s in others]
-        moves += [(1, rows + NOTE, rows, 1, s * rows) for s in range(size)]
         line, block = stack_call(
-            chain, spot, (line, own), (line_rows + (size - 1) * NOTE, size * rows), tuple(moves)
+            chain, spot, (line,), (line_rows + (size - 1) * NOTE,), tuple(moves), through=(second_block,)
         )
         first = spread_out(line)
         line = self.along_z(block)
@@ -1068,15 +1085,8 @@
             notes += [(4 + p, line_rows + (s - 1) * NOTE, near + (s, False)) for p, near in enumerate(self.near[:3])]
             notes.append((7, line_rows // 2 + (s - 1) * NOTE, (1, 1, s, False)))
         sides.append(([own, own_x, own_y, corner[0], *first, *first_corner], plan(0), tuple(notes)))
-        units, count = gate_mine.shape[0], down_low.shape[0]
-        ffn_rows = 2 * units + count
         moves = [(0, (rows, s, 0), rows, 0, (s - 1) * rows) for s in others]
-        for s in range(size):
-            at = s * ffn_rows
-            moves += [(1, 0, units, 1, at), (2, 0, units, 1, at + units), (3, 0, count, 1, at + 2 * units)]
-        line, block = stack_call(
-            chain, spot, (line, gate_mine, gate_came, down_low), (line_rows, size * ffn_rows), tuple(moves)
-        )
+        line, block = stack_call(chain, spot, (line,), (line_rows,), tuple(moves), through=(ffn_block,))
         across, line = line, self.along_z(block)
         second = spread_out(*chain.pause(first_corner, (across,)))
         yield sides, None
@@ -1150,7 +1160,7 @@
     gains = next(weights)
     tokens = hat_tokens = normed_call(chain, spot, inputs, source_other)
     blocks = taps.shape[0]
-    cuts, spread = (0, blocks // 3, blocks * 4 // 9, blocks), None
+    cuts, spread = (0, blocks * 2 // 9, blocks // 3, blocks), None
     for at in range(3):
         spread = spread_call(chain, sums, taps_turned, *tokens, cuts[at], cuts[at + 1] - cuts[at], spread)
         sides = next(weights)

time: 290 us -> 290 us (level)
  starting transfers between devices: 71.7 us -> 67.6 us
    ppermute x44, starting transfers between devices: 37.7 us -> 33.3 us  [flip(): return lax.ppermute(v, axis, [(i, i ^ bits) for i in range(size)])]
    pallas_call x39 -> x40, Pallas kernels: 156 us -> 157 us  [call(): pl.pallas_call(whole, name=name, in_specs=list(in_specs) + [anywhere() fo...]
  transfers between devices with their start and end apart: 52 -> 52, of which waited for: 26 -> 25; matrix products, arithmetic and copies ran while one was open for 1% -> 1% of each run, Pallas kernels for 44% -> 44%
where the time goes in v2:
time: 290 us; the launch traced here: 288 us
  Pallas kernels  157 us (54%)
  starting transfers between devices  67.6 us (23%)
  waiting for transfers between devices  57.9 us (20%)
    pallas_call x40, Pallas kernels, call(): pl.pallas_call(whole, name=name, in_specs=list(in_specs) + [anywhere() fo...  157 us
    ppermute x44, waiting for transfers between devices, flip(): return lax.ppermute(v, axis, [(i, i ^ bits) for i in range(size)])  36.7 us
    ppermute x44, starting transfers between devices, flip(): return lax.ppermute(v, axis, [(i, i ^ bits) for i in range(size)])  33.3 us
    all_to_all x5, starting transfers between devices, along_z(): return lax.all_to_all(v, 'z', 0, 0, tiled=True)  24.4 us
    all_to_all x2, waiting for transfers between devices, everyone(): return lax.all_to_all(rows, EVERY, 0, 0, tiled=True)  15.3 us
    all_to_all x2, starting transfers between devices, everyone(): return lax.all_to_all(rows, EVERY, 0, 0, tiled=True)  8.12 us
    all_to_all x5, waiting for transfers between devices, along_z(): return lax.all_to_all(v, 'z', 0, 0, tiled=True)  5.91 us
  transfers between devices with their start and end apart: 52, of which 25 were waited for; matrix products, arithmetic and copies ran while one was open for 1% of the time, Pallas kernels for 44%

profile of v2, /device:TPU:0, one launch (start us, length us, event | category | flops | bytes accessed | tf_op | source)
XLA Modules:
  0.0 288.1 jit_solution(23482950693961955)
XLA Ops:
  8.5 6.2 %all-to-all-start = ((bf16[4,880,128]{2,1,0:T(8,128)(2,1)}), bf16[4,880,128]{2,1,0:T(8,128)(2,1)}, u32[]{:S(2)}, u32[]{:S(2)}) async-start(bf16[4,880,128]{2,1,0:T(8,128)(2,1)} %bitcast.33), calls=%async_computation | async-start | bytes 1802240 | tf_op jit(solution)/shard_map/all_to_all | solution.py:1101
  24.6 5.5 %spread.3 = (bf16[2,1024,3456]{2,1,0:T(8,128)(2,1)}, f32[8,128]{1,0:T(8,128)}) custom-call(s32[1,3]{1,0:T(1,128)} %refs_1_.9, s32[1,3]{1,0:T(1,128)} %collective-permute-done.refs_5_.refs_1_.refs_2_, f32[9,3,512]{2,1,0:T(4,128)} %reshape.69.refs_2_, bf16[512,256]{1,0:T(8,128)(2,1)} %get-tuple-element.169.refs_3_.refs_10_, ...), custom_call_target="tpu_custom_call" | custom-call | flops 1 | bytes 1 | tf_op jit(solution)/shard_map/spread/pallas_call | solution.py:57
  33.0 4.1 %spread.4 = (bf16[2,1024,3456]{2,1,0:T(8,128)(2,1)}, f32[8,128]{1,0:T(8,128)}) custom-call(s32[1,3]{1,0:T(1,128)} %refs_1_.9, s32[1,3]{1,0:T(1,128)} %collective-permute-done.refs_5_.refs_1_.refs_2_, f32[9,3,512]{2,1,0:T(4,128)} %reshape.69.refs_2_, bf16[512,256]{1,0:T(8,128)(2,1)} %get-tuple-element.169.refs_3_.refs_10_, ...), custom_call_target="tpu_custom_call", output_to_operand_aliasing={{0}: (5, {})} | custom-call | flops 1 | bytes 1 | tf_op jit(solution)/shard_map/spread/pallas_call | solution.py:57
  41.3 4.8 %all-to-all-start.1 = ((bf16[4,864,128]{2,1,0:T(8,128)(2,1)}), bf16[4,864,128]{2,1,0:T(8,128)(2,1)}, u32[]{:S(2)}, u32[]{:S(2)}) async-start(bf16[4,864,128]{2,1,0:T(8,128)(2,1)} %bitcast.31), calls=%async_computation.1 | async-start | bytes 1769472 | tf_op jit(solution)/shard_map/all_to_all | solution.py:1101
  48.1 11.2 %spread.5 = (bf16[2,1024,3456]{2,1,0:T(8,128)(2,1)}, f32[8,128]{1,0:T(8,128)}) custom-call(s32[1,3]{1,0:T(1,128)} %refs_1_.9, s32[1,3]{1,0:T(1,128)} %collective-permute-done.refs_5_.refs_1_.refs_2_, f32[9,3,512]{2,1,0:T(4,128)} %reshape.69.refs_2_, bf16[512,256]{1,0:T(8,128)(2,1)} %get-tuple-element.169.refs_3_.refs_10_, ...), custom_call_target="tpu_custom_call", output_to_operand_aliasing={{0}: (5, {})} | custom-call | flops 1 | bytes 1 | tf_op jit(solution)/shard_map/spread/pallas_call | solution.py:57
  68.6 4.2 %all-to-all-start.2 = ((bf16[4,192,512]{2,1,0:T(8,128)(2,1)}), bf16[4,192,512]{2,1,0:T(8,128)(2,1)}, u32[]{:S(2)}, u32[]{:S(2)}) async-start(bf16[4,192,512]{2,1,0:T(8,128)(2,1)} %bitcast.32), calls=%async_computation.2 | async-start | bytes 1572864 | tf_op jit(solution)/shard_map/all_to_all | solution.py:1101
  75.5 10.7 %mix.2 = (f32[512,512]{1,0:T(8,128)}, f32[512,512]{1,0:T(8,128)}, bf16[13824,128]{1,0:T(8,128)(2,1)}, f32[16,512]{1,0:T(8,128)}, f32[8,128]{1,0:T(8,128)}) custom-call(s32[4]{0:T(128)} %pad_add_fusion.refs_0_, bf16[2,1024,3456]{2,1,0:T(8,128)(2,1)} %get-tuple-element.182.refs_1_.refs_4_, bf16[1760,128]{1,0:T(8,128)(2,1)} %get-tuple-element.164.refs_1_.refs_2_, ...), custom_call_target="tpu_custom_call" | custom-call | flops 1 | bytes 1 | tf_op jit(solution)/shard_map/mix/pallas_call | solution.py:57
  86.2 2.8 collective-permute-done.13.refs_0_.refs_7_
  93.6 6.5 %collective-permute-done.15.refs_1_.refs_9_ = bf16[1296,128]{1,0:T(8,128)(2,1)} collective-permute-done((bf16[1296,128]{1,0:T(8,128)(2,1)}, bf16[1296,128]{1,0:T(8,128)(2,1)}, u32[]{:S(2)}, u32[]{:S(2)}) %collective-permute-start.15) | collective-permute-done | bytes 331808 | tf_op jit(solution)/shard_map/ppermute | solution.py:926
  102.8 11.5 %mix.3 = (f32[512,512]{1,0:T(8,128)}, bf16[512,512]{1,0:T(8,128)(2,1)}, bf16[13824,128]{1,0:T(8,128)(2,1)}, f32[8,128]{1,0:T(8,128)}) custom-call(s32[4]{0:T(128)} %pad_add_fusion.refs_0_, bf16[2,1024,3456]{2,1,0:T(8,128)(2,1)} %get-tuple-element.182.refs_1_.refs_4_, bf16[1760,128]{1,0:T(8,128)(2,1)} %get-tuple-element.164.refs_1_.refs_2_, ...), custom_call_target="tpu_custom_call" | custom-call | flops 1 | bytes 1 | tf_op jit(solution)/shard_map/mix/pallas_call | solution.py:57
  114.5 2.4 collective-permute-done.18.refs_0_
  121.4 2.5 hidden.1
  128.8 16.5 %ffn.1 = (f32[512,512]{1,0:T(8,128)}, bf16[512,512]{1,0:T(8,128)(2,1)}, f32[512,512]{1,0:T(8,128)}, bf16[512,512]{1,0:T(8,128)(2,1)}, bf16[16,192,512]{2,1,0:T(8,128)(2,1)}, /*index=5*/f32[8,128]{1,0:T(8,128)}) custom-call(s32[4]{0:T(128)} %pad_add_fusion.refs_0_, s32[1,3]{1,0:T(1,128)} %refs_1_.9, s32[1,3]{1,0:T(1,128)} %collective-permute-done.refs_5_.refs_1_.refs_2_, ...), custom_call_target="tpu_custom_call" | custom-call | flops 1 | bytes 1 | tf_op jit(solution)/shard_map/ffn/pallas_call | solution.py:57
  145.3 5.0 %all-to-all-start.3 = ((bf16[4,768,512]{2,1,0:T(8,128)(2,1)}), bf16[4,768,512]{2,1,0:T(8,128)(2,1)}, u32[]{:S(2)}, u32[]{:S(2)}) async-start(bf16[4,768,512]{2,1,0:T(8,128)(2,1)} %bitcast.29), calls=%async_computation.3 | async-start | bytes 6291456 | tf_op jit(solution)/shard_map/all_to_all | solution.py:1101
  152.4 3.1 %turn.1 = (f32[512,512]{1,0:T(8,128)}, bf16[512,512]{1,0:T(8,128)(2,1)}, f32[1,512]{1,0:T(1,128)}, f32[8,128]{1,0:T(8,128)}) custom-call(s32[1,3]{1,0:T(1,128)} %refs_1_.9, f32[512,512]{1,0:T(8,128)} %get-tuple-element.208.refs_1_.refs_0_, bf16[512,512]{1,0:T(8,128)(2,1)} %refs_2_.5, f32[512,512]{1,0:T(8,128)} %get-tuple-element.215.refs_3_, ...), custom_call_target="tpu_custom_call" | custom-call | flops 1 | bytes 1 | tf_op jit(solution)/shard_map/turn/pallas_call | solution.py:57
  157.9 9.1 %mixer_grad.2 = (bf16[3456,128]{1,0:T(8,128)(2,1)}, bf16[3456,128]{1,0:T(8,128)(2,1)}, bf16[3456,128]{1,0:T(8,128)(2,1)}, bf16[1728,128]{1,0:T(8,128)(2,1)}, bf1...) custom-call(s32[4]{0:T(128)} %pad_add_fusion.refs_0_, f32[16,512]{1,0:T(8,128)} %get-tuple-element.199.refs_13_.refs_3_.refs_5_.refs_1_, ...), custom_call_target="tpu_custom_call" | custom-call | flops 1 | bytes 1 | tf_op jit(solution)/shard_map/mixer_grad/pallas_call | solution.py:57
  169.3 9.1 %mixer_grad.3 = (bf16[3456,128]{1,0:T(8,128)(2,1)}, bf16[3456,128]{1,0:T(8,128)(2,1)}, bf16[3456,128]{1,0:T(8,128)(2,1)}, bf16[1728,128]{1,0:T(8,128)(2,1)}, bf1...) custom-call(s32[4]{0:T(128)} %pad_add_fusion.refs_0_, f32[16,512]{1,0:T(8,128)} %get-tuple-element.199.refs_13_.refs_3_.refs_5_.refs_1_, ...), custom_call_target="tpu_custom_call" | custom-call | flops 1 | bytes 1 | tf_op jit(solution)/shard_map/mixer_grad/pallas_call | solution.py:57
  186.4 9.5 %spread_back.2 = (f32[512,256]{1,0:T(8,128)}, f32[512,256]{1,0:T(8,128)}, f32[8,128]{1,0:T(8,128)}) custom-call(s32[4]{0:T(128)} %pad_add_fusion.refs_0_, s32[1,3]{1,0:T(1,128)} %refs_1_.9, s32[1,3]{1,0:T(1,128)} %collective-permute-done.refs_5_.refs_1_.refs_2_, f32[9,3,512]{2,1,0:T(4,128)} %reshape.75.refs_3_, ...), custom_call_target="tpu_custom_call" | custom-call | flops 1 | bytes 1 | tf_op jit(solution)/shard_map/spread_back/pallas_call | solution.py:57
  200.5 12.1 %spread_back.3 = (f32[512,256]{1,0:T(8,128)}, f32[512,256]{1,0:T(8,128)}, f32[1,256]{1,0:T(1,128)}, f32[32,128]{1,0:T(8,128)}, f32[8,128]{1,0:T(8,128)}) custom-call(s32[4]{0:T(128)} %pad_add_fusion.refs_0_, s32[1,3]{1,0:T(1,128)} %refs_1_.9, s32[1,3]{1,0:T(1,128)} %collective-permute-done.refs_5_.refs_1_.refs_2_, f32[9,3,512]{2,1,0:T(4,128)} %reshape.75.refs_3_, ...), custom_call_target="tpu_custom_call" | custom-call | flops 1 | bytes 1 | tf_op jit(solution)/shard_map/spread_back/pallas_call | solution.py:57
  212.6 2.8 line.3
  219.8 4.9 %all-to-all-start.4 = ((f32[32,1,128]{2,1,0:T(1,128)}), f32[32,1,128]{2,1,0:T(1,128)}, u32[]{:S(2)}, u32[]{:S(2)}) async-start(f32[32,1,128]{2,1,0:T(1,128)} %bitcast.35), calls=%async_computation.4 | async-start | bytes 32768 | tf_op jit(solution)/shard_map/all_to_all | solution.py:1133
  224.7 3.7 %collective-permute-done.35.refs_1_ = bf16[3456,128]{1,0:T(8,128)(2,1)} collective-permute-done((bf16[3456,128]{1,0:T(8,128)(2,1)}, bf16[3456,128]{1,0:T(8,128)(2,1)}, u32[]{:S(2)}, u32[]{:S(2)}) %collective-permute-start.35) | collective-permute-done | bytes 884768 | tf_op jit(solution)/shard_map/ppermute | solution.py:926
  228.6 2.6 line.4
  231.2 8.2 %all-to-all-done.4 = f32[32,1,128]{2,1,0:T(1,128)} async-done(((f32[32,1,128]{2,1,0:T(1,128)}), f32[32,1,128]{2,1,0:T(1,128)}, u32[]{:S(2)}, u32[]{:S(2)}) %all-to-all-start.4) | async-done | bytes 16416 | tf_op jit(solution)/shard_map/all_to_all | solution.py:1133
  241.7 4.2 %all-to-all-start.5 = ((bf16[4,864,128]{2,1,0:T(8,128)(2,1)}), bf16[4,864,128]{2,1,0:T(8,128)(2,1)}, u32[]{:S(2)}, u32[]{:S(2)}) async-start(bf16[4,864,128]{2,1,0:T(8,128)(2,1)} %bitcast.30), calls=%async_computation.5 | async-start | bytes 1769472 | tf_op jit(solution)/shard_map/all_to_all | solution.py:1101
  246.5 2.9 %line.5 = (f32[192,512]{1,0:T(8,128)}, bf16[192,512]{1,0:T(8,128)(2,1)}, bf16[192,512]{1,0:T(8,128)(2,1)}, bf16[192,512]{1,0:T(8,128)(2,1)}, f32[8,128]{1,0:T(8,128)}) custom-call(bf16[3072,512]{1,0:T(8,128)(2,1)} %bitcast.16.refs_1_.refs_0_.refs_2_.refs_3_, bf16[3072,512]{1,0:T(8,128)(2,1)} %bitcast.16.refs_1_.refs_0_.refs_2_.refs_3_, ...), custom_call_target="tpu_custom_call" | custom-call | flops 1 | bytes 1 | tf_op jit(solution)/shard_map/line/pallas_call | solution.py:57
  255.3 2.8 last.1
  258.1 3.2 %collective-permute-done.40.refs_3_ = bf16[192,512]{1,0:T(8,128)(2,1)} collective-permute-done((bf16[192,512]{1,0:T(8,128)(2,1)}, bf16[192,512]{1,0:T(8,128)(2,1)}, u32[]{:S(2)}, u32[]{:S(2)}) %collective-permute-start.40) | collective-permute-done | bytes 196640 | tf_op jit(solution)/shard_map/ppermute | solution.py:926
  263.3 5.4 %all-to-all-done.5 = bf16[4,864,128]{2,1,0:T(8,128)(2,1)} async-done(((bf16[4,864,128]{2,1,0:T(8,128)(2,1)}), bf16[4,864,128]{2,1,0:T(8,128)(2,1)}, u32[]{:S(2)}, u32[]{:S(2)}) %all-to-all-start.5) | async-done | bytes 884768 | tf_op jit(solution)/shard_map/all_to_all | solution.py:1101
  271.4 3.2 %all-to-all-start.6 = ((f32[32,1,128]{2,1,0:T(1,128)}), f32[32,1,128]{2,1,0:T(1,128)}, u32[]{:S(2)}, u32[]{:S(2)}) async-start(f32[32,1,128]{2,1,0:T(1,128)} %bitcast.36), calls=%async_computation.6 | async-start | bytes 32768 | tf_op jit(solution)/shard_map/all_to_all | solution.py:1133
  274.6 7.0 %all-to-all-done.6 = f32[32,1,128]{2,1,0:T(1,128)} async-done(((f32[32,1,128]{2,1,0:T(1,128)}), f32[32,1,128]{2,1,0:T(1,128)}, u32[]{:S(2)}, u32[]{:S(2)}) %all-to-all-start.6) | async-done | bytes 16416 | tf_op jit(solution)/shard_map/all_to_all | solution.py:1133
  281.6 6.3 %adam.1 = (f32[432,512]{1,0:T(8,128)}, f32[432,512]{1,0:T(8,128)}, f32[432,512]{1,0:T(8,128)}, f32[432,512]{1,0:T(8,128)}, f32[128,512]{1,0:T(8,128)}, /*index=5...) custom-call(s32[4]{0:T(128)} %pad_add_fusion.refs_0_, ...), custom_call_target="tpu_custom_call" | custom-call | flops 1 | bytes 1 | tf_op jit(solution)/shard_map/adam/pallas_call | solution.py:57
  (130 shorter events, 93.0 us)
Async XLA Ops:
  8.5 30.8 %all-to-all-start = ((bf16[4,880,128]{2,1,0:T(8,128)(2,1)}), bf16[4,880,128]{2,1,0:T(8,128)(2,1)}, u32[]{:S(2)}, u32[]{:S(2)}) async-start(bf16[4,880,128]{2,1,0:T(8,128)(2,1)} %bitcast.33), calls=%async_computation | async-start | bytes 1802240 | tf_op jit(solution)/shard_map/all_to_all | solution.py:1101
  15.4 14.7 %collective-permute-start.5 = (bf16[1760,128]{1,0:T(8,128)(2,1)}, bf16[1760,128]{1,0:T(8,128)(2,1)}, u32[]{:S(2)}, u32[]{:S(2)}) collective-permute-start(bf16[1760,128]{1,0:T(8,128)(2,1)} %get-tuple-element.164.refs_1_.refs_2_), channel_id=1, source_target_pairs={{0,8},{8,0},{1,9},{9,1},{2,10},{10,2},{3,11},{11,3},{4,12},{12,4},... | collective-permute-start | bytes 1351688 | tf_op jit(solution)/shard_map/ppermute | solution.py:926
  16.9 13.2 %collective-permute-start.6 = (bf16[1760,128]{1,0:T(8,128)(2,1)}, bf16[1760,128]{1,0:T(8,128)(2,1)}, u32[]{:S(2)}, u32[]{:S(2)}) collective-permute-start(bf16[1760,128]{1,0:T(8,128)(2,1)} %get-tuple-element.164.refs_1_.refs_2_), channel_id=1, source_target_pairs={{0,16},{16,0},{1,17},{17,1},{2,18},{18,2},{3,19},{19,3},{4,20},{20... | collective-permute-start | bytes 1351688 | tf_op jit(solution)/shard_map/ppermute | solution.py:926
  41.3 25.2 %all-to-all-start.1 = ((bf16[4,864,128]{2,1,0:T(8,128)(2,1)}), bf16[4,864,128]{2,1,0:T(8,128)(2,1)}, u32[]{:S(2)}, u32[]{:S(2)}) async-start(bf16[4,864,128]{2,1,0:T(8,128)(2,1)} %bitcast.31), calls=%async_computation.1 | async-start | bytes 1769472 | tf_op jit(solution)/shard_map/all_to_all | solution.py:1101
  46.1 15.1 %collective-permute-start.9 = (bf16[2640,128]{1,0:T(8,128)(2,1)}, bf16[2640,128]{1,0:T(8,128)(2,1)}, u32[]{:S(2)}, u32[]{:S(2)}) collective-permute-start(bf16[2640,128]{1,0:T(8,128)(2,1)} %get-tuple-element.185.refs_6_), channel_id=1, source_target_pairs={{0,8},{8,0},{1,9},{9,1},{2,10},{10,2},{3,11},{11,3},{4,12},{12,4},... | collective-permute-start | bytes 2027528 | tf_op jit(solution)/shard_map/ppermute | solution.py:926
  47.6 14.8 %collective-permute-start.10 = (bf16[2640,128]{1,0:T(8,128)(2,1)}, bf16[2640,128]{1,0:T(8,128)(2,1)}, u32[]{:S(2)}, u32[]{:S(2)}) collective-permute-start(bf16[2640,128]{1,0:T(8,128)(2,1)} %get-tuple-element.185.refs_6_), channel_id=1, source_target_pairs={{0,16},{16,0},{1,17},{17,1},{2,18},{18,2},{3,19},{19,3},{4,20},{20... | collective-permute-start | bytes 2027528 | tf_op jit(solution)/shard_map/ppermute | solution.py:926
  68.6 31.7 %all-to-all-start.2 = ((bf16[4,192,512]{2,1,0:T(8,128)(2,1)}), bf16[4,192,512]{2,1,0:T(8,128)(2,1)}, u32[]{:S(2)}, u32[]{:S(2)}) async-start(bf16[4,192,512]{2,1,0:T(8,128)(2,1)} %bitcast.32), calls=%async_computation.2 | async-start | bytes 1572864 | tf_op jit(solution)/shard_map/all_to_all | solution.py:1101
  72.8 16.2 %collective-permute-start.13 = (bf16[2592,128]{1,0:T(8,128)(2,1)}, bf16[2592,128]{1,0:T(8,128)(2,1)}, u32[]{:S(2)}, u32[]{:S(2)}) collective-permute-start(bf16[2592,128]{1,0:T(8,128)(2,1)} %get-tuple-element.192.refs_6_), channel_id=1, source_target_pairs={{0,8},{8,0},{1,9},{9,1},{2,10},{10,2},{3,11},{11,3},{4,12},{12,4},... | collective-permute-start | bytes 1990664 | tf_op jit(solution)/shard_map/ppermute | solution.py:926
  74.4 15.9 %collective-permute-start.14 = (bf16[2592,128]{1,0:T(8,128)(2,1)}, bf16[2592,128]{1,0:T(8,128)(2,1)}, u32[]{:S(2)}, u32[]{:S(2)}) collective-permute-start(bf16[2592,128]{1,0:T(8,128)(2,1)} %get-tuple-element.192.refs_6_), channel_id=1, source_target_pairs={{0,16},{16,0},{1,17},{17,1},{2,18},{18,2},{3,19},{19,3},{4,20},{20... | collective-permute-start | bytes 1990664 | tf_op jit(solution)/shard_map/ppermute | solution.py:926
  100.4 16.6 %collective-permute-start.18 = (bf16[768,512]{1,0:T(8,128)(2,1)}, bf16[768,512]{1,0:T(8,128)(2,1)}, u32[]{:S(2)}, u32[]{:S(2)}) collective-permute-start(bf16[768,512]{1,0:T(8,128)(2,1)} %get-tuple-element.205), channel_id=1, source_target_pairs={{0,8},{8,0},{1,9},{9,1},{2,10},{10,2},{3,11},{11,3},{4,12},{12,4},... | collective-permute-start | bytes 2359304 | tf_op jit(solution)/shard_map/ppermute | solution.py:926
  101.8 16.1 %collective-permute-start.19 = (bf16[768,512]{1,0:T(8,128)(2,1)}, bf16[768,512]{1,0:T(8,128)(2,1)}, u32[]{:S(2)}, u32[]{:S(2)}) collective-permute-start(bf16[768,512]{1,0:T(8,128)(2,1)} %get-tuple-element.205), channel_id=1, source_target_pairs={{0,16},{16,0},{1,17},{17,1},{2,18},{18,2},{3,19},{19,3},{4,20},{20... | collective-permute-start | bytes 2359304 | tf_op jit(solution)/shard_map/ppermute | solution.py:926
  145.3 74.5 %all-to-all-start.3 = ((bf16[4,768,512]{2,1,0:T(8,128)(2,1)}), bf16[4,768,512]{2,1,0:T(8,128)(2,1)}, u32[]{:S(2)}, u32[]{:S(2)}) async-start(bf16[4,768,512]{2,1,0:T(8,128)(2,1)} %bitcast.29), calls=%async_computation.3 | async-start | bytes 6291456 | tf_op jit(solution)/shard_map/all_to_all | solution.py:1101
  166.9 13.3 %collective-permute-start.26 = (bf16[1728,128]{1,0:T(8,128)(2,1)}, bf16[1728,128]{1,0:T(8,128)(2,1)}, u32[]{:S(2)}, u32[]{:S(2)}) collective-permute-start(bf16[1728,128]{1,0:T(8,128)(2,1)} %get-tuple-element.225), channel_id=1, source_target_pairs={{0,8},{8,0},{1,9},{9,1},{2,10},{10,2},{3,11},{11,3},{4,12},{12,4},... | collective-permute-start | bytes 1327112 | tf_op jit(solution)/shard_map/ppermute | solution.py:926
  168.4 12.3 %collective-permute-start.27 = (bf16[1728,128]{1,0:T(8,128)(2,1)}, bf16[1728,128]{1,0:T(8,128)(2,1)}, u32[]{:S(2)}, u32[]{:S(2)}) collective-permute-start(bf16[1728,128]{1,0:T(8,128)(2,1)} %get-tuple-element.226), channel_id=1, source_target_pairs={{0,16},{16,0},{1,17},{17,1},{2,18},{18,2},{3,19},{19,3},{4,20},{20... | collective-permute-start | bytes 1327112 | tf_op jit(solution)/shard_map/ppermute | solution.py:926
  178.4 17.5 %collective-permute-start.30 = (bf16[1728,128]{1,0:T(8,128)(2,1)}, bf16[1728,128]{1,0:T(8,128)(2,1)}, u32[]{:S(2)}, u32[]{:S(2)}) collective-permute-start(bf16[1728,128]{1,0:T(8,128)(2,1)} %get-tuple-element.239), channel_id=1, source_target_pairs={{0,8},{8,0},{1,9},{9,1},{2,10},{10,2},{3,11},{11,3},{4,12},{12,4},... | collective-permute-start | bytes 1327112 | tf_op jit(solution)/shard_map/ppermute | solution.py:926
  179.0 16.9 %collective-permute-start.31 = (bf16[1728,128]{1,0:T(8,128)(2,1)}, bf16[1728,128]{1,0:T(8,128)(2,1)}, u32[]{:S(2)}, u32[]{:S(2)}) collective-permute-start(bf16[1728,128]{1,0:T(8,128)(2,1)} %get-tuple-element.240), channel_id=1, source_target_pairs={{0,16},{16,0},{1,17},{17,1},{2,18},{18,2},{3,19},{19,3},{4,20},{20... | collective-permute-start | bytes 1327112 | tf_op jit(solution)/shard_map/ppermute | solution.py:926
  183.0 29.5 %collective-permute-start.28 = (bf16[3456,128]{1,0:T(8,128)(2,1)}, bf16[3456,128]{1,0:T(8,128)(2,1)}, u32[]{:S(2)}, u32[]{:S(2)}) collective-permute-start(bf16[3456,128]{1,0:T(8,128)(2,1)} %get-tuple-element.229), channel_id=1, source_target_pairs={{0,8},{8,0},{1,9},{9,1},{2,10},{10,2},{3,11},{11,3},{4,12},{12,4},... | collective-permute-start | bytes 2654216 | tf_op jit(solution)/shard_map/ppermute | solution.py:926
  184.0 28.6 %collective-permute-start.29 = (bf16[3456,128]{1,0:T(8,128)(2,1)}, bf16[3456,128]{1,0:T(8,128)(2,1)}, u32[]{:S(2)}, u32[]{:S(2)}) collective-permute-start(bf16[3456,128]{1,0:T(8,128)(2,1)} %get-tuple-element.230), channel_id=1, source_target_pairs={{0,16},{16,0},{1,17},{17,1},{2,18},{18,2},{3,19},{19,3},{4,20},{20... | collective-permute-start | bytes 2654216 | tf_op jit(solution)/shard_map/ppermute | solution.py:926
  198.3 30.1 %collective-permute-start.35 = (bf16[3456,128]{1,0:T(8,128)(2,1)}, bf16[3456,128]{1,0:T(8,128)(2,1)}, u32[]{:S(2)}, u32[]{:S(2)}) collective-permute-start(bf16[3456,128]{1,0:T(8,128)(2,1)} %get-tuple-element.253), channel_id=1, source_target_pairs={{0,8},{8,0},{1,9},{9,1},{2,10},{10,2},{3,11},{11,3},{4,12},{12,4},... | collective-permute-start | bytes 2654216 | tf_op jit(solution)/shard_map/ppermute | solution.py:926
  199.4 29.3 %collective-permute-start.36 = (bf16[3456,128]{1,0:T(8,128)(2,1)}, bf16[3456,128]{1,0:T(8,128)(2,1)}, u32[]{:S(2)}, u32[]{:S(2)}) collective-permute-start(bf16[3456,128]{1,0:T(8,128)(2,1)} %get-tuple-element.254), channel_id=1, source_target_pairs={{0,16},{16,0},{1,17},{17,1},{2,18},{18,2},{3,19},{19,3},{4,20},{20... | collective-permute-start | bytes 2654216 | tf_op jit(solution)/shard_map/ppermute | solution.py:926
  215.4 24.1 %collective-permute-start.32 = (bf16[864,128]{1,0:T(8,128)(2,1)}, bf16[864,128]{1,0:T(8,128)(2,1)}, u32[]{:S(2)}, u32[]{:S(2)}) collective-permute-start(bf16[864,128]{1,0:T(8,128)(2,1)} %get-tuple-element.245), channel_id=1, source_target_pairs={{0,2},{2,0},{4,6},{6,4},{1,3},{3,1},{5,7},{7,5},{8,10},{10,8},{12,... | collective-permute-start | bytes 663560 | tf_op jit(solution)/shard_map/ppermute | solution.py:926
  217.4 22.1 %collective-permute-start.33 = (bf16[864,128]{1,0:T(8,128)(2,1)}, bf16[864,128]{1,0:T(8,128)(2,1)}, u32[]{:S(2)}, u32[]{:S(2)}) collective-permute-start(bf16[864,128]{1,0:T(8,128)(2,1)} %get-tuple-element.246), channel_id=1, source_target_pairs={{0,4},{2,6},{4,0},{6,2},{1,5},{3,7},{5,1},{7,3},{8,12},{10,14},{12... | collective-permute-start | bytes 663560 | tf_op jit(solution)/shard_map/ppermute | solution.py:926
  219.7 19.8 %collective-permute-start.34 = (bf16[864,128]{1,0:T(8,128)(2,1)}, bf16[864,128]{1,0:T(8,128)(2,1)}, u32[]{:S(2)}, u32[]{:S(2)}) collective-permute-start(bf16[864,128]{1,0:T(8,128)(2,1)} %get-tuple-element.247), channel_id=1, source_target_pairs={{0,6},{2,4},{4,2},{6,0},{1,7},{3,5},{5,3},{7,1},{8,14},{10,12},{12... | collective-permute-start | bytes 663560 | tf_op jit(solution)/shard_map/ppermute | solution.py:926
  219.8 19.7 %all-to-all-start.4 = ((f32[32,1,128]{2,1,0:T(1,128)}), f32[32,1,128]{2,1,0:T(1,128)}, u32[]{:S(2)}, u32[]{:S(2)}) async-start(f32[32,1,128]{2,1,0:T(1,128)} %bitcast.35), calls=%async_computation.4 | async-start | bytes 32768 | tf_op jit(solution)/shard_map/all_to_all | solution.py:1133
  241.7 27.0 %all-to-all-start.5 = ((bf16[4,864,128]{2,1,0:T(8,128)(2,1)}), bf16[4,864,128]{2,1,0:T(8,128)(2,1)}, u32[]{:S(2)}, u32[]{:S(2)}) async-start(bf16[4,864,128]{2,1,0:T(8,128)(2,1)} %bitcast.30), calls=%async_computation.5 | async-start | bytes 1769472 | tf_op jit(solution)/shard_map/all_to_all | solution.py:1101
  246.0 9.3 %collective-permute-start.38 = (f32[512,256]{1,0:T(8,128)}, f32[512,256]{1,0:T(8,128)}, u32[]{:S(2)}, u32[]{:S(2)}) collective-permute-start(f32[512,256]{1,0:T(8,128)} %get-tuple-element.267), channel_id=1, source_target_pairs={{0,1},{1,0},{2,3},{3,2},{4,5},{5,4},{6,7},{7,6},{8,9},{9,8},{10,11... | collective-permute-start | bytes 1572872 | tf_op jit(solution)/shard_map/ppermute | solution.py:926
  249.4 8.7 %collective-permute-start.39 = (bf16[192,512]{1,0:T(8,128)(2,1)}, bf16[192,512]{1,0:T(8,128)(2,1)}, u32[]{:S(2)}, u32[]{:S(2)}) collective-permute-start(bf16[192,512]{1,0:T(8,128)(2,1)} %get-tuple-element.272), channel_id=1, source_target_pairs={{0,8},{8,0},{1,9},{9,1},{2,10},{10,2},{3,11},{11,3},{4,12},{12,4},... | collective-permute-start | bytes 589832 | tf_op jit(solution)/shard_map/ppermute | solution.py:926
  250.1 11.1 %collective-permute-start.40 = (bf16[192,512]{1,0:T(8,128)(2,1)}, bf16[192,512]{1,0:T(8,128)(2,1)}, u32[]{:S(2)}, u32[]{:S(2)}) collective-permute-start(bf16[192,512]{1,0:T(8,128)(2,1)} %get-tuple-element.273), channel_id=1, source_target_pairs={{0,16},{16,0},{1,17},{17,1},{2,18},{18,2},{3,19},{19,3},{4,20},{20... | collective-permute-start | bytes 589832 | tf_op jit(solution)/shard_map/ppermute | solution.py:926
  251.1 10.1 %collective-permute-start.41 = (bf16[192,512]{1,0:T(8,128)(2,1)}, bf16[192,512]{1,0:T(8,128)(2,1)}, u32[]{:S(2)}, u32[]{:S(2)}) collective-permute-start(bf16[192,512]{1,0:T(8,128)(2,1)} %get-tuple-element.274), channel_id=1, source_target_pairs={{0,24},{8,16},{16,8},{24,0},{1,25},{9,17},{17,9},{25,1},{2,26},{10... | collective-permute-start | bytes 589832 | tf_op jit(solution)/shard_map/ppermute | solution.py:1118
  252.9 21.7 %collective-permute-start.42 = (f32[432,128]{1,0:T(8,128)}, f32[432,128]{1,0:T(8,128)}, u32[]{:S(2)}, u32[]{:S(2)}) collective-permute-start(f32[432,128]{1,0:T(8,128)} %get-tuple-element.282), channel_id=1, source_target_pairs={{0,1},{1,0},{2,3},{3,2},{4,5},{5,4},{6,7},{7,6},{8,9},{9,8},{10,11... | collective-permute-start | bytes 663560 | tf_op jit(solution)/shard_map/ppermute | solution.py:926
  270.9 10.7 %collective-permute-start.43 = (f32[432,128]{1,0:T(8,128)}, f32[432,128]{1,0:T(8,128)}, u32[]{:S(2)}, u32[]{:S(2)}) collective-permute-start(f32[432,128]{1,0:T(8,128)} %get-tuple-element.283), channel_id=1, source_target_pairs={{0,1},{1,0},{2,3},{3,2},{4,5},{5,4},{6,7},{7,6},{8,9},{9,8},{10,11... | collective-permute-start | bytes 663560 | tf_op jit(solution)/shard_map/ppermute | solution.py:926
  271.4 10.2 %all-to-all-start.6 = ((f32[32,1,128]{2,1,0:T(1,128)}), f32[32,1,128]{2,1,0:T(1,128)}, u32[]{:S(2)}, u32[]{:S(2)}) async-start(f32[32,1,128]{2,1,0:T(1,128)} %bitcast.36), calls=%async_computation.6 | async-start | bytes 32768 | tf_op jit(solution)/shard_map/all_to_all | solution.py:1133
  (23 other events, 112.4 us)

commit v3 on v2

--- a/solution.py
+++ b/solution.py
@@ -1160,7 +1160,7 @@
     gains = next(weights)
     tokens = hat_tokens = normed_call(chain, spot, inputs, source_other)
     blocks = taps.shape[0]
-    cuts, spread = (0, blocks * 2 // 9, blocks // 3, blocks), None
+    cuts, spread = (0, blocks // 9, blocks * 2 // 9, blocks), None
     for at in range(3):
         spread = spread_call(chain, sums, taps_turned, *tokens, cuts[at], cuts[at + 1] - cuts[at], spread)
         sides = next(weights)

time: 290 us -> 289 us (level)
  waiting for transfers between devices: 57.9 us -> 52.5 us
  starting transfers between devices: 67.6 us -> 72.3 us
    ppermute x44, waiting for transfers between devices: 36.7 us -> 31.4 us  [flip(): return lax.ppermute(v, axis, [(i, i ^ bits) for i in range(size)])]
    ppermute x44, starting transfers between devices: 33.3 us -> 38.3 us  [flip(): return lax.ppermute(v, axis, [(i, i ^ bits) for i in range(size)])]
  transfers between devices with their start and end apart: 52 -> 52, of which waited for: 25 -> 27; matrix products, arithmetic and copies ran while one was open for 1% -> 1% of each run, Pallas kernels for 44% -> 44%
where the time goes in v3:
time: 289 us; the launch traced here: 287 us
  Pallas kernels  157 us (54%)
  starting transfers between devices  72.3 us (25%)
  waiting for transfers between devices  52.5 us (18%)
    pallas_call x40, Pallas kernels, call(): pl.pallas_call(whole, name=name, in_specs=list(in_specs) + [anywhere() fo...  157 us
    ppermute x44, starting transfers between devices, flip(): return lax.ppermute(v, axis, [(i, i ^ bits) for i in range(size)])  38.3 us
    ppermute x44, waiting for transfers between devices, flip(): return lax.ppermute(v, axis, [(i, i ^ bits) for i in range(size)])  31.4 us
    all_to_all x5, starting transfers between devices, along_z(): return lax.all_to_all(v, 'z', 0, 0, tiled=True)  24.9 us
    all_to_all x2, waiting for transfers between devices, everyone(): return lax.all_to_all(rows, EVERY, 0, 0, tiled=True)  14.8 us
    all_to_all x2, starting transfers between devices, everyone(): return lax.all_to_all(rows, EVERY, 0, 0, tiled=True)  7.74 us
  transfers between devices with their start and end apart: 52, of which 27 were waited for; matrix products, arithmetic and copies ran while one was open for 1% of the time, Pallas kernels for 44%

profile of v3, /device:TPU:0, one launch (start us, length us, event | category | flops | bytes accessed | tf_op | source)
XLA Modules:
  0.0 287.4 jit_solution(2793776789069969272)
XLA Ops:
  8.5 6.2 %all-to-all-start = ((bf16[4,880,128]{2,1,0:T(8,128)(2,1)}), bf16[4,880,128]{2,1,0:T(8,128)(2,1)}, u32[]{:S(2)}, u32[]{:S(2)}) async-start(bf16[4,880,128]{2,1,0:T(8,128)(2,1)} %bitcast.33), calls=%async_computation | async-start | bytes 1802240 | tf_op jit(solution)/shard_map/all_to_all | solution.py:1101
  24.6 4.1 %spread.3 = (bf16[2,1024,3456]{2,1,0:T(8,128)(2,1)}, f32[8,128]{1,0:T(8,128)}) custom-call(s32[1,3]{1,0:T(1,128)} %refs_1_.9, s32[1,3]{1,0:T(1,128)} %collective-permute-done.refs_5_.refs_1_.refs_2_, f32[9,3,512]{2,1,0:T(4,128)} %reshape.69.refs_2_, bf16[512,256]{1,0:T(8,128)(2,1)} %get-tuple-element.169.refs_3_.refs_10_, ...), custom_call_target="tpu_custom_call" | custom-call | flops 1 | bytes 1 | tf_op jit(solution)/shard_map/spread/pallas_call | solution.py:57
  33.0 4.0 %spread.4 = (bf16[2,1024,3456]{2,1,0:T(8,128)(2,1)}, f32[8,128]{1,0:T(8,128)}) custom-call(s32[1,3]{1,0:T(1,128)} %refs_1_.9, s32[1,3]{1,0:T(1,128)} %collective-permute-done.refs_5_.refs_1_.refs_2_, f32[9,3,512]{2,1,0:T(4,128)} %reshape.69.refs_2_, bf16[512,256]{1,0:T(8,128)(2,1)} %get-tuple-element.169.refs_3_.refs_10_, ...), custom_call_target="tpu_custom_call", output_to_operand_aliasing={{0}: (5, {})} | custom-call | flops 1 | bytes 1 | tf_op jit(solution)/shard_map/spread/pallas_call | solution.py:57
  40.0 4.8 %all-to-all-start.1 = ((bf16[4,864,128]{2,1,0:T(8,128)(2,1)}), bf16[4,864,128]{2,1,0:T(8,128)(2,1)}, u32[]{:S(2)}, u32[]{:S(2)}) async-start(bf16[4,864,128]{2,1,0:T(8,128)(2,1)} %bitcast.31), calls=%async_computation.1 | async-start | bytes 1769472 | tf_op jit(solution)/shard_map/all_to_all | solution.py:1101
  47.7 12.6 %spread.5 = (bf16[2,1024,3456]{2,1,0:T(8,128)(2,1)}, f32[8,128]{1,0:T(8,128)}) custom-call(s32[1,3]{1,0:T(1,128)} %refs_1_.9, s32[1,3]{1,0:T(1,128)} %collective-permute-done.refs_5_.refs_1_.refs_2_, f32[9,3,512]{2,1,0:T(4,128)} %reshape.69.refs_2_, bf16[512,256]{1,0:T(8,128)(2,1)} %get-tuple-element.169.refs_3_.refs_10_, ...), custom_call_target="tpu_custom_call", output_to_operand_aliasing={{0}: (5, {})} | custom-call | flops 1 | bytes 1 | tf_op jit(solution)/shard_map/spread/pallas_call | solution.py:57
  68.1 4.7 %all-to-all-start.2 = ((bf16[4,192,512]{2,1,0:T(8,128)(2,1)}), bf16[4,192,512]{2,1,0:T(8,128)(2,1)}, u32[]{:S(2)}, u32[]{:S(2)}) async-start(bf16[4,192,512]{2,1,0:T(8,128)(2,1)} %bitcast.32), calls=%async_computation.2 | async-start | bytes 1572864 | tf_op jit(solution)/shard_map/all_to_all | solution.py:1101
  75.2 10.7 %mix.2 = (f32[512,512]{1,0:T(8,128)}, f32[512,512]{1,0:T(8,128)}, bf16[13824,128]{1,0:T(8,128)(2,1)}, f32[16,512]{1,0:T(8,128)}, f32[8,128]{1,0:T(8,128)}) custom-call(s32[4]{0:T(128)} %pad_add_fusion.refs_0_, bf16[2,1024,3456]{2,1,0:T(8,128)(2,1)} %get-tuple-element.182.refs_1_.refs_4_, bf16[1760,128]{1,0:T(8,128)(2,1)} %get-tuple-element.164.refs_1_.refs_2_, ...), custom_call_target="tpu_custom_call" | custom-call | flops 1 | bytes 1 | tf_op jit(solution)/shard_map/mix/pallas_call | solution.py:57
  85.9 2.4 collective-permute-done.13.refs_0_.refs_7_
  93.6 5.4 %collective-permute-done.15.refs_1_.refs_9_ = bf16[1296,128]{1,0:T(8,128)(2,1)} collective-permute-done((bf16[1296,128]{1,0:T(8,128)(2,1)}, bf16[1296,128]{1,0:T(8,128)(2,1)}, u32[]{:S(2)}, u32[]{:S(2)}) %collective-permute-start.15) | collective-permute-done | bytes 331808 | tf_op jit(solution)/shard_map/ppermute | solution.py:926
  102.7 11.5 %mix.3 = (f32[512,512]{1,0:T(8,128)}, bf16[512,512]{1,0:T(8,128)(2,1)}, bf16[13824,128]{1,0:T(8,128)(2,1)}, f32[8,128]{1,0:T(8,128)}) custom-call(s32[4]{0:T(128)} %pad_add_fusion.refs_0_, bf16[2,1024,3456]{2,1,0:T(8,128)(2,1)} %get-tuple-element.182.refs_1_.refs_4_, bf16[1760,128]{1,0:T(8,128)(2,1)} %get-tuple-element.164.refs_1_.refs_2_, ...), custom_call_target="tpu_custom_call" | custom-call | flops 1 | bytes 1 | tf_op jit(solution)/shard_map/mix/pallas_call | solution.py:57
  121.5 2.5 hidden.1
  128.4 16.5 %ffn.1 = (f32[512,512]{1,0:T(8,128)}, bf16[512,512]{1,0:T(8,128)(2,1)}, f32[512,512]{1,0:T(8,128)}, bf16[512,512]{1,0:T(8,128)(2,1)}, bf16[16,192,512]{2,1,0:T(8,128)(2,1)}, /*index=5*/f32[8,128]{1,0:T(8,128)}) custom-call(s32[4]{0:T(128)} %pad_add_fusion.refs_0_, s32[1,3]{1,0:T(1,128)} %refs_1_.9, s32[1,3]{1,0:T(1,128)} %collective-permute-done.refs_5_.refs_1_.refs_2_, ...), custom_call_target="tpu_custom_call" | custom-call | flops 1 | bytes 1 | tf_op jit(solution)/shard_map/ffn/pallas_call | solution.py:57
  144.9 5.0 %all-to-all-start.3 = ((bf16[4,768,512]{2,1,0:T(8,128)(2,1)}), bf16[4,768,512]{2,1,0:T(8,128)(2,1)}, u32[]{:S(2)}, u32[]{:S(2)}) async-start(bf16[4,768,512]{2,1,0:T(8,128)(2,1)} %bitcast.29), calls=%async_computation.3 | async-start | bytes 6291456 | tf_op jit(solution)/shard_map/all_to_all | solution.py:1101
  152.1 3.1 %turn.1 = (f32[512,512]{1,0:T(8,128)}, bf16[512,512]{1,0:T(8,128)(2,1)}, f32[1,512]{1,0:T(1,128)}, f32[8,128]{1,0:T(8,128)}) custom-call(s32[1,3]{1,0:T(1,128)} %refs_1_.9, f32[512,512]{1,0:T(8,128)} %get-tuple-element.208.refs_1_.refs_0_, bf16[512,512]{1,0:T(8,128)(2,1)} %refs_2_.5, f32[512,512]{1,0:T(8,128)} %get-tuple-element.215.refs_3_, ...), custom_call_target="tpu_custom_call" | custom-call | flops 1 | bytes 1 | tf_op jit(solution)/shard_map/turn/pallas_call | solution.py:57
  157.5 9.1 %mixer_grad.2 = (bf16[3456,128]{1,0:T(8,128)(2,1)}, bf16[3456,128]{1,0:T(8,128)(2,1)}, bf16[3456,128]{1,0:T(8,128)(2,1)}, bf16[1728,128]{1,0:T(8,128)(2,1)}, bf1...) custom-call(s32[4]{0:T(128)} %pad_add_fusion.refs_0_, f32[16,512]{1,0:T(8,128)} %get-tuple-element.199.refs_13_.refs_3_.refs_5_.refs_1_, ...), custom_call_target="tpu_custom_call" | custom-call | flops 1 | bytes 1 | tf_op jit(solution)/shard_map/mixer_grad/pallas_call | solution.py:57
  169.2 9.1 %mixer_grad.3 = (bf16[3456,128]{1,0:T(8,128)(2,1)}, bf16[3456,128]{1,0:T(8,128)(2,1)}, bf16[3456,128]{1,0:T(8,128)(2,1)}, bf16[1728,128]{1,0:T(8,128)(2,1)}, bf1...) custom-call(s32[4]{0:T(128)} %pad_add_fusion.refs_0_, f32[16,512]{1,0:T(8,128)} %get-tuple-element.199.refs_13_.refs_3_.refs_5_.refs_1_, ...), custom_call_target="tpu_custom_call" | custom-call | flops 1 | bytes 1 | tf_op jit(solution)/shard_map/mixer_grad/pallas_call | solution.py:57
  186.2 9.5 %spread_back.2 = (f32[512,256]{1,0:T(8,128)}, f32[512,256]{1,0:T(8,128)}, f32[8,128]{1,0:T(8,128)}) custom-call(s32[4]{0:T(128)} %pad_add_fusion.refs_0_, s32[1,3]{1,0:T(1,128)} %refs_1_.9, s32[1,3]{1,0:T(1,128)} %collective-permute-done.refs_5_.refs_1_.refs_2_, f32[9,3,512]{2,1,0:T(4,128)} %reshape.75.refs_3_, ...), custom_call_target="tpu_custom_call" | custom-call | flops 1 | bytes 1 | tf_op jit(solution)/shard_map/spread_back/pallas_call | solution.py:57
  195.7 2.4 near.3
  200.2 12.1 %spread_back.3 = (f32[512,256]{1,0:T(8,128)}, f32[512,256]{1,0:T(8,128)}, f32[1,256]{1,0:T(1,128)}, f32[32,128]{1,0:T(8,128)}, f32[8,128]{1,0:T(8,128)}) custom-call(s32[4]{0:T(128)} %pad_add_fusion.refs_0_, s32[1,3]{1,0:T(1,128)} %refs_1_.9, s32[1,3]{1,0:T(1,128)} %collective-permute-done.refs_5_.refs_1_.refs_2_, f32[9,3,512]{2,1,0:T(4,128)} %reshape.75.refs_3_, ...), custom_call_target="tpu_custom_call" | custom-call | flops 1 | bytes 1 | tf_op jit(solution)/shard_map/spread_back/pallas_call | solution.py:57
  212.3 2.8 line.3
  219.7 4.6 %all-to-all-start.4 = ((f32[32,1,128]{2,1,0:T(1,128)}), f32[32,1,128]{2,1,0:T(1,128)}, u32[]{:S(2)}, u32[]{:S(2)}) async-start(f32[32,1,128]{2,1,0:T(1,128)} %bitcast.35), calls=%async_computation.4 | async-start | bytes 32768 | tf_op jit(solution)/shard_map/all_to_all | solution.py:1133
  224.3 3.9 %collective-permute-done.35.refs_1_ = bf16[3456,128]{1,0:T(8,128)(2,1)} collective-permute-done((bf16[3456,128]{1,0:T(8,128)(2,1)}, bf16[3456,128]{1,0:T(8,128)(2,1)}, u32[]{:S(2)}, u32[]{:S(2)}) %collective-permute-start.35) | collective-permute-done | bytes 884768 | tf_op jit(solution)/shard_map/ppermute | solution.py:926
  228.7 2.6 line.4
  231.3 7.8 %all-to-all-done.4 = f32[32,1,128]{2,1,0:T(1,128)} async-done(((f32[32,1,128]{2,1,0:T(1,128)}), f32[32,1,128]{2,1,0:T(1,128)}, u32[]{:S(2)}, u32[]{:S(2)}) %all-to-all-start.4) | async-done | bytes 16416 | tf_op jit(solution)/shard_map/all_to_all | solution.py:1133
  241.2 4.2 %all-to-all-start.5 = ((bf16[4,864,128]{2,1,0:T(8,128)(2,1)}), bf16[4,864,128]{2,1,0:T(8,128)(2,1)}, u32[]{:S(2)}, u32[]{:S(2)}) async-start(bf16[4,864,128]{2,1,0:T(8,128)(2,1)} %bitcast.30), calls=%async_computation.5 | async-start | bytes 1769472 | tf_op jit(solution)/shard_map/all_to_all | solution.py:1101
  246.1 2.9 %line.5 = (f32[192,512]{1,0:T(8,128)}, bf16[192,512]{1,0:T(8,128)(2,1)}, bf16[192,512]{1,0:T(8,128)(2,1)}, bf16[192,512]{1,0:T(8,128)(2,1)}, f32[8,128]{1,0:T(8,128)}) custom-call(bf16[3072,512]{1,0:T(8,128)(2,1)} %bitcast.16.refs_1_.refs_0_.refs_2_.refs_3_, bf16[3072,512]{1,0:T(8,128)(2,1)} %bitcast.16.refs_1_.refs_0_.refs_2_.refs_3_, ...), custom_call_target="tpu_custom_call" | custom-call | flops 1 | bytes 1 | tf_op jit(solution)/shard_map/line/pallas_call | solution.py:57
  252.4 2.4 output.1
  254.9 2.8 last.1
  263.3 4.6 %all-to-all-done.5 = bf16[4,864,128]{2,1,0:T(8,128)(2,1)} async-done(((bf16[4,864,128]{2,1,0:T(8,128)(2,1)}), bf16[4,864,128]{2,1,0:T(8,128)(2,1)}, u32[]{:S(2)}, u32[]{:S(2)}) %all-to-all-start.5) | async-done | bytes 884768 | tf_op jit(solution)/shard_map/all_to_all | solution.py:1101
  270.6 3.2 %all-to-all-start.6 = ((f32[32,1,128]{2,1,0:T(1,128)}), f32[32,1,128]{2,1,0:T(1,128)}, u32[]{:S(2)}, u32[]{:S(2)}) async-start(f32[32,1,128]{2,1,0:T(1,128)} %bitcast.36), calls=%async_computation.6 | async-start | bytes 32768 | tf_op jit(solution)/shard_map/all_to_all | solution.py:1133
  273.8 7.0 %all-to-all-done.6 = f32[32,1,128]{2,1,0:T(1,128)} async-done(((f32[32,1,128]{2,1,0:T(1,128)}), f32[32,1,128]{2,1,0:T(1,128)}, u32[]{:S(2)}, u32[]{:S(2)}) %all-to-all-start.6) | async-done | bytes 16416 | tf_op jit(solution)/shard_map/all_to_all | solution.py:1133
  280.9 6.3 %adam.1 = (f32[432,512]{1,0:T(8,128)}, f32[432,512]{1,0:T(8,128)}, f32[432,512]{1,0:T(8,128)}, f32[432,512]{1,0:T(8,128)}, f32[128,512]{1,0:T(8,128)}, /*index=5...) custom-call(s32[4]{0:T(128)} %pad_add_fusion.refs_0_, ...), custom_call_target="tpu_custom_call" | custom-call | flops 1 | bytes 1 | tf_op jit(solution)/shard_map/adam/pallas_call | solution.py:57
  (130 shorter events, 95.4 us)
Async XLA Ops:
  8.5 29.4 %all-to-all-start = ((bf16[4,880,128]{2,1,0:T(8,128)(2,1)}), bf16[4,880,128]{2,1,0:T(8,128)(2,1)}, u32[]{:S(2)}, u32[]{:S(2)}) async-start(bf16[4,880,128]{2,1,0:T(8,128)(2,1)} %bitcast.33), calls=%async_computation | async-start | bytes 1802240 | tf_op jit(solution)/shard_map/all_to_all | solution.py:1101
  15.4 13.3 %collective-permute-start.5 = (bf16[1760,128]{1,0:T(8,128)(2,1)}, bf16[1760,128]{1,0:T(8,128)(2,1)}, u32[]{:S(2)}, u32[]{:S(2)}) collective-permute-start(bf16[1760,128]{1,0:T(8,128)(2,1)} %get-tuple-element.164.refs_1_.refs_2_), channel_id=1, source_target_pairs={{0,8},{8,0},{1,9},{9,1},{2,10},{10,2},{3,11},{11,3},{4,12},{12,4},... | collective-permute-start | bytes 1351688 | tf_op jit(solution)/shard_map/ppermute | solution.py:926
  16.9 12.2 %collective-permute-start.6 = (bf16[1760,128]{1,0:T(8,128)(2,1)}, bf16[1760,128]{1,0:T(8,128)(2,1)}, u32[]{:S(2)}, u32[]{:S(2)}) collective-permute-start(bf16[1760,128]{1,0:T(8,128)(2,1)} %get-tuple-element.164.refs_1_.refs_2_), channel_id=1, source_target_pairs={{0,16},{16,0},{1,17},{17,1},{2,18},{18,2},{3,19},{19,3},{4,20},{20... | collective-permute-start | bytes 1351688 | tf_op jit(solution)/shard_map/ppermute | solution.py:926
  40.0 26.0 %all-to-all-start.1 = ((bf16[4,864,128]{2,1,0:T(8,128)(2,1)}), bf16[4,864,128]{2,1,0:T(8,128)(2,1)}, u32[]{:S(2)}, u32[]{:S(2)}) async-start(bf16[4,864,128]{2,1,0:T(8,128)(2,1)} %bitcast.31), calls=%async_computation.1 | async-start | bytes 1769472 | tf_op jit(solution)/shard_map/all_to_all | solution.py:1101
  44.8 15.8 %collective-permute-start.9 = (bf16[2640,128]{1,0:T(8,128)(2,1)}, bf16[2640,128]{1,0:T(8,128)(2,1)}, u32[]{:S(2)}, u32[]{:S(2)}) collective-permute-start(bf16[2640,128]{1,0:T(8,128)(2,1)} %get-tuple-element.185.refs_6_), channel_id=1, source_target_pairs={{0,8},{8,0},{1,9},{9,1},{2,10},{10,2},{3,11},{11,3},{4,12},{12,4},... | collective-permute-start | bytes 2027528 | tf_op jit(solution)/shard_map/ppermute | solution.py:926
  46.3 15.5 %collective-permute-start.10 = (bf16[2640,128]{1,0:T(8,128)(2,1)}, bf16[2640,128]{1,0:T(8,128)(2,1)}, u32[]{:S(2)}, u32[]{:S(2)}) collective-permute-start(bf16[2640,128]{1,0:T(8,128)(2,1)} %get-tuple-element.185.refs_6_), channel_id=1, source_target_pairs={{0,16},{16,0},{1,17},{17,1},{2,18},{18,2},{3,19},{19,3},{4,20},{20... | collective-permute-start | bytes 2027528 | tf_op jit(solution)/shard_map/ppermute | solution.py:926
  68.1 31.4 %all-to-all-start.2 = ((bf16[4,192,512]{2,1,0:T(8,128)(2,1)}), bf16[4,192,512]{2,1,0:T(8,128)(2,1)}, u32[]{:S(2)}, u32[]{:S(2)}) async-start(bf16[4,192,512]{2,1,0:T(8,128)(2,1)} %bitcast.32), calls=%async_computation.2 | async-start | bytes 1572864 | tf_op jit(solution)/shard_map/all_to_all | solution.py:1101
  72.8 15.6 %collective-permute-start.13 = (bf16[2592,128]{1,0:T(8,128)(2,1)}, bf16[2592,128]{1,0:T(8,128)(2,1)}, u32[]{:S(2)}, u32[]{:S(2)}) collective-permute-start(bf16[2592,128]{1,0:T(8,128)(2,1)} %get-tuple-element.192.refs_6_), channel_id=1, source_target_pairs={{0,8},{8,0},{1,9},{9,1},{2,10},{10,2},{3,11},{11,3},{4,12},{12,4},... | collective-permute-start | bytes 1990664 | tf_op jit(solution)/shard_map/ppermute | solution.py:926
  74.4 15.2 %collective-permute-start.14 = (bf16[2592,128]{1,0:T(8,128)(2,1)}, bf16[2592,128]{1,0:T(8,128)(2,1)}, u32[]{:S(2)}, u32[]{:S(2)}) collective-permute-start(bf16[2592,128]{1,0:T(8,128)(2,1)} %get-tuple-element.192.refs_6_), channel_id=1, source_target_pairs={{0,16},{16,0},{1,17},{17,1},{2,18},{18,2},{3,19},{19,3},{4,20},{20... | collective-permute-start | bytes 1990664 | tf_op jit(solution)/shard_map/ppermute | solution.py:926
  99.5 16.3 %collective-permute-start.18 = (bf16[768,512]{1,0:T(8,128)(2,1)}, bf16[768,512]{1,0:T(8,128)(2,1)}, u32[]{:S(2)}, u32[]{:S(2)}) collective-permute-start(bf16[768,512]{1,0:T(8,128)(2,1)} %get-tuple-element.205), channel_id=1, source_target_pairs={{0,8},{8,0},{1,9},{9,1},{2,10},{10,2},{3,11},{11,3},{4,12},{12,4},... | collective-permute-start | bytes 2359304 | tf_op jit(solution)/shard_map/ppermute | solution.py:926
  101.1 16.0 %collective-permute-start.19 = (bf16[768,512]{1,0:T(8,128)(2,1)}, bf16[768,512]{1,0:T(8,128)(2,1)}, u32[]{:S(2)}, u32[]{:S(2)}) collective-permute-start(bf16[768,512]{1,0:T(8,128)(2,1)} %get-tuple-element.205), channel_id=1, source_target_pairs={{0,16},{16,0},{1,17},{17,1},{2,18},{18,2},{3,19},{19,3},{4,20},{20... | collective-permute-start | bytes 2359304 | tf_op jit(solution)/shard_map/ppermute | solution.py:926
  119.1 9.1 %collective-permute-start.22 = (bf16[384,512]{1,0:T(8,128)(2,1)}, bf16[384,512]{1,0:T(8,128)(2,1)}, u32[]{:S(2)}, u32[]{:S(2)}) collective-permute-start(bf16[384,512]{1,0:T(8,128)(2,1)} %get-tuple-element.211), channel_id=1, source_target_pairs={{0,8},{8,0},{1,9},{9,1},{2,10},{10,2},{3,11},{11,3},{4,12},{12,4},... | collective-permute-start | bytes 1179656 | tf_op jit(solution)/shard_map/ppermute | solution.py:926
  144.9 74.8 %all-to-all-start.3 = ((bf16[4,768,512]{2,1,0:T(8,128)(2,1)}), bf16[4,768,512]{2,1,0:T(8,128)(2,1)}, u32[]{:S(2)}, u32[]{:S(2)}) async-start(bf16[4,768,512]{2,1,0:T(8,128)(2,1)} %bitcast.29), calls=%async_computation.3 | async-start | bytes 6291456 | tf_op jit(solution)/shard_map/all_to_all | solution.py:1101
  166.6 13.3 %collective-permute-start.26 = (bf16[1728,128]{1,0:T(8,128)(2,1)}, bf16[1728,128]{1,0:T(8,128)(2,1)}, u32[]{:S(2)}, u32[]{:S(2)}) collective-permute-start(bf16[1728,128]{1,0:T(8,128)(2,1)} %get-tuple-element.225), channel_id=1, source_target_pairs={{0,8},{8,0},{1,9},{9,1},{2,10},{10,2},{3,11},{11,3},{4,12},{12,4},... | collective-permute-start | bytes 1327112 | tf_op jit(solution)/shard_map/ppermute | solution.py:926
  168.1 12.3 %collective-permute-start.27 = (bf16[1728,128]{1,0:T(8,128)(2,1)}, bf16[1728,128]{1,0:T(8,128)(2,1)}, u32[]{:S(2)}, u32[]{:S(2)}) collective-permute-start(bf16[1728,128]{1,0:T(8,128)(2,1)} %get-tuple-element.226), channel_id=1, source_target_pairs={{0,16},{16,0},{1,17},{17,1},{2,18},{18,2},{3,19},{19,3},{4,20},{20... | collective-permute-start | bytes 1327112 | tf_op jit(solution)/shard_map/ppermute | solution.py:926
  178.2 17.5 %collective-permute-start.30 = (bf16[1728,128]{1,0:T(8,128)(2,1)}, bf16[1728,128]{1,0:T(8,128)(2,1)}, u32[]{:S(2)}, u32[]{:S(2)}) collective-permute-start(bf16[1728,128]{1,0:T(8,128)(2,1)} %get-tuple-element.239), channel_id=1, source_target_pairs={{0,8},{8,0},{1,9},{9,1},{2,10},{10,2},{3,11},{11,3},{4,12},{12,4},... | collective-permute-start | bytes 1327112 | tf_op jit(solution)/shard_map/ppermute | solution.py:926
  179.0 16.7 %collective-permute-start.31 = (bf16[1728,128]{1,0:T(8,128)(2,1)}, bf16[1728,128]{1,0:T(8,128)(2,1)}, u32[]{:S(2)}, u32[]{:S(2)}) collective-permute-start(bf16[1728,128]{1,0:T(8,128)(2,1)} %get-tuple-element.240), channel_id=1, source_target_pairs={{0,16},{16,0},{1,17},{17,1},{2,18},{18,2},{3,19},{19,3},{4,20},{20... | collective-permute-start | bytes 1327112 | tf_op jit(solution)/shard_map/ppermute | solution.py:926
  182.8 29.5 %collective-permute-start.28 = (bf16[3456,128]{1,0:T(8,128)(2,1)}, bf16[3456,128]{1,0:T(8,128)(2,1)}, u32[]{:S(2)}, u32[]{:S(2)}) collective-permute-start(bf16[3456,128]{1,0:T(8,128)(2,1)} %get-tuple-element.229), channel_id=1, source_target_pairs={{0,8},{8,0},{1,9},{9,1},{2,10},{10,2},{3,11},{11,3},{4,12},{12,4},... | collective-permute-start | bytes 2654216 | tf_op jit(solution)/shard_map/ppermute | solution.py:926
  183.7 28.6 %collective-permute-start.29 = (bf16[3456,128]{1,0:T(8,128)(2,1)}, bf16[3456,128]{1,0:T(8,128)(2,1)}, u32[]{:S(2)}, u32[]{:S(2)}) collective-permute-start(bf16[3456,128]{1,0:T(8,128)(2,1)} %get-tuple-element.230), channel_id=1, source_target_pairs={{0,16},{16,0},{1,17},{17,1},{2,18},{18,2},{3,19},{19,3},{4,20},{20... | collective-permute-start | bytes 2654216 | tf_op jit(solution)/shard_map/ppermute | solution.py:926
  198.1 30.1 %collective-permute-start.35 = (bf16[3456,128]{1,0:T(8,128)(2,1)}, bf16[3456,128]{1,0:T(8,128)(2,1)}, u32[]{:S(2)}, u32[]{:S(2)}) collective-permute-start(bf16[3456,128]{1,0:T(8,128)(2,1)} %get-tuple-element.253), channel_id=1, source_target_pairs={{0,8},{8,0},{1,9},{9,1},{2,10},{10,2},{3,11},{11,3},{4,12},{12,4},... | collective-permute-start | bytes 2654216 | tf_op jit(solution)/shard_map/ppermute | solution.py:926
  199.2 29.5 %collective-permute-start.36 = (bf16[3456,128]{1,0:T(8,128)(2,1)}, bf16[3456,128]{1,0:T(8,128)(2,1)}, u32[]{:S(2)}, u32[]{:S(2)}) collective-permute-start(bf16[3456,128]{1,0:T(8,128)(2,1)} %get-tuple-element.254), channel_id=1, source_target_pairs={{0,16},{16,0},{1,17},{17,1},{2,18},{18,2},{3,19},{19,3},{4,20},{20... | collective-permute-start | bytes 2654216 | tf_op jit(solution)/shard_map/ppermute | solution.py:926
  215.1 24.0 %collective-permute-start.32 = (bf16[864,128]{1,0:T(8,128)(2,1)}, bf16[864,128]{1,0:T(8,128)(2,1)}, u32[]{:S(2)}, u32[]{:S(2)}) collective-permute-start(bf16[864,128]{1,0:T(8,128)(2,1)} %get-tuple-element.245), channel_id=1, source_target_pairs={{0,2},{2,0},{4,6},{6,4},{1,3},{3,1},{5,7},{7,5},{8,10},{10,8},{12,... | collective-permute-start | bytes 663560 | tf_op jit(solution)/shard_map/ppermute | solution.py:926
  217.0 22.1 %collective-permute-start.33 = (bf16[864,128]{1,0:T(8,128)(2,1)}, bf16[864,128]{1,0:T(8,128)(2,1)}, u32[]{:S(2)}, u32[]{:S(2)}) collective-permute-start(bf16[864,128]{1,0:T(8,128)(2,1)} %get-tuple-element.246), channel_id=1, source_target_pairs={{0,4},{2,6},{4,0},{6,2},{1,5},{3,7},{5,1},{7,3},{8,12},{10,14},{12... | collective-permute-start | bytes 663560 | tf_op jit(solution)/shard_map/ppermute | solution.py:926
  219.4 19.7 %collective-permute-start.34 = (bf16[864,128]{1,0:T(8,128)(2,1)}, bf16[864,128]{1,0:T(8,128)(2,1)}, u32[]{:S(2)}, u32[]{:S(2)}) collective-permute-start(bf16[864,128]{1,0:T(8,128)(2,1)} %get-tuple-element.247), channel_id=1, source_target_pairs={{0,6},{2,4},{4,2},{6,0},{1,7},{3,5},{5,3},{7,1},{8,14},{10,12},{12... | collective-permute-start | bytes 663560 | tf_op jit(solution)/shard_map/ppermute | solution.py:926
  219.7 19.3 %all-to-all-start.4 = ((f32[32,1,128]{2,1,0:T(1,128)}), f32[32,1,128]{2,1,0:T(1,128)}, u32[]{:S(2)}, u32[]{:S(2)}) async-start(f32[32,1,128]{2,1,0:T(1,128)} %bitcast.35), calls=%async_computation.4 | async-start | bytes 32768 | tf_op jit(solution)/shard_map/all_to_all | solution.py:1133
  241.2 26.6 %all-to-all-start.5 = ((bf16[4,864,128]{2,1,0:T(8,128)(2,1)}), bf16[4,864,128]{2,1,0:T(8,128)(2,1)}, u32[]{:S(2)}, u32[]{:S(2)}) async-start(bf16[4,864,128]{2,1,0:T(8,128)(2,1)} %bitcast.30), calls=%async_computation.5 | async-start | bytes 1769472 | tf_op jit(solution)/shard_map/all_to_all | solution.py:1101
  245.6 9.3 %collective-permute-start.38 = (f32[512,256]{1,0:T(8,128)}, f32[512,256]{1,0:T(8,128)}, u32[]{:S(2)}, u32[]{:S(2)}) collective-permute-start(f32[512,256]{1,0:T(8,128)} %get-tuple-element.267), channel_id=1, source_target_pairs={{0,1},{1,0},{2,3},{3,2},{4,5},{5,4},{6,7},{7,6},{8,9},{9,8},{10,11... | collective-permute-start | bytes 1572872 | tf_op jit(solution)/shard_map/ppermute | solution.py:926
  249.6 10.2 %collective-permute-start.40 = (bf16[192,512]{1,0:T(8,128)(2,1)}, bf16[192,512]{1,0:T(8,128)(2,1)}, u32[]{:S(2)}, u32[]{:S(2)}) collective-permute-start(bf16[192,512]{1,0:T(8,128)(2,1)} %get-tuple-element.273), channel_id=1, source_target_pairs={{0,16},{16,0},{1,17},{17,1},{2,18},{18,2},{3,19},{19,3},{4,20},{20... | collective-permute-start | bytes 589832 | tf_op jit(solution)/shard_map/ppermute | solution.py:926
  251.1 10.1 %collective-permute-start.41 = (bf16[192,512]{1,0:T(8,128)(2,1)}, bf16[192,512]{1,0:T(8,128)(2,1)}, u32[]{:S(2)}, u32[]{:S(2)}) collective-permute-start(bf16[192,512]{1,0:T(8,128)(2,1)} %get-tuple-element.274), channel_id=1, source_target_pairs={{0,24},{8,16},{16,8},{24,0},{1,25},{9,17},{17,9},{25,1},{2,26},{10... | collective-permute-start | bytes 589832 | tf_op jit(solution)/shard_map/ppermute | solution.py:1118
  252.4 21.4 %collective-permute-start.42 = (f32[432,128]{1,0:T(8,128)}, f32[432,128]{1,0:T(8,128)}, u32[]{:S(2)}, u32[]{:S(2)}) collective-permute-start(f32[432,128]{1,0:T(8,128)} %get-tuple-element.282), channel_id=1, source_target_pairs={{0,1},{1,0},{2,3},{3,2},{4,5},{5,4},{6,7},{7,6},{8,9},{9,8},{10,11... | collective-permute-start | bytes 663560 | tf_op jit(solution)/shard_map/ppermute | solution.py:926
  270.1 10.7 %collective-permute-start.43 = (f32[432,128]{1,0:T(8,128)}, f32[432,128]{1,0:T(8,128)}, u32[]{:S(2)}, u32[]{:S(2)}) collective-permute-start(f32[432,128]{1,0:T(8,128)} %get-tuple-element.283), channel_id=1, source_target_pairs={{0,1},{1,0},{2,3},{3,2},{4,5},{5,4},{6,7},{7,6},{8,9},{9,8},{10,11... | collective-permute-start | bytes 663560 | tf_op jit(solution)/shard_map/ppermute | solution.py:926
  270.6 10.2 %all-to-all-start.6 = ((f32[32,1,128]{2,1,0:T(1,128)}), f32[32,1,128]{2,1,0:T(1,128)}, u32[]{:S(2)}, u32[]{:S(2)}) async-start(f32[32,1,128]{2,1,0:T(1,128)} %bitcast.36), calls=%async_computation.6 | async-start | bytes 32768 | tf_op jit(solution)/shard_map/all_to_all | solution.py:1133
  (23 other events, 113.3 us)
